TPU v7x, 512 devices: a whole 4x8x8 slice. The times are simulated.
512 devices in a mesh: rows: 64 (over x, z, core), cols: 8 (over y).
Axes of the slice: x: 4, y: 8, z: 8, core: 2. Of those that a mesh axis runs over, the one named last changes fastest.
Arguments:
- momentum: float32 [3584, 13312], P('rows', 'cols'), may hold values from -200 to 200
Outputs:
- update: bfloat16 [3584, 13312], P('rows', 'cols')
All inputs are finite; a program needn't handle non-finite values.
Results may differ from a plain program's by a relative error of at most 0.0052.
Values may be sent and summed in bfloat16 or wider, within the bound.
No kernel may reach another device: no remote copies, remote signals or barrier semaphores. Data moves between devices by JAX's collectives and lax.ppermute only.
A program may use at most 64 MiB of HBM per device.

v0:
```python
import math

import jax
import jax.numpy as jnp
from jax import lax
from jax.sharding import PartitionSpec as P

M = 3584
N = 13312


coef_a = 3.4445
coef_b = -4.775
coef_c = 2.0315


def per_device(momentum):
    total = lax.psum(jnp.sum(momentum * momentum), ("rows", "cols"))
    factor = math.sqrt(M) / 3.0 / (jnp.sqrt(total) + 1e-07)
    scaled_rows = (momentum * factor).astype(jnp.bfloat16)
    column_slab = lax.all_gather(scaled_rows, "rows", axis=0, tiled=True)
    partial_value = lax.dot_general(
        scaled_rows, column_slab, (((1,), (1,)), ((), ())), preferred_element_type=jnp.float32
    )
    part_width = M // lax.axis_size("cols")
    gram_full = lax.psum(partial_value, "cols")
    gram_here = gram_full.astype(jnp.bfloat16)
    gram_part = lax.dynamic_slice_in_dim(
        gram_here, lax.axis_index("cols") * part_width, part_width, 1
    )
    square_part = jnp.dot(
        gram_here,
        lax.all_gather(gram_part, "rows", axis=0, tiled=True),
        preferred_element_type=jnp.float32,
    ).astype(jnp.bfloat16)
    square_rows = lax.all_gather(square_part, "cols", axis=1, tiled=True)
    polynomial = (
        coef_b * gram_here.astype(jnp.float32) + coef_c * square_rows.astype(jnp.float32)
    ).astype(jnp.bfloat16)
    product = jnp.dot(polynomial, column_slab, preferred_element_type=jnp.float32)
    result = (coef_a * scaled_rows.astype(jnp.float32) + product) * (0.2 * math.sqrt(N))
    return result.astype(jnp.bfloat16)


def solution(mesh):
    return jax.shard_map(
        per_device,
        mesh=mesh,
        in_specs=(P("rows", "cols"),),
        out_specs=P("rows", "cols"),
        check_vma=False,
    )
```

profile of v0, /device:TPU:1, one launch (start us, length us, event | category | flops | bytes accessed | tf_op | source)
XLA Modules:
  0.0 370.5 jit_solution(1037218194668060944)
XLA Ops:
  6.5 0.0 all-gather.4.cloned.1.call-start
  6.5 1.7 multiply_reduce_fusion
  8.2 106.1 %psum.14 = f32[]{:T(128)} all-reduce(f32[]{:T(128)} %multiply_reduce_fusion), channel_id=1, replica_groups=mesh['rows'=64,'cols'=8] {'rows','cols'}, use_global_device_ids=true, to_apply=%region_1.0 | all-reduce | flops 1 | bytes 8 | tf_op jit(solution)/shard_map/psum | solution.py:18
  115.0 1.7 multiply_convert_fusion
  116.7 0.0 all-gather.4.cloned.1.call-update
  116.8 0.0 all-gather.6.cloned.1.call-start
  116.8 0.0 copy-start
  116.8 89.3 %all-gather.4.cloned.1.call-done = bf16[3584,1664]{1,0:T(8,128)(2,1)} async-done(((bf16[56,1664]{1,0:T(8,128)(2,1)}), bf16[3584,1664]{1,0:T(8,128)(2,1)}) %all-gather.4.cloned.1.call-update) | async-done | bytes 11927568 | tf_op jit(solution)/shard_map/all_gather | solution.py:21
  206.1 8.4 %fusion.7 = f32[56,3584]{1,0:T(8,128)S(1)} fusion(bf16[56,1664]{1,0:T(8,128)(2,1)} %multiply_convert_fusion, bf16[3584,1664]{1,0:T(8,128)(2,1)} %all-gather.4.cloned.1.call-done), kind=kOutput, calls=%fused_computation.13 | convolution fusion | flops 667942912 | bytes 12916736 | tf_op jit(solution)/shard_map/dot_general | solution.py:22
  214.5 31.6 %all-reduce.1 = bf16[56,3584]{1,0:T(8,128)(2,1)S(1)} all-reduce(f32[56,3584]{1,0:T(8,128)S(1)} %fusion.7), channel_id=1, replica_groups=mesh['rows'=64,'cols'=8] {'cols'}, use_global_device_ids=true, to_apply=%region_2.0 | all-reduce | flops 200704 | bytes 1204224 | tf_op jit(solution)/shard_map/psum | solution.py:26
  246.2 0.7 constant_dynamic-slice_fusion
  246.9 0.0 all-gather.6.cloned.1.call-update
  246.9 85.6 %all-gather.6.cloned.1.call-done = bf16[3584,448]{1,0:T(8,128)(2,1)} async-done(((bf16[56,448]{1,0:T(8,128)(2,1)}), bf16[3584,448]{1,0:T(8,128)(2,1)}) %all-gather.6.cloned.1.call-update) | async-done | bytes 3211280 | tf_op jit(solution)/shard_map/all_gather | solution.py:33
  332.6 2.8 fusion.2
  335.3 20.3 %all-gather = bf16[8,448,56]{1,2,0:T(8,128)(2,1)S(1)} all-gather(bf16[1,448,56]{1,2,0:T(8,128)(2,1)S(1)} %fusion.2), channel_id=1, replica_groups=mesh['rows'=64,'cols'=8] {'cols'}, dimensions={0}, use_global_device_ids=true | all-gather | bytes 451584 | tf_op jit(solution)/shard_map/all_gather | solution.py:36
  355.6 0.1 convert_multiply_fusion
  355.7 0.5 copy.3
  356.3 0.4 reshape.4
  356.6 0.0 copy-done
  356.6 7.1 %fusion.1 = bf16[56,1664]{1,0:T(8,128)(2,1)} fusion(bf16[3584,1664]{1,0:T(8,128)(2,1)} %all-gather.4.cloned.1.call-done, f32[3584,56]{0,1:T(8,128)S(1)} %reshape.4, bf16[56,3584]{1,0:T(8,128)(2,1)S(1)} %all-reduce.1, bf16[56,1664]{1,0:T(8,128)(2,1)S(1)} %copy-done), kind=kOutput, calls=%fused_computation.2 | convolution fusion | flops 669211648 | bytes 13504512 | tf_op jit(solution)/shard_map/dot_general | solution.py:40
Async XLA Ops:
  6.5 199.6 %all-gather.4.cloned.1.call-start = ((), (), s32[]{:S(2)}) async-start(), calls=%async_computation | async-start | bytes 12113920 | tf_op jit(solution)/shard_map/all_gather | solution.py:21
  116.8 215.8 %all-gather.6.cloned.1.call-start = ((), (), s32[]{:S(2)}) async-start(), calls=%async_computation.1 | async-start | bytes 3727360 | tf_op jit(solution)/shard_map/all_gather | solution.py:33
  116.8 239.8 %copy-start = (bf16[56,1664]{1,0:T(8,128)(2,1)S(1)}, bf16[56,1664]{1,0:T(8,128)(2,1)}, u32[]{:S(2)}) copy-start(bf16[56,1664]{1,0:T(8,128)(2,1)} %multiply_convert_fusion) | copy-start | bytes 559108
Sparse Core Ops, SparseCore 0:
  116.9 89.1 all-gather.3
  247.0 85.4 all-gather.5
where the time goes:
time: 375 us; the launch traced here: 371 us
  waiting for transfers between devices  175 us (47%)
  blocking collectives  158 us (42%)
  matrix products  18.2 us (5%)
  between operations  14.2 us (4%)
    psum x1, blocking collectives, per_device(): total = lax.psum(jnp.sum(momentum * momentum), ('rows', 'cols'))  106 us
    all_gather x1, waiting for transfers between devices, per_device(): column_slab = lax.all_gather(scaled_rows, 'rows', axis=0, tiled=True)  89.3 us
    all_gather x1, waiting for transfers between devices, per_device(): lax.all_gather(gram_part, 'rows', axis=0, tiled=True)  85.6 us
    psum x1, blocking collectives, per_device(): gram_full = lax.psum(partial_value, 'cols')  31.6 us
    all_gather x1, blocking collectives, per_device(): square_rows = lax.all_gather(square_part, 'cols', axis=1, tiled=True)  20.3 us
    dot_general x1, matrix products, per_device(): lax.dot_general(scaled_rows, column_slab, (((1,), (1,)), ((), ())), prefe...  8.42 us
  transfers between devices with their start and end apart: 2, of which 2 were waited for; matrix products, arithmetic and copies ran while one was open for 0% of the time, Pallas kernels for 0%

commit v1 on v0

v1 whole, which is shorter than its diff:
```python
import math

import jax
import jax.numpy as jnp
from jax import lax
from jax.sharding import Mesh, PartitionSpec as P

M = 3584
N = 13312

coef_a = 3.4445
coef_b = -4.775
coef_c = 2.0315

lift = 128.0

bf16 = jnp.bfloat16
f32 = jnp.float32


def shift(size, by):
    return [(i, (i + by) % size) for i in range(size)]


def swap(size, bit):
    return [(i, i ^ bit) for i in range(size)]


def ring_z(block, total, steps):
    up, down = [block], []
    left, right = block, block
    for step in range(4):
        left, right, total = lax.optimization_barrier((left, right, total))
        left = lax.ppermute(left, "z", shift(8, 1))
        if step < 3:
            right = lax.ppermute(right, "z", shift(8, -1))
            down.append(right)
        up.append(left)
        total = add_swapped(total, *steps[step])
    return jnp.concatenate(up + down, axis=0), total


def add_swapped(total, axis, size, bit):
    return total + lax.ppermute(total, axis, swap(size, bit))


def spread(partial_rows, core):
    mine = lax.dynamic_index_in_dim(partial_rows, core, 0, keepdims=False)
    other = lax.dynamic_index_in_dim(partial_rows, 1 - core, 0, keepdims=False)
    got = lax.ppermute(other.astype(bf16), "c", swap(2, 1))
    pieces = (mine + got.astype(f32)).astype(bf16)
    pieces = lax.all_to_all(pieces, "x", 0, 0)
    return jnp.sum(pieces.astype(f32), axis=0)


def per_device(momentum):
    core = lax.axis_index("c")
    raw = (momentum * lift).astype(bf16)
    total = jnp.broadcast_to(jnp.sum(momentum * momentum).reshape(1, 1), (8, 128))

    rows_j, total = ring_z(
        raw, total, (("c", 2, 1), ("z", 8, 1), ("z", 8, 2), ("z", 8, 4))
    )
    over_x = lax.all_to_all(jnp.broadcast_to(raw[None], (4, 56, 1664)), "x", 0, 0)
    other_x = lax.ppermute(over_x, "c", swap(2, 1))
    first = jnp.where(core == 0, over_x, other_x)
    second = jnp.where(core == 0, other_x, over_x)
    rows_r = jnp.concatenate([first, second], axis=0).reshape(448, 1664)

    part = lax.dot_general(
        rows_j, rows_r, (((1,), (1,)), ((), ())), preferred_element_type=f32
    ).astype(bf16)
    part = lax.all_to_all(part.reshape(8, 56, 448), "y", 0, 0)
    piece = jnp.sum(part.astype(f32), axis=0).astype(bf16)
    gram = lax.all_to_all(
        jnp.broadcast_to(piece[None], (8, 56, 448)), "y", 0, 0
    ).reshape(448, 448)

    def apply(block):
        return lax.dot_general(
            gram, block, (((0,), (0,)), ((), ())), preferred_element_type=f32
        ).reshape(2, 4, 56, 1664)

    once = spread(apply(rows_j), core)
    rows_once, total = ring_z(
        once.astype(bf16), total, (("y", 8, 1), ("y", 8, 2), ("y", 8, 4), ("x", 4, 1))
    )
    total, rows_once = lax.optimization_barrier((total, rows_once))
    total = add_swapped(total, "x", 4, 2)
    twice = spread(apply(rows_once), core)

    factor = math.sqrt(M) / 3.0 / (jnp.sqrt(total[0, 0]) + 1e-07)
    iterate = (momentum * factor).astype(bf16).astype(f32)
    small = factor / lift
    product = small * (small * (small * (coef_b * once + small * (small * (coef_c * twice)))))
    result = (coef_a * iterate + product) * (0.2 * math.sqrt(N))
    return result.astype(bf16)


def solution(mesh):
    fine = Mesh(mesh.devices.reshape(4, 8, 2, 8), ("x", "z", "c", "y"))
    spec = P(("x", "z", "c"), "y")
    return jax.shard_map(
        per_device, mesh=fine, in_specs=(spec,), out_specs=spec, check_vma=False
    )
```

time: 375 us -> 209 us (0.56)
  blocking collectives: 158 us -> 18.7 us
  waiting for transfers between devices: 175 us -> 52.5 us
  starting transfers between devices: 0.04 us -> 119 us
  matrix products: 18.2 us -> 4.38 us
  between operations: 14.2 us -> 1.22 us
  other arithmetic: 3.48 us -> 7.33 us
    all_gather x2 -> x0, waiting for transfers between devices: 175 us -> none  [the longest x1 89.3 us: per_device(): column_slab = lax.all_gather(scaled_rows, 'rows', axis=0, tiled=True)]
    psum x2 -> x0, blocking collectives: 138 us -> none  [the longest x1 106 us: per_device(): total = lax.psum(jnp.sum(momentum * momentum), ('rows', 'cols'))]
    ppermute x0 -> x26, starting transfers between devices: none -> 103 us  [the longest x6 28.3 us: ring_z(): right = lax.ppermute(right, 'z', shift(8, -1))]
    ppermute x0 -> x26, waiting for transfers between devices: none -> 38 us  [the longest x9 13.9 us: add_swapped(): return total + lax.ppermute(total, axis, swap(size, bit))]
    all_gather x1 -> x0, blocking collectives: 20.3 us -> none  [per_device(): square_rows = lax.all_gather(square_part, 'cols', axis=1, tiled=True)]
    all_to_all x0 -> x1, blocking collectives: none -> 18.7 us  [per_device(): part = lax.all_to_all(part.reshape(8, 56, 448), 'y', 0, 0)]
    all_to_all x0 -> x4, starting transfers between devices: none -> 15.6 us  [the longest x2 8.13 us: spread(): pieces = lax.all_to_all(pieces, 'x', 0, 0)]
    all_to_all x0 -> x4, waiting for transfers between devices: none -> 14.4 us  [the longest x1 11.4 us: per_device(): lax.all_to_all(jnp.broadcast_to(piece[None], (8, 56, 448)), 'y', 0, 0)]
  transfers between devices with their start and end apart: 2 -> 30, of which waited for: 2 -> 20; matrix products, arithmetic and copies ran while one was open for 0% -> 1% of each run, Pallas kernels for 0% -> 0%
where the time goes in v1:
time: 209 us; the launch traced here: 207 us
  starting transfers between devices  119 us (57%)
  waiting for transfers between devices  52.5 us (25%)
  blocking collectives  18.7 us (9%)
  other arithmetic  7.33 us (4%)
  local copies, waits for them, and re-layouts  4.5 us (2%)
  matrix products  4.38 us (2%)
    ppermute x6, starting transfers between devices, ring_z(): right = lax.ppermute(right, 'z', shift(8, -1))  28.3 us
    ppermute x9, starting transfers between devices, add_swapped(): return total + lax.ppermute(total, axis, swap(size, bit))  27.6 us
    ppermute x8, starting transfers between devices, ring_z(): left = lax.ppermute(left, 'z', shift(8, 1))  25.5 us
    all_to_all x1, blocking collectives, per_device(): part = lax.all_to_all(part.reshape(8, 56, 448), 'y', 0, 0)  18.7 us
    ppermute x2, starting transfers between devices, spread(): got = lax.ppermute(other.astype(bf16), 'c', swap(2, 1))  16.8 us
    ppermute x9, waiting for transfers between devices, add_swapped(): return total + lax.ppermute(total, axis, swap(size, bit))  13.9 us
    all_to_all x1, waiting for transfers between devices, per_device(): lax.all_to_all(jnp.broadcast_to(piece[None], (8, 56, 448)), 'y', 0, 0)  11.4 us
    ppermute x8, waiting for transfers between devices, ring_z(): left = lax.ppermute(left, 'z', shift(8, 1))  11.3 us
  transfers between devices with their start and end apart: 30, of which 20 were waited for; matrix products, arithmetic and copies ran while one was open for 1% of the time, Pallas kernels for 0%

profile of v1, /device:TPU:1, one launch (start us, length us, event | category | flops | bytes accessed | tf_op | source)
XLA Modules:
  0.0 207.5 jit_solution(8896888544852574618)
XLA Ops:
  0.0 1.7 multiply_reduce_fusion
  1.7 1.0 constant_dynamic-update-slice_fusion.7
  2.7 0.6 broadcast_in_dim.6
  3.4 4.8 %collective-permute-start = (bf16[56,1664]{1,0:T(8,128)(2,1)S(1)}, bf16[56,1664]{1,0:T(8,128)(2,1)S(1)}, u32[]{:S(2)}, u32[]{:S(2)}) collective-permute-start(bf16[56,1664]{1,0:T(8,128)(2,1)S(1)} %get-tuple-element.30), channel_id=1, source_target_pairs={{0,16},{16,32},{32,48},{48,64},{64,80},{80,96},{96,112},{112,0},{1... | collective-permute-start | bytes 559112 | tf_op jit(solution)/shard_map/ppermute | solution.py:34
  8.2 8.6 %collective-permute-start.1 = (bf16[56,1664]{1,0:T(8,128)(2,1)S(1)}, bf16[56,1664]{1,0:T(8,128)(2,1)S(1)}, u32[]{:S(2)}, u32[]{:S(2)}) collective-permute-start(bf16[56,1664]{1,0:T(8,128)(2,1)S(1)} %get-tuple-element.30), channel_id=1, source_target_pairs={{0,112},{16,0},{32,16},{48,32},{64,48},{80,64},{96,80},{112,96},{1... | collective-permute-start | bytes 559112 | tf_op jit(solution)/shard_map/ppermute | solution.py:36
  16.8 0.9 broadcast_in_dim.7
  17.7 4.0 %all-to-all-start = ((bf16[4,56,1664]{2,1,0:T(8,128)(2,1)}), bf16[4,56,1664]{2,1,0:T(8,128)(2,1)S(1)}, u32[]{:S(2)}, u32[]{:S(2)}) async-start(bf16[4,56,1664]{2,1,0:T(8,128)(2,1)} %broadcast_in_dim.7), calls=%async_computation | async-start | bytes 1490944 | tf_op jit(solution)/shard_map/all_to_all | solution.py:64
  21.7 3.1 %collective-permute-start.2 = (f32[8,128]{1,0:T(8,128)S(1)}, f32[8,128]{1,0:T(8,128)S(1)}, u32[]{:S(2)}, u32[]{:S(2)}) collective-permute-start(f32[8,128]{1,0:T(8,128)S(1)} %broadcast_in_dim.6), channel_id=1, source_target_pairs={{0,8},{8,0},{1,9},{9,1},{2,10},{10,2},{3,11},{11,3},{4,12},{12,4},... | collective-permute-start | bytes 12296 | tf_op jit(solution)/shard_map/ppermute | solution.py:44
  24.9 0.8 collective-permute-done.2
  25.7 1.9 collective-permute-start.5
  27.6 3.4 %collective-permute-start.3 = (bf16[56,1664]{1,0:T(8,128)(2,1)S(1)}, bf16[56,1664]{1,0:T(8,128)(2,1)S(1)}, u32[]{:S(2)}, u32[]{:S(2)}) collective-permute-start(bf16[56,1664]{1,0:T(8,128)(2,1)S(1)} %collective-permute-done), channel_id=1, source_target_pairs={{0,16},{16,32},{32,48},{48,64},{64,80},{80,96},{96,112},{112,0},{1... | collective-permute-start | bytes 559112 | tf_op jit(solution)/shard_map/ppermute | solution.py:34
  31.0 3.1 %collective-permute-start.4 = (bf16[56,1664]{1,0:T(8,128)(2,1)S(1)}, bf16[56,1664]{1,0:T(8,128)(2,1)S(1)}, u32[]{:S(2)}, u32[]{:S(2)}) collective-permute-start(bf16[56,1664]{1,0:T(8,128)(2,1)S(1)} %collective-permute-done.1), channel_id=1, source_target_pairs={{0,112},{16,0},{32,16},{48,32},{64,48},{80,64},{96,80},{112,96},{1... | collective-permute-start | bytes 559112 | tf_op jit(solution)/shard_map/ppermute | solution.py:36
  34.2 2.5 %collective-permute-done.3 = bf16[56,1664]{1,0:T(8,128)(2,1)S(1)} collective-permute-done((bf16[56,1664]{1,0:T(8,128)(2,1)S(1)}, bf16[56,1664]{1,0:T(8,128)(2,1)S(1)}, u32[]{:S(2)}, u32[]{:S(2)}) %collective-permute-start.3) | collective-permute-done | bytes 186400 | tf_op jit(solution)/shard_map/ppermute | solution.py:34
  36.6 1.5 collective-permute-done.4
  38.2 2.8 %collective-permute-start.8 = (f32[8,128]{1,0:T(8,128)S(1)}, f32[8,128]{1,0:T(8,128)S(1)}, u32[]{:S(2)}, u32[]{:S(2)}) collective-permute-start(f32[8,128]{1,0:T(8,128)S(1)} %add.54), channel_id=1, source_target_pairs={{0,32},{16,48},{32,0},{48,16},{64,96},{80,112},{96,64},{112,80},{1... | collective-permute-start | bytes 12296 | tf_op jit(solution)/shard_map/ppermute | solution.py:44
  41.0 4.3 %collective-permute-start.6 = (bf16[56,1664]{1,0:T(8,128)(2,1)S(1)}, bf16[56,1664]{1,0:T(8,128)(2,1)S(1)}, u32[]{:S(2)}, u32[]{:S(2)}) collective-permute-start(bf16[56,1664]{1,0:T(8,128)(2,1)S(1)} %collective-permute-done.3), channel_id=1, source_target_pairs={{0,16},{16,32},{32,48},{48,64},{64,80},{80,96},{96,112},{112,0},{1... | collective-permute-start | bytes 559112 | tf_op jit(solution)/shard_map/ppermute | solution.py:34
  45.3 2.2 %collective-permute-start.7 = (bf16[56,1664]{1,0:T(8,128)(2,1)S(1)}, bf16[56,1664]{1,0:T(8,128)(2,1)S(1)}, u32[]{:S(2)}, u32[]{:S(2)}) collective-permute-start(bf16[56,1664]{1,0:T(8,128)(2,1)S(1)} %collective-permute-done.4), channel_id=1, source_target_pairs={{0,112},{16,0},{32,16},{48,32},{64,48},{80,64},{96,80},{112,96},{1... | collective-permute-start | bytes 559112 | tf_op jit(solution)/shard_map/ppermute | solution.py:36
  47.6 1.0 collective-permute-done.6
  48.5 3.1 %collective-permute-done.7 = bf16[56,1664]{1,0:T(8,128)(2,1)S(1)} collective-permute-done((bf16[56,1664]{1,0:T(8,128)(2,1)S(1)}, bf16[56,1664]{1,0:T(8,128)(2,1)S(1)}, u32[]{:S(2)}, u32[]{:S(2)}) %collective-permute-start.7) | collective-permute-done | bytes 186400 | tf_op jit(solution)/shard_map/ppermute | solution.py:36
  51.6 2.2 %collective-permute-start.9 = (bf16[56,1664]{1,0:T(8,128)(2,1)S(1)}, bf16[56,1664]{1,0:T(8,128)(2,1)S(1)}, u32[]{:S(2)}, u32[]{:S(2)}) collective-permute-start(bf16[56,1664]{1,0:T(8,128)(2,1)S(1)} %collective-permute-done.6), channel_id=1, source_target_pairs={{0,16},{16,32},{32,48},{48,64},{64,80},{80,96},{96,112},{112,0},{1... | collective-permute-start | bytes 559112 | tf_op jit(solution)/shard_map/ppermute | solution.py:34
  53.8 5.1 %collective-permute-start.10 = (bf16[4,56,1664]{2,1,0:T(8,128)(2,1)S(1)}, bf16[4,56,1664]{2,1,0:T(8,128)(2,1)S(1)}, u32[]{:S(2)}, u32[]{:S(2)}) collective-permute-start(bf16[4,56,1664]{2,1,0:T(8,128)(2,1)S(1)} %all-to-all-done), channel_id=1, source_target_pairs={{0,8},{8,0},{1,9},{9,1},{2,10},{10,2},{3,11},{11,3},{4,12},{12,4},... | collective-permute-start | bytes 2236424 | tf_op jit(solution)/shard_map/ppermute | solution.py:65
  59.2 1.5 collective-permute-done.10
  60.7 0.2 broadcast_select_fusion.1
  61.0 1.0 convolution_convert_fusion
  62.1 18.7 %all_to_all.25 = bf16[8,56,448]{2,1,0:T(8,128)(2,1)S(1)} all-to-all(bf16[8,56,448]{2,1,0:T(8,128)(2,1)S(1)} %bitcast.37), channel_id=1, replica_groups=mesh['x'=4,'z'=8,'c'=2,'y'=8] {'y'}, dimensions={0} | all-to-all | bytes 802816 | tf_op jit(solution)/shard_map/all_to_all | solution.py:73
  80.9 0.8 broadcast_in_dim.8
  81.7 3.5 %all-to-all-start.2 = ((bf16[8,56,448]{2,1,0:T(8,128)(2,1)}), bf16[8,56,448]{2,1,0:T(8,128)(2,1)S(1)}, u32[]{:S(2)}, u32[]{:S(2)}) async-start(bf16[8,56,448]{2,1,0:T(8,128)(2,1)} %broadcast_in_dim.8), calls=%async_computation.2 | async-start | bytes 917504 | tf_op jit(solution)/shard_map/all_to_all | solution.py:75
  85.2 11.4 %all-to-all-done.2 = bf16[8,56,448]{2,1,0:T(8,128)(2,1)S(1)} async-done(((bf16[8,56,448]{2,1,0:T(8,128)(2,1)}), bf16[8,56,448]{2,1,0:T(8,128)(2,1)S(1)}, u32[]{:S(2)}, u32[]{:S(2)}) %all-to-all-start.2) | async-done | bytes 401440 | tf_op jit(solution)/shard_map/all_to_all | solution.py:75
  96.6 0.2 copy.2
  96.8 2.4 %fusion.2 = f32[2,4,56,1664]{3,2,1,0:T(8,128)S(1)} fusion(bf16[2,4,56,448]{3,2,1,0:T(8,128)(2,1)S(1)} %bitcast.33, bf16[448,1664]{1,0:T(8,128)(2,1)} %copy-done.1), kind=kOutput, calls=%fused_computation.3 | convolution fusion | flops 667942912 | bytes 4874240 | tf_op jit(solution)/shard_map/dot_general | solution.py:80
  99.1 1.0 fusion.6
  100.1 8.0 %collective-permute-start.11 = (bf16[4,56,1664]{2,1,0:T(8,128)(2,1)}, bf16[4,56,1664]{2,1,0:T(8,128)(2,1)}, u32[]{:S(2)}, u32[]{:S(2)}) collective-permute-start(bf16[4,56,1664]{2,1,0:T(8,128)(2,1)} %fusion.6), channel_id=1, source_target_pairs={{0,8},{8,0},{1,9},{9,1},{2,10},{10,2},{3,11},{11,3},{4,12},{12,4},... | collective-permute-start | bytes 2236424 | tf_op jit(solution)/shard_map/ppermute | solution.py:50
  108.1 2.2 %collective-permute-done.11 = bf16[4,56,1664]{2,1,0:T(8,128)(2,1)} collective-permute-done((bf16[4,56,1664]{2,1,0:T(8,128)(2,1)}, bf16[4,56,1664]{2,1,0:T(8,128)(2,1)}, u32[]{:S(2)}, u32[]{:S(2)}) %collective-permute-start.11) | collective-permute-done | bytes 745504 | tf_op jit(solution)/shard_map/ppermute | solution.py:50
  110.3 2.2 %fusion.5 = bf16[4,56,1664]{2,1,0:T(8,128)(2,1)} fusion(bf16[4,56,1664]{2,1,0:T(8,128)(2,1)} %collective-permute-done.11, f32[2,4,56,1664]{3,2,1,0:T(8,128)S(1)} %fusion.2, s32[]{:T(128)S(6)} %select_n.24), kind=kLoop, calls=%fused_computation.8 | loop fusion | flops 1118208 | bytes 2981892 | tf_op jit(solution)/shard_map/convert_element_type | solution.py:51
  112.4 4.5 %all-to-all-start.3 = ((bf16[4,56,1664]{2,1,0:T(8,128)(2,1)}), bf16[4,56,1664]{2,1,0:T(8,128)(2,1)S(1)}, u32[]{:S(2)}, u32[]{:S(2)}) async-start(bf16[4,56,1664]{2,1,0:T(8,128)(2,1)} %fusion.5), calls=%async_computation.3 | async-start | bytes 1490944 | tf_op jit(solution)/shard_map/all_to_all | solution.py:52
  116.9 4.5 %collective-permute-start.12 = (f32[8,128]{1,0:T(8,128)S(1)}, f32[8,128]{1,0:T(8,128)S(1)}, u32[]{:S(2)}, u32[]{:S(2)}) collective-permute-start(f32[8,128]{1,0:T(8,128)S(1)} %add.55), channel_id=1, source_target_pairs={{0,64},{16,80},{32,96},{48,112},{64,0},{80,16},{96,32},{112,48},{1... | collective-permute-start | bytes 12296 | tf_op jit(solution)/shard_map/ppermute | solution.py:44
  121.4 3.7 %collective-permute-done.12 = f32[8,128]{1,0:T(8,128)S(1)} collective-permute-done((f32[8,128]{1,0:T(8,128)S(1)}, f32[8,128]{1,0:T(8,128)S(1)}, u32[]{:S(2)}, u32[]{:S(2)}) %collective-permute-start.12) | collective-permute-done | bytes 4128 | tf_op jit(solution)/shard_map/ppermute | solution.py:44
  125.2 3.0 %all-to-all-done.3 = bf16[4,56,1664]{2,1,0:T(8,128)(2,1)S(1)} async-done(((bf16[4,56,1664]{2,1,0:T(8,128)(2,1)}), bf16[4,56,1664]{2,1,0:T(8,128)(2,1)S(1)}, u32[]{:S(2)}, u32[]{:S(2)}) %all-to-all-start.3) | async-done | bytes 745504 | tf_op jit(solution)/shard_map/all_to_all | solution.py:52
  128.4 3.8 %collective-permute-start.13 = (bf16[56,1664]{1,0:T(8,128)(2,1)S(1)}, bf16[56,1664]{1,0:T(8,128)(2,1)S(1)}, u32[]{:S(2)}, u32[]{:S(2)}) collective-permute-start(bf16[56,1664]{1,0:T(8,128)(2,1)S(1)} %get-tuple-element.41), channel_id=1, source_target_pairs={{0,16},{16,32},{32,48},{48,64},{64,80},{80,96},{96,112},{112,0},{1... | collective-permute-start | bytes 559112 | tf_op jit(solution)/shard_map/ppermute | solution.py:34
  132.2 5.6 %collective-permute-start.14 = (bf16[56,1664]{1,0:T(8,128)(2,1)S(1)}, bf16[56,1664]{1,0:T(8,128)(2,1)S(1)}, u32[]{:S(2)}, u32[]{:S(2)}) collective-permute-start(bf16[56,1664]{1,0:T(8,128)(2,1)S(1)} %get-tuple-element.41), channel_id=1, source_target_pairs={{0,112},{16,0},{32,16},{48,32},{64,48},{80,64},{96,80},{112,96},{1... | collective-permute-start | bytes 559112 | tf_op jit(solution)/shard_map/ppermute | solution.py:36
  137.8 2.2 %collective-permute-start.15 = (f32[8,128]{1,0:T(8,128)S(1)}, f32[8,128]{1,0:T(8,128)S(1)}, u32[]{:S(2)}, u32[]{:S(2)}) collective-permute-start(f32[8,128]{1,0:T(8,128)S(1)} %add.59), channel_id=1, source_target_pairs={{0,1},{1,0},{2,3},{3,2},{4,5},{5,4},{6,7},{7,6},{8,9},{9,8},{10,11... | collective-permute-start | bytes 12296 | tf_op jit(solution)/shard_map/ppermute | solution.py:44
  140.1 2.4 %collective-permute-done.15 = f32[8,128]{1,0:T(8,128)S(1)} collective-permute-done((f32[8,128]{1,0:T(8,128)S(1)}, f32[8,128]{1,0:T(8,128)S(1)}, u32[]{:S(2)}, u32[]{:S(2)}) %collective-permute-start.15) | collective-permute-done | bytes 4128 | tf_op jit(solution)/shard_map/ppermute | solution.py:44
  142.5 1.9 collective-permute-start.18
  144.4 1.9 collective-permute-start.16
  146.4 4.6 %collective-permute-start.17 = (bf16[56,1664]{1,0:T(8,128)(2,1)S(1)}, bf16[56,1664]{1,0:T(8,128)(2,1)S(1)}, u32[]{:S(2)}, u32[]{:S(2)}) collective-permute-start(bf16[56,1664]{1,0:T(8,128)(2,1)S(1)} %collective-permute-done.14), channel_id=1, source_target_pairs={{0,112},{16,0},{32,16},{48,32},{64,48},{80,64},{96,80},{112,96},{1... | collective-permute-start | bytes 559112 | tf_op jit(solution)/shard_map/ppermute | solution.py:36
  151.0 1.0 collective-permute-done.16
  151.9 1.5 collective-permute-done.17
  153.4 4.1 %collective-permute-start.21 = (f32[8,128]{1,0:T(8,128)S(1)}, f32[8,128]{1,0:T(8,128)S(1)}, u32[]{:S(2)}, u32[]{:S(2)}) collective-permute-start(f32[8,128]{1,0:T(8,128)S(1)} %add.61), channel_id=1, source_target_pairs={{0,4},{1,5},{2,6},{3,7},{4,0},{5,1},{6,2},{7,3},{8,12},{9,13},{10,... | collective-permute-start | bytes 12296 | tf_op jit(solution)/shard_map/ppermute | solution.py:44
  157.5 2.8 %collective-permute-start.19 = (bf16[56,1664]{1,0:T(8,128)(2,1)S(1)}, bf16[56,1664]{1,0:T(8,128)(2,1)S(1)}, u32[]{:S(2)}, u32[]{:S(2)}) collective-permute-start(bf16[56,1664]{1,0:T(8,128)(2,1)S(1)} %collective-permute-done.16), channel_id=1, source_target_pairs={{0,16},{16,32},{32,48},{48,64},{64,80},{80,96},{96,112},{112,0},{1... | collective-permute-start | bytes 559112 | tf_op jit(solution)/shard_map/ppermute | solution.py:34
  160.3 4.1 %collective-permute-start.20 = (bf16[56,1664]{1,0:T(8,128)(2,1)S(1)}, bf16[56,1664]{1,0:T(8,128)(2,1)S(1)}, u32[]{:S(2)}, u32[]{:S(2)}) collective-permute-start(bf16[56,1664]{1,0:T(8,128)(2,1)S(1)} %collective-permute-done.17), channel_id=1, source_target_pairs={{0,112},{16,0},{32,16},{48,32},{64,48},{80,64},{96,80},{112,96},{1... | collective-permute-start | bytes 559112 | tf_op jit(solution)/shard_map/ppermute | solution.py:36
  164.5 1.3 collective-permute-done.19
  165.8 1.2 collective-permute-done.20
  166.9 2.2 %collective-permute-start.22 = (f32[8,128]{1,0:T(8,128)S(1)}, f32[8,128]{1,0:T(8,128)S(1)}, u32[]{:S(2)}, u32[]{:S(2)}) collective-permute-start(f32[8,128]{1,0:T(8,128)S(1)} %add.62), channel_id=1, source_target_pairs={{0,128},{128,0},{256,384},{384,256},{1,129},{129,1},{257,385},{385... | collective-permute-start | bytes 12296 | tf_op jit(solution)/shard_map/ppermute | solution.py:44
  169.1 2.3 %collective-permute-start.23 = (bf16[56,1664]{1,0:T(8,128)(2,1)S(1)}, bf16[56,1664]{1,0:T(8,128)(2,1)S(1)}, u32[]{:S(2)}, u32[]{:S(2)}) collective-permute-start(bf16[56,1664]{1,0:T(8,128)(2,1)S(1)} %collective-permute-done.19), channel_id=1, source_target_pairs={{0,16},{16,32},{32,48},{48,64},{64,80},{80,96},{96,112},{112,0},{1... | collective-permute-start | bytes 559112 | tf_op jit(solution)/shard_map/ppermute | solution.py:34
  171.6 5.5 %collective-permute-done.23 = bf16[56,1664]{1,0:T(8,128)(2,1)S(1)} collective-permute-done((bf16[56,1664]{1,0:T(8,128)(2,1)S(1)}, bf16[56,1664]{1,0:T(8,128)(2,1)S(1)}, u32[]{:S(2)}, u32[]{:S(2)}) %collective-permute-start.23) | collective-permute-done | bytes 186400 | tf_op jit(solution)/shard_map/ppermute | solution.py:34
  177.2 1.0 fusion
  178.3 8.9 %collective-permute-start.25 = (bf16[4,56,1664]{2,1,0:T(8,128)(2,1)S(1)}, bf16[4,56,1664]{2,1,0:T(8,128)(2,1)S(1)}, u32[]{:S(2)}, u32[]{:S(2)}) collective-permute-start(bf16[4,56,1664]{2,1,0:T(8,128)(2,1)S(1)} %fusion.7), channel_id=1, source_target_pairs={{0,8},{8,0},{1,9},{9,1},{2,10},{10,2},{3,11},{11,3},{4,12},{12,4},... | collective-permute-start | bytes 2236424 | tf_op jit(solution)/shard_map/ppermute | solution.py:50
  187.2 1.8 collective-permute-done.25
  189.0 1.0 fusion.4
  190.0 3.6 %all-to-all-start.4 = ((bf16[4,56,1664]{2,1,0:T(8,128)(2,1)}), bf16[4,56,1664]{2,1,0:T(8,128)(2,1)S(1)}, u32[]{:S(2)}, u32[]{:S(2)}) async-start(bf16[4,56,1664]{2,1,0:T(8,128)(2,1)} %fusion.4), calls=%async_computation.4 | async-start | bytes 1490944 | tf_op jit(solution)/shard_map/all_to_all | solution.py:52
  193.6 4.8 %collective-permute-start.24 = (f32[8,128]{1,0:T(8,128)S(1)}, f32[8,128]{1,0:T(8,128)S(1)}, u32[]{:S(2)}, u32[]{:S(2)}) collective-permute-start(f32[8,128]{1,0:T(8,128)S(1)} %add.63), channel_id=1, source_target_pairs={{0,256},{128,384},{256,0},{384,128},{1,257},{129,385},{257,1},{385... | collective-permute-start | bytes 12296 | tf_op jit(solution)/shard_map/ppermute | solution.py:44
  198.5 6.8 %collective-permute-done.24 = f32[8,128]{1,0:T(8,128)S(1)} collective-permute-done((f32[8,128]{1,0:T(8,128)S(1)}, f32[8,128]{1,0:T(8,128)S(1)}, u32[]{:S(2)}, u32[]{:S(2)}) %collective-permute-start.24) | collective-permute-done | bytes 4128 | tf_op jit(solution)/shard_map/ppermute | solution.py:44
  205.3 0.5 slice.3
  206.7 0.8 multiply_convert_fusion
  (45 shorter events, 1.2 us)
Async XLA Ops:
  3.4 22.3 %collective-permute-start = (bf16[56,1664]{1,0:T(8,128)(2,1)S(1)}, bf16[56,1664]{1,0:T(8,128)(2,1)S(1)}, u32[]{:S(2)}, u32[]{:S(2)}) collective-permute-start(bf16[56,1664]{1,0:T(8,128)(2,1)S(1)} %get-tuple-element.30), channel_id=1, source_target_pairs={{0,16},{16,32},{32,48},{48,64},{64,80},{80,96},{96,112},{112,0},{1... | collective-permute-start | bytes 559112 | tf_op jit(solution)/shard_map/ppermute | solution.py:34
  8.2 17.5 %collective-permute-start.1 = (bf16[56,1664]{1,0:T(8,128)(2,1)S(1)}, bf16[56,1664]{1,0:T(8,128)(2,1)S(1)}, u32[]{:S(2)}, u32[]{:S(2)}) collective-permute-start(bf16[56,1664]{1,0:T(8,128)(2,1)S(1)} %get-tuple-element.30), channel_id=1, source_target_pairs={{0,112},{16,0},{32,16},{48,32},{64,48},{80,64},{96,80},{112,96},{1... | collective-permute-start | bytes 559112 | tf_op jit(solution)/shard_map/ppermute | solution.py:36
  17.7 36.1 %all-to-all-start = ((bf16[4,56,1664]{2,1,0:T(8,128)(2,1)}), bf16[4,56,1664]{2,1,0:T(8,128)(2,1)S(1)}, u32[]{:S(2)}, u32[]{:S(2)}) async-start(bf16[4,56,1664]{2,1,0:T(8,128)(2,1)} %broadcast_in_dim.7), calls=%async_computation | async-start | bytes 1490944 | tf_op jit(solution)/shard_map/all_to_all | solution.py:64
  21.7 3.9 %collective-permute-start.2 = (f32[8,128]{1,0:T(8,128)S(1)}, f32[8,128]{1,0:T(8,128)S(1)}, u32[]{:S(2)}, u32[]{:S(2)}) collective-permute-start(f32[8,128]{1,0:T(8,128)S(1)} %broadcast_in_dim.6), channel_id=1, source_target_pairs={{0,8},{8,0},{1,9},{9,1},{2,10},{10,2},{3,11},{11,3},{4,12},{12,4},... | collective-permute-start | bytes 12296 | tf_op jit(solution)/shard_map/ppermute | solution.py:44
  25.7 8.5 %collective-permute-start.5 = (f32[8,128]{1,0:T(8,128)S(1)}, f32[8,128]{1,0:T(8,128)S(1)}, u32[]{:S(2)}, u32[]{:S(2)}) collective-permute-start(f32[8,128]{1,0:T(8,128)S(1)} %add.53), channel_id=1, source_target_pairs={{0,16},{16,0},{32,48},{48,32},{64,80},{80,64},{96,112},{112,96},{1... | collective-permute-start | bytes 12296 | tf_op jit(solution)/shard_map/ppermute | solution.py:44
  27.6 9.0 %collective-permute-start.3 = (bf16[56,1664]{1,0:T(8,128)(2,1)S(1)}, bf16[56,1664]{1,0:T(8,128)(2,1)S(1)}, u32[]{:S(2)}, u32[]{:S(2)}) collective-permute-start(bf16[56,1664]{1,0:T(8,128)(2,1)S(1)} %collective-permute-done), channel_id=1, source_target_pairs={{0,16},{16,32},{32,48},{48,64},{64,80},{80,96},{96,112},{112,0},{1... | collective-permute-start | bytes 559112 | tf_op jit(solution)/shard_map/ppermute | solution.py:34
  31.0 7.2 %collective-permute-start.4 = (bf16[56,1664]{1,0:T(8,128)(2,1)S(1)}, bf16[56,1664]{1,0:T(8,128)(2,1)S(1)}, u32[]{:S(2)}, u32[]{:S(2)}) collective-permute-start(bf16[56,1664]{1,0:T(8,128)(2,1)S(1)} %collective-permute-done.1), channel_id=1, source_target_pairs={{0,112},{16,0},{32,16},{48,32},{64,48},{80,64},{96,80},{112,96},{1... | collective-permute-start | bytes 559112 | tf_op jit(solution)/shard_map/ppermute | solution.py:36
  38.2 9.4 %collective-permute-start.8 = (f32[8,128]{1,0:T(8,128)S(1)}, f32[8,128]{1,0:T(8,128)S(1)}, u32[]{:S(2)}, u32[]{:S(2)}) collective-permute-start(f32[8,128]{1,0:T(8,128)S(1)} %add.54), channel_id=1, source_target_pairs={{0,32},{16,48},{32,0},{48,16},{64,96},{80,112},{96,64},{112,80},{1... | collective-permute-start | bytes 12296 | tf_op jit(solution)/shard_map/ppermute | solution.py:44
  41.0 7.5 %collective-permute-start.6 = (bf16[56,1664]{1,0:T(8,128)(2,1)S(1)}, bf16[56,1664]{1,0:T(8,128)(2,1)S(1)}, u32[]{:S(2)}, u32[]{:S(2)}) collective-permute-start(bf16[56,1664]{1,0:T(8,128)(2,1)S(1)} %collective-permute-done.3), channel_id=1, source_target_pairs={{0,16},{16,32},{32,48},{48,64},{64,80},{80,96},{96,112},{112,0},{1... | collective-permute-start | bytes 559112 | tf_op jit(solution)/shard_map/ppermute | solution.py:34
  45.3 6.3 %collective-permute-start.7 = (bf16[56,1664]{1,0:T(8,128)(2,1)S(1)}, bf16[56,1664]{1,0:T(8,128)(2,1)S(1)}, u32[]{:S(2)}, u32[]{:S(2)}) collective-permute-start(bf16[56,1664]{1,0:T(8,128)(2,1)S(1)} %collective-permute-done.4), channel_id=1, source_target_pairs={{0,112},{16,0},{32,16},{48,32},{64,48},{80,64},{96,80},{112,96},{1... | collective-permute-start | bytes 559112 | tf_op jit(solution)/shard_map/ppermute | solution.py:36
  51.6 7.5 %collective-permute-start.9 = (bf16[56,1664]{1,0:T(8,128)(2,1)S(1)}, bf16[56,1664]{1,0:T(8,128)(2,1)S(1)}, u32[]{:S(2)}, u32[]{:S(2)}) collective-permute-start(bf16[56,1664]{1,0:T(8,128)(2,1)S(1)} %collective-permute-done.6), channel_id=1, source_target_pairs={{0,16},{16,32},{32,48},{48,64},{64,80},{80,96},{96,112},{112,0},{1... | collective-permute-start | bytes 559112 | tf_op jit(solution)/shard_map/ppermute | solution.py:34
  53.8 6.9 %collective-permute-start.10 = (bf16[4,56,1664]{2,1,0:T(8,128)(2,1)S(1)}, bf16[4,56,1664]{2,1,0:T(8,128)(2,1)S(1)}, u32[]{:S(2)}, u32[]{:S(2)}) collective-permute-start(bf16[4,56,1664]{2,1,0:T(8,128)(2,1)S(1)} %all-to-all-done), channel_id=1, source_target_pairs={{0,8},{8,0},{1,9},{9,1},{2,10},{10,2},{3,11},{11,3},{4,12},{12,4},... | collective-permute-start | bytes 2236424 | tf_op jit(solution)/shard_map/ppermute | solution.py:65
  59.2 2.9 %copy-start.1 = (bf16[448,1664]{1,0:T(8,128)(2,1)}, bf16[448,1664]{1,0:T(8,128)(2,1)S(1)}, u32[]{:S(2)}) copy-start(bf16[448,1664]{1,0:T(8,128)(2,1)S(1)} %constant_dynamic-update-slice_fusion) | copy-start | bytes 4472836
  81.7 14.9 %all-to-all-start.2 = ((bf16[8,56,448]{2,1,0:T(8,128)(2,1)}), bf16[8,56,448]{2,1,0:T(8,128)(2,1)S(1)}, u32[]{:S(2)}, u32[]{:S(2)}) async-start(bf16[8,56,448]{2,1,0:T(8,128)(2,1)} %broadcast_in_dim.8), calls=%async_computation.2 | async-start | bytes 917504 | tf_op jit(solution)/shard_map/all_to_all | solution.py:75
  100.1 10.1 %collective-permute-start.11 = (bf16[4,56,1664]{2,1,0:T(8,128)(2,1)}, bf16[4,56,1664]{2,1,0:T(8,128)(2,1)}, u32[]{:S(2)}, u32[]{:S(2)}) collective-permute-start(bf16[4,56,1664]{2,1,0:T(8,128)(2,1)} %fusion.6), channel_id=1, source_target_pairs={{0,8},{8,0},{1,9},{9,1},{2,10},{10,2},{3,11},{11,3},{4,12},{12,4},... | collective-permute-start | bytes 2236424 | tf_op jit(solution)/shard_map/ppermute | solution.py:50
  112.4 15.8 %all-to-all-start.3 = ((bf16[4,56,1664]{2,1,0:T(8,128)(2,1)}), bf16[4,56,1664]{2,1,0:T(8,128)(2,1)S(1)}, u32[]{:S(2)}, u32[]{:S(2)}) async-start(bf16[4,56,1664]{2,1,0:T(8,128)(2,1)} %fusion.5), calls=%async_computation.3 | async-start | bytes 1490944 | tf_op jit(solution)/shard_map/all_to_all | solution.py:52
  116.9 8.2 %collective-permute-start.12 = (f32[8,128]{1,0:T(8,128)S(1)}, f32[8,128]{1,0:T(8,128)S(1)}, u32[]{:S(2)}, u32[]{:S(2)}) collective-permute-start(f32[8,128]{1,0:T(8,128)S(1)} %add.55), channel_id=1, source_target_pairs={{0,64},{16,80},{32,96},{48,112},{64,0},{80,16},{96,32},{112,48},{1... | collective-permute-start | bytes 12296 | tf_op jit(solution)/shard_map/ppermute | solution.py:44
  128.4 14.1 %collective-permute-start.13 = (bf16[56,1664]{1,0:T(8,128)(2,1)S(1)}, bf16[56,1664]{1,0:T(8,128)(2,1)S(1)}, u32[]{:S(2)}, u32[]{:S(2)}) collective-permute-start(bf16[56,1664]{1,0:T(8,128)(2,1)S(1)} %get-tuple-element.41), channel_id=1, source_target_pairs={{0,16},{16,32},{32,48},{48,64},{64,80},{80,96},{96,112},{112,0},{1... | collective-permute-start | bytes 559112 | tf_op jit(solution)/shard_map/ppermute | solution.py:34
  132.2 10.3 %collective-permute-start.14 = (bf16[56,1664]{1,0:T(8,128)(2,1)S(1)}, bf16[56,1664]{1,0:T(8,128)(2,1)S(1)}, u32[]{:S(2)}, u32[]{:S(2)}) collective-permute-start(bf16[56,1664]{1,0:T(8,128)(2,1)S(1)} %get-tuple-element.41), channel_id=1, source_target_pairs={{0,112},{16,0},{32,16},{48,32},{64,48},{80,64},{96,80},{112,96},{1... | collective-permute-start | bytes 559112 | tf_op jit(solution)/shard_map/ppermute | solution.py:36
  137.8 4.6 %collective-permute-start.15 = (f32[8,128]{1,0:T(8,128)S(1)}, f32[8,128]{1,0:T(8,128)S(1)}, u32[]{:S(2)}, u32[]{:S(2)}) collective-permute-start(f32[8,128]{1,0:T(8,128)S(1)} %add.59), channel_id=1, source_target_pairs={{0,1},{1,0},{2,3},{3,2},{4,5},{5,4},{6,7},{7,6},{8,9},{9,8},{10,11... | collective-permute-start | bytes 12296 | tf_op jit(solution)/shard_map/ppermute | solution.py:44
  142.5 8.5 %collective-permute-start.18 = (f32[8,128]{1,0:T(8,128)S(1)}, f32[8,128]{1,0:T(8,128)S(1)}, u32[]{:S(2)}, u32[]{:S(2)}) collective-permute-start(f32[8,128]{1,0:T(8,128)S(1)} %add.60), channel_id=1, source_target_pairs={{0,2},{1,3},{2,0},{3,1},{4,6},{5,7},{6,4},{7,5},{8,10},{9,11},{10,... | collective-permute-start | bytes 12296 | tf_op jit(solution)/shard_map/ppermute | solution.py:44
  144.4 7.5 %collective-permute-start.16 = (bf16[56,1664]{1,0:T(8,128)(2,1)S(1)}, bf16[56,1664]{1,0:T(8,128)(2,1)S(1)}, u32[]{:S(2)}, u32[]{:S(2)}) collective-permute-start(bf16[56,1664]{1,0:T(8,128)(2,1)S(1)} %collective-permute-done.13), channel_id=1, source_target_pairs={{0,16},{16,32},{32,48},{48,64},{64,80},{80,96},{96,112},{112,0},{1... | collective-permute-start | bytes 559112 | tf_op jit(solution)/shard_map/ppermute | solution.py:34
  146.4 7.1 %collective-permute-start.17 = (bf16[56,1664]{1,0:T(8,128)(2,1)S(1)}, bf16[56,1664]{1,0:T(8,128)(2,1)S(1)}, u32[]{:S(2)}, u32[]{:S(2)}) collective-permute-start(bf16[56,1664]{1,0:T(8,128)(2,1)S(1)} %collective-permute-done.14), channel_id=1, source_target_pairs={{0,112},{16,0},{32,16},{48,32},{64,48},{80,64},{96,80},{112,96},{1... | collective-permute-start | bytes 559112 | tf_op jit(solution)/shard_map/ppermute | solution.py:36
  153.4 11.1 %collective-permute-start.21 = (f32[8,128]{1,0:T(8,128)S(1)}, f32[8,128]{1,0:T(8,128)S(1)}, u32[]{:S(2)}, u32[]{:S(2)}) collective-permute-start(f32[8,128]{1,0:T(8,128)S(1)} %add.61), channel_id=1, source_target_pairs={{0,4},{1,5},{2,6},{3,7},{4,0},{5,1},{6,2},{7,3},{8,12},{9,13},{10,... | collective-permute-start | bytes 12296 | tf_op jit(solution)/shard_map/ppermute | solution.py:44
  157.5 8.3 %collective-permute-start.19 = (bf16[56,1664]{1,0:T(8,128)(2,1)S(1)}, bf16[56,1664]{1,0:T(8,128)(2,1)S(1)}, u32[]{:S(2)}, u32[]{:S(2)}) collective-permute-start(bf16[56,1664]{1,0:T(8,128)(2,1)S(1)} %collective-permute-done.16), channel_id=1, source_target_pairs={{0,16},{16,32},{32,48},{48,64},{64,80},{80,96},{96,112},{112,0},{1... | collective-permute-start | bytes 559112 | tf_op jit(solution)/shard_map/ppermute | solution.py:34
  160.3 6.6 %collective-permute-start.20 = (bf16[56,1664]{1,0:T(8,128)(2,1)S(1)}, bf16[56,1664]{1,0:T(8,128)(2,1)S(1)}, u32[]{:S(2)}, u32[]{:S(2)}) collective-permute-start(bf16[56,1664]{1,0:T(8,128)(2,1)S(1)} %collective-permute-done.17), channel_id=1, source_target_pairs={{0,112},{16,0},{32,16},{48,32},{64,48},{80,64},{96,80},{112,96},{1... | collective-permute-start | bytes 559112 | tf_op jit(solution)/shard_map/ppermute | solution.py:36
  166.9 4.6 %collective-permute-start.22 = (f32[8,128]{1,0:T(8,128)S(1)}, f32[8,128]{1,0:T(8,128)S(1)}, u32[]{:S(2)}, u32[]{:S(2)}) collective-permute-start(f32[8,128]{1,0:T(8,128)S(1)} %add.62), channel_id=1, source_target_pairs={{0,128},{128,0},{256,384},{384,256},{1,129},{129,1},{257,385},{385... | collective-permute-start | bytes 12296 | tf_op jit(solution)/shard_map/ppermute | solution.py:44
  169.1 8.0 %collective-permute-start.23 = (bf16[56,1664]{1,0:T(8,128)(2,1)S(1)}, bf16[56,1664]{1,0:T(8,128)(2,1)S(1)}, u32[]{:S(2)}, u32[]{:S(2)}) collective-permute-start(bf16[56,1664]{1,0:T(8,128)(2,1)S(1)} %collective-permute-done.19), channel_id=1, source_target_pairs={{0,16},{16,32},{32,48},{48,64},{64,80},{80,96},{96,112},{112,0},{1... | collective-permute-start | bytes 559112 | tf_op jit(solution)/shard_map/ppermute | solution.py:34
  178.3 10.7 %collective-permute-start.25 = (bf16[4,56,1664]{2,1,0:T(8,128)(2,1)S(1)}, bf16[4,56,1664]{2,1,0:T(8,128)(2,1)S(1)}, u32[]{:S(2)}, u32[]{:S(2)}) collective-permute-start(bf16[4,56,1664]{2,1,0:T(8,128)(2,1)S(1)} %fusion.7), channel_id=1, source_target_pairs={{0,8},{8,0},{1,9},{9,1},{2,10},{10,2},{3,11},{11,3},{4,12},{12,4},... | collective-permute-start | bytes 2236424 | tf_op jit(solution)/shard_map/ppermute | solution.py:50
  190.0 16.7 %copy-start = (f32[56,1664]{1,0:T(8,128)S(1)}, f32[56,1664]{1,0:T(8,128)}, u32[]{:S(2)}) copy-start(f32[56,1664]{1,0:T(8,128)} %param.1) | copy-start | bytes 1118212
  190.0 16.5 %all-to-all-start.4 = ((bf16[4,56,1664]{2,1,0:T(8,128)(2,1)}), bf16[4,56,1664]{2,1,0:T(8,128)(2,1)S(1)}, u32[]{:S(2)}, u32[]{:S(2)}) async-start(bf16[4,56,1664]{2,1,0:T(8,128)(2,1)} %fusion.4), calls=%async_computation.4 | async-start | bytes 1490944 | tf_op jit(solution)/shard_map/all_to_all | solution.py:52
  193.6 11.7 %collective-permute-start.24 = (f32[8,128]{1,0:T(8,128)S(1)}, f32[8,128]{1,0:T(8,128)S(1)}, u32[]{:S(2)}, u32[]{:S(2)}) collective-permute-start(f32[8,128]{1,0:T(8,128)S(1)} %add.63), channel_id=1, source_target_pairs={{0,256},{128,384},{256,0},{384,128},{1,257},{129,385},{257,1},{385... | collective-permute-start | bytes 12296 | tf_op jit(solution)/shard_map/ppermute | solution.py:44

commit v2 on v0

v2 whole, which is shorter than its diff:
```python
import math

import jax
import jax.numpy as jnp
from jax import lax
from jax.experimental import pallas as pl
from jax.experimental.pallas import tpu as pltpu
from jax.sharding import Mesh, PartitionSpec as P

M = 3584
N = 13312

coef_a = 3.4445
coef_b = -4.775
coef_c = 2.0315

bf16 = jnp.bfloat16
f32 = jnp.float32


def swap(size, bit):
    return [(i, i ^ bit) for i in range(size)]


def to_all(block, axis, size):
    return lax.all_to_all(jnp.broadcast_to(block[None], (size, *block.shape)), axis, 0, 0)


def other_core(block):
    return lax.ppermute(block, "c", swap(2, 1))


def add_swapped(total, steps):
    for axis, size, bit in steps:
        total = total + lax.ppermute(total, axis, swap(size, bit))
    return total


def rows_dot(left, right):
    return lax.dot_general(left, right, (((1,), (1,)), ((), ())), preferred_element_type=f32)


def depth_dot(left, right):
    return lax.dot_general(left, right, (((0,), (0,)), ((), ())), preferred_element_type=f32)


def split(value):
    high = lax.reduce_precision(value, 8, 7)
    middle = lax.reduce_precision(value - high, 8, 7)
    return high, middle, lax.reduce_precision(value - high - middle, 8, 7)


def in_lanes(lane, parts, rest):
    high, middle, low = parts
    return jnp.where(lane == 0, high, jnp.where(lane == 1, middle, jnp.where(lane == 2, low, rest)))


def local(kernel, out_shape, in_spaces, flops):
    spaces = [pl.BlockSpec(memory_space=space) for space in in_spaces]
    return pl.pallas_call(
        kernel,
        out_shape=out_shape,
        in_specs=spaces,
        out_specs=jax.tree.map(lambda _: pl.BlockSpec(memory_space=pltpu.VMEM), out_shape),
        compiler_params=pltpu.CompilerParams(vmem_limit_bytes=32 * 1024 * 1024),
        cost_estimate=pl.CostEstimate(flops=flops, bytes_accessed=3_000_000, transcendentals=0),
    )


def add_shares_kernel(shares_ref, piece_ref, copies_ref):
    summed = shares_ref[0].astype(f32)
    for share in range(1, 8):
        summed += shares_ref[share].astype(f32)
    total = jnp.sum(summed[:, 224:], axis=1, keepdims=True)
    high = total.astype(bf16).astype(f32)
    middle = (total - high).astype(bf16).astype(f32)
    lane = lax.broadcasted_iota(jnp.int32, (112, 256), 1) - 224
    rest = jnp.where(lane < 0, summed, 0.0)
    piece = in_lanes(lane, (high, middle, total - high - middle), rest).astype(bf16)
    piece_ref[...] = piece
    for share in range(8):
        copies_ref[share] = piece


def polynomial_kernel(left_ref, right_ref, gram_ref, poly_ref, factor_ref):
    square = jnp.zeros((112, 224), f32)
    lanes = jnp.zeros((112, 32), f32)
    for g in range(16):
        left = left_ref[g]
        square += jnp.dot(left[:, :224], right_ref[g][:, :224], preferred_element_type=f32)
        lanes += left[:, 224:].astype(f32)
    total = jnp.sum(lanes, axis=1, keepdims=True)
    factor = math.sqrt(M) / 3.0 / (jnp.sqrt(total) + 1e-07)
    factor2 = factor * factor
    gram = (gram_ref[:, :224].astype(f32) * factor2).astype(bf16).astype(f32)
    square = ((square * factor2) * factor2).astype(bf16).astype(f32)
    poly = (coef_b * gram + coef_c * square).astype(bf16)
    for g in range(8):
        poly_ref[g] = poly
    factor_ref[...] = jnp.broadcast_to(factor, (112, 128))


def update_kernel(momentum_ref, product_ref, factor_ref, update_ref):
    factor = factor_ref[:56, :1]
    product = product_ref[0].astype(f32)
    for x in range(1, 4):
        product += product_ref[x].astype(f32)
    iterate = (momentum_ref[...] * factor).astype(bf16).astype(f32)
    update = (coef_a * iterate + factor * product) * (0.2 * math.sqrt(N))
    update_ref[...] = update.astype(bf16)


def per_device(momentum):
    core = lax.axis_index("c")
    raw = momentum.astype(bf16)

    rows_own = to_all(raw, "z", 8).reshape(448, 1664)
    rows_x = lax.all_gather(raw, "x", axis=0, tiled=True)
    rows_x_other = other_core(rows_x)
    late, rows_x_other = lax.optimization_barrier((momentum, rows_x_other))
    total = jnp.broadcast_to(jnp.sum(late * late).reshape(1, 1), (8, 128))
    total = add_swapped(total, [("x", 4, 1), ("x", 4, 2)])
    lane = lax.broadcasted_iota(jnp.int32, (1, 32), 1)
    lanes = in_lanes(lane, split(total[:1, :32]), 0.0).astype(bf16)
    rows_own, rows_x, rows_x_other, lanes = lax.optimization_barrier(
        (rows_own, rows_x, rows_x_other, lanes)
    )

    part_own = rows_dot(rows_own, rows_x).astype(bf16).reshape(8, 1, 56, 224)
    part_given = rows_dot(rows_own, rows_x_other).astype(bf16)
    part_other = other_core(part_given).reshape(8, 1, 56, 224)
    part = jnp.where(
        core == 0,
        jnp.concatenate([part_own, part_other], axis=1),
        jnp.concatenate([part_other, part_own], axis=1),
    ).reshape(8, 112, 224)
    part = jnp.concatenate([part, jnp.broadcast_to(lanes[None], (8, 112, 32))], axis=2)
    piece, copies = local(
        add_shares_kernel,
        [jax.ShapeDtypeStruct((112, 256), bf16), jax.ShapeDtypeStruct((8, 112, 256), bf16)],
        [pltpu.VMEM],
        1_000_000,
    )(lax.all_to_all(part, "y", 0, 0))

    right = lax.all_to_all(copies, "y", 0, 0).reshape(8, 2, 56, 256)
    right, piece = lax.optimization_barrier((right, piece))
    right = to_all(right, "x", 4).transpose(1, 2, 0, 3, 4).reshape(16, 224, 256)
    left = lax.all_gather(piece, ("z", "c"), axis=0)
    poly, factor = local(
        polynomial_kernel,
        [jax.ShapeDtypeStruct((8, 112, 224), bf16), jax.ShapeDtypeStruct((112, 128), f32)],
        [pltpu.VMEM] * 3,
        2 * 112 * 224 * M,
    )(left, right, piece)

    poly, rows_own = lax.optimization_barrier((poly, rows_own))
    rows_other = other_core(rows_own)
    poly = lax.all_to_all(poly, "y", 0, 0).reshape(8, 2, 56, 224)
    poly_own = lax.dynamic_index_in_dim(poly, core, 1, keepdims=False).reshape(448, 224)
    poly_other = lax.dynamic_index_in_dim(poly, 1 - core, 1, keepdims=False).reshape(448, 224)
    product = depth_dot(poly_own, rows_own) + depth_dot(poly_other, rows_other)
    product = lax.all_to_all(product.astype(bf16).reshape(4, 56, 1664), "x", 0, 0)
    return local(
        update_kernel,
        jax.ShapeDtypeStruct((56, 1664), bf16),
        [pltpu.VMEM] * 3,
        1_000_000,
    )(momentum, product, factor)


def solution(mesh):
    fine = Mesh(mesh.devices.reshape(4, 8, 2, 8), ("x", "z", "c", "y"))
    spec = P(("x", "z", "c"), "y")
    return jax.shard_map(
        per_device, mesh=fine, in_specs=(spec,), out_specs=spec, check_vma=False
    )
```

time: 375 us -> 166 us (0.44)
  waiting for transfers between devices: 175 us -> 26.5 us
  blocking collectives: 158 us -> 84.8 us
  starting transfers between devices: 0.04 us -> 40.7 us
  matrix products: 18.2 us -> 3.81 us
  between operations: 14.2 us -> 0.17 us
    all_gather x2 -> x0, waiting for transfers between devices: 175 us -> none  [the longest x1 89.3 us: per_device(): column_slab = lax.all_gather(scaled_rows, 'rows', axis=0, tiled=True)]
    psum x2 -> x0, blocking collectives: 138 us -> none  [the longest x1 106 us: per_device(): total = lax.psum(jnp.sum(momentum * momentum), ('rows', 'cols'))]
    all_to_all x0 -> x3, blocking collectives: none -> 51.8 us  [the longest x1 21.9 us: per_device(): lax.all_to_all(part, 'y', 0, 0)]
    ppermute x0 -> x5, starting transfers between devices: none -> 22.2 us  [the longest x3 14.1 us: other_core(): return lax.ppermute(block, 'c', swap(2, 1))]
    all_to_all x0 -> x3, waiting for transfers between devices: none -> 21.1 us  [the longest x1 16.6 us: per_device(): poly = lax.all_to_all(poly, 'y', 0, 0).reshape(8, 2, 56, 224)]
    all_to_all x0 -> x3, starting transfers between devices: none -> 18.5 us  [the longest x2 15 us: to_all(): lax.all_to_all(jnp.broadcast_to(block[None], (size, *block.shape)), axis,...]
    dot_general x3 -> x4, matrix products: 18.2 us -> 3.81 us  [the longest x2 2.6 us: depth_dot(): lax.dot_general(left, right, (((0,), (0,)), ((), ())), preferred_element_...]
    all_gather x1 -> x2, blocking collectives: 20.3 us -> 33 us  [the longest x1 20.5 us: per_device(): left = lax.all_gather(piece, ('z', 'c'), axis=0)]
  transfers between devices with their start and end apart: 2 -> 8, of which waited for: 2 -> 6; matrix products, arithmetic and copies ran while one was open for 0% -> 2% of each run, Pallas kernels for 0% -> 0%
where the time goes in v2:
time: 166 us; the launch traced here: 165 us
  blocking collectives  84.8 us (51%)
  starting transfers between devices  40.7 us (25%)
  waiting for transfers between devices  26.5 us (16%)
  matrix products  3.81 us (2%)
  local copies, waits for them, and re-layouts  3.66 us (2%)
  other arithmetic  3.24 us (2%)
  Pallas kernels  2.42 us (1%)
    all_to_all x1, blocking collectives, per_device(): lax.all_to_all(part, 'y', 0, 0)  21.9 us
    all_gather x1, blocking collectives, per_device(): left = lax.all_gather(piece, ('z', 'c'), axis=0)  20.5 us
    all_to_all x1, waiting for transfers between devices, per_device(): poly = lax.all_to_all(poly, 'y', 0, 0).reshape(8, 2, 56, 224)  16.6 us
    all_to_all x1, blocking collectives, per_device(): right = lax.all_to_all(copies, 'y', 0, 0).reshape(8, 2, 56, 256)  16.3 us
    all_to_all x2, starting transfers between devices, to_all(): lax.all_to_all(jnp.broadcast_to(block[None], (size, *block.shape)), axis,...  15 us
    ppermute x3, starting transfers between devices, other_core(): return lax.ppermute(block, 'c', swap(2, 1))  14.1 us
    all_to_all x1, blocking collectives, per_device(): lax.all_to_all(product.astype(bf16).reshape(4, 56, 1664), 'x', 0, 0)  13.6 us
    all_gather x1, blocking collectives, per_device(): rows_x = lax.all_gather(raw, 'x', axis=0, tiled=True)  12.5 us
  transfers between devices with their start and end apart: 8, of which 6 were waited for; matrix products, arithmetic and copies ran while one was open for 2% of the time, Pallas kernels for 0%

profile of v2, /device:TPU:1, one launch (start us, length us, event | category | flops | bytes accessed | tf_op | source)
XLA Modules:
  0.0 165.3 jit_solution(10395856304643022953)
XLA Ops:
  0.0 1.0 convert_element_type.15
  1.0 1.2 broadcast_in_dim.14
  2.2 0.0 copy-start
  2.2 11.0 %all-to-all-start = ((bf16[8,56,1664]{2,1,0:T(8,128)(2,1)}), bf16[8,56,1664]{2,1,0:T(8,128)(2,1)S(1)}, u32[]{:S(2)}, u32[]{:S(2)}) async-start(bf16[8,56,1664]{2,1,0:T(8,128)(2,1)} %broadcast_in_dim.14), calls=%async_computation | async-start | bytes 2981888 | tf_op jit(solution)/shard_map/all_to_all | solution.py:26
  13.2 12.5 %all_gather.9 = bf16[224,1664]{1,0:T(8,128)(2,1)S(1)} all-gather(bf16[56,1664]{1,0:T(8,128)(2,1)S(1)} %convert_element_type.15), channel_id=1, replica_groups=mesh['x'=4,'z'=8,'c'=2,'y'=8] {'x'}, dimensions={0}, use_global_device_ids=true | all-gather | bytes 931840 | tf_op jit(solution)/shard_map/all_gather | solution.py:118
  25.8 3.9 %collective-permute-start = (bf16[224,1664]{1,0:T(8,128)(2,1)S(1)}, bf16[224,1664]{1,0:T(8,128)(2,1)S(1)}, u32[]{:S(2)}, u32[]{:S(2)}) collective-permute-start(bf16[224,1664]{1,0:T(8,128)(2,1)S(1)} %all_gather.9), channel_id=1, source_target_pairs={{0,8},{8,0},{1,9},{9,1},{2,10},{10,2},{3,11},{11,3},{4,12},{12,4},... | collective-permute-start | bytes 2236424 | tf_op jit(solution)/shard_map/ppermute | solution.py:30
  29.7 1.8 %collective-permute-done = bf16[224,1664]{1,0:T(8,128)(2,1)S(1)} collective-permute-done((bf16[224,1664]{1,0:T(8,128)(2,1)S(1)}, bf16[224,1664]{1,0:T(8,128)(2,1)S(1)}, u32[]{:S(2)}, u32[]{:S(2)}) %collective-permute-start) | collective-permute-done | bytes 745504 | tf_op jit(solution)/shard_map/ppermute | solution.py:30
  31.5 0.0 copy-done
  31.5 0.7 multiply_reduce_fusion
  32.2 0.6 broadcast_in_dim.15
  32.9 3.8 %collective-permute-start.1 = (f32[8,128]{1,0:T(8,128)S(1)}, f32[8,128]{1,0:T(8,128)S(1)}, u32[]{:S(2)}, u32[]{:S(2)}) collective-permute-start(f32[8,128]{1,0:T(8,128)S(1)} %broadcast_in_dim.15), channel_id=1, source_target_pairs={{0,128},{128,0},{256,384},{384,256},{1,129},{129,1},{257,385},{385... | collective-permute-start | bytes 12296 | tf_op jit(solution)/shard_map/ppermute | solution.py:35
  36.7 1.3 collective-permute-done.1
  38.0 0.6 broadcast_add_fusion
  38.6 4.3 %collective-permute-start.2 = (f32[8,128]{1,0:T(8,128)S(1)}, f32[8,128]{1,0:T(8,128)S(1)}, u32[]{:S(2)}, u32[]{:S(2)}) collective-permute-start(f32[8,128]{1,0:T(8,128)S(1)} %broadcast_add_fusion), channel_id=1, source_target_pairs={{0,256},{128,384},{256,0},{384,128},{1,257},{129,385},{257,1},{385... | collective-permute-start | bytes 12296 | tf_op jit(solution)/shard_map/ppermute | solution.py:35
  42.9 1.8 %collective-permute-done.2 = f32[8,128]{1,0:T(8,128)S(1)} collective-permute-done((f32[8,128]{1,0:T(8,128)S(1)}, f32[8,128]{1,0:T(8,128)S(1)}, u32[]{:S(2)}, u32[]{:S(2)}) %collective-permute-start.2) | collective-permute-done | bytes 4128 | tf_op jit(solution)/shard_map/ppermute | solution.py:35
  44.8 0.6 fusion.12
  45.4 4.6 %all-to-all-done = bf16[8,56,1664]{2,1,0:T(8,128)(2,1)S(1)} async-done(((bf16[8,56,1664]{2,1,0:T(8,128)(2,1)}), bf16[8,56,1664]{2,1,0:T(8,128)(2,1)S(1)}, u32[]{:S(2)}, u32[]{:S(2)}) %all-to-all-start) | async-done | bytes 1490976 | tf_op jit(solution)/shard_map/all_to_all | solution.py:26
  50.0 0.0 copy-start.1
  50.0 0.6 convolution_convert_fusion
  50.6 4.3 %collective-permute-start.3 = (bf16[448,224]{1,0:T(8,128)(2,1)S(1)}, bf16[448,224]{1,0:T(8,128)(2,1)S(1)}, u32[]{:S(2)}, u32[]{:S(2)}) collective-permute-start(bf16[448,224]{1,0:T(8,128)(2,1)S(1)} %convolution_convert_fusion), channel_id=1, source_target_pairs={{0,8},{8,0},{1,9},{9,1},{2,10},{10,2},{3,11},{11,3},{4,12},{12,4},... | collective-permute-start | bytes 602120 | tf_op jit(solution)/shard_map/ppermute | solution.py:30
  54.9 0.1 pad.1.clone
  55.0 0.6 convolution_convert_fusion.1
  55.6 0.0 copy-done.1
  55.6 0.4 collective-permute-done.3
  56.0 0.1 maximum_select_fusion
  56.2 0.1 pad_maximum_fusion
  56.3 21.9 %all_to_all.30.shares_ref = bf16[8,112,256]{2,1,0:T(8,128)(2,1)S(1)} all-to-all(bf16[8,112,256]{2,1,0:T(8,128)(2,1)S(1)} %pad_maximum_fusion), channel_id=1, replica_groups=mesh['x'=4,'z'=8,'c'=2,'y'=8] {'y'}, dimensions={0} | all-to-all | bytes 917504 | tf_op jit(solution)/shard_map/all_to_all | solution.py:143
  78.1 0.2 shard_map.17
  78.4 16.3 %all_to_all.31 = bf16[8,112,256]{2,1,0:T(8,128)(2,1)S(1)} all-to-all(bf16[8,112,256]{2,1,0:T(8,128)(2,1)S(1)} %get-tuple-element.25), channel_id=1, replica_groups=mesh['x'=4,'z'=8,'c'=2,'y'=8] {'y'}, dimensions={0} | all-to-all | bytes 917504 | tf_op jit(solution)/shard_map/all_to_all | solution.py:145
  94.6 1.4 broadcast_in_dim.34
  96.0 4.0 %all-to-all-start.3 = ((bf16[4,8,2,56,256]{4,3,2,1,0:T(8,128)(2,1)}), bf16[4,8,2,56,256]{4,3,2,1,0:T(8,128)(2,1)S(1)}, u32[]{:S(2)}, u32[]{:S(2)}) async-start(bf16[4,8,2,56,256]{4,3,2,1,0:T(8,128)(2,1)} %broadcast_in_dim.34), calls=%async_computation.3 | async-start | bytes 3670016 | tf_op jit(solution)/shard_map/all_to_all | solution.py:26
  100.0 20.5 %all-gather = bf16[1792,256]{1,0:T(8,128)(2,1)S(1)} all-gather(bf16[112,256]{1,0:T(8,128)(2,1)S(1)} %get-tuple-element.27.gram_ref), channel_id=2, replica_groups=mesh['x'=4,'z'=8,'c'=2,'y'=8] {'z','c'}, dimensions={0}, use_global_device_ids=true | all-gather | bytes 974848 | tf_op jit(solution)/shard_map/all_gather | solution.py:148
  120.5 0.0 all-to-all-done.3
  120.5 0.2 copy.10
  120.7 0.0 copy-start.2
  120.7 1.3 shard_map.18
  122.0 0.1 copy-done.2
  122.1 5.9 %collective-permute-start.4 = (bf16[448,1664]{1,0:T(8,128)(2,1)S(1)}, bf16[448,1664]{1,0:T(8,128)(2,1)}, u32[]{:S(2)}, u32[]{:S(2)}) collective-permute-start(bf16[448,1664]{1,0:T(8,128)(2,1)S(1)} %bitcast.32), channel_id=1, source_target_pairs={{0,8},{8,0},{1,9},{9,1},{2,10},{10,2},{3,11},{11,3},{4,12},{12,4},... | collective-permute-start | bytes 4472840 | tf_op jit(solution)/shard_map/ppermute | solution.py:30
  128.0 3.5 %all-to-all-start.4 = ((bf16[8,112,224]{2,1,0:T(8,128)(2,1)}), bf16[8,112,224]{2,1,0:T(8,128)(2,1)S(1)}, u32[]{:S(2)}, u32[]{:S(2)}) async-start(bf16[8,112,224]{2,1,0:T(8,128)(2,1)} %get-tuple-element.30), calls=%async_computation.4 | async-start | bytes 917504 | tf_op jit(solution)/shard_map/all_to_all | solution.py:158
  131.5 16.6 %all-to-all-done.4 = bf16[8,112,224]{2,1,0:T(8,128)(2,1)S(1)} async-done(((bf16[8,112,224]{2,1,0:T(8,128)(2,1)}), bf16[8,112,224]{2,1,0:T(8,128)(2,1)S(1)}, u32[]{:S(2)}, u32[]{:S(2)}) %all-to-all-start.4) | async-done | bytes 401440 | tf_op jit(solution)/shard_map/all_to_all | solution.py:158
  148.1 0.6 fusion.3
  148.7 0.0 collective-permute-done.4
  148.7 2.0 %fusion = bf16[224,1664]{1,0:T(8,128)(2,1)S(1)} fusion(f32[224,1664]{1,0:T(8,128)S(1)} %fusion.3, bf16[448,224]{1,0:T(8,128)(2,1)S(1)} %bitcast.39, bf16[448,1664]{1,0:T(8,128)(2,1)} %collective-permute-done.4), kind=kOutput, calls=%fused_computation.1 | convolution fusion | flops 334716928 | bytes 3928064 | tf_op jit(solution)/shard_map/dot_general | solution.py:44
  150.7 13.6 %all_to_all.32.product_ref = bf16[4,56,1664]{2,1,0:T(8,128)(2,1)S(1)} all-to-all(bf16[4,56,1664]{2,1,0:T(8,128)(2,1)S(1)} %bitcast.34), channel_id=1, replica_groups=mesh['x'=4,'z'=8,'c'=2,'y'=8] {'x'}, dimensions={0} | all-to-all | bytes 1490944 | tf_op jit(solution)/shard_map/all_to_all | solution.py:162
  164.3 0.9 shard_map.19
  (2 shorter events, 0.0 us)
Async XLA Ops:
  2.2 29.3 %copy-start = (f32[56,1664]{1,0:T(8,128)S(1)}, f32[56,1664]{1,0:T(8,128)}, u32[]{:S(2)}) copy-start(f32[56,1664]{1,0:T(8,128)} %momentum_ref.1) | copy-start | bytes 1118212
  2.2 47.8 %all-to-all-start = ((bf16[8,56,1664]{2,1,0:T(8,128)(2,1)}), bf16[8,56,1664]{2,1,0:T(8,128)(2,1)S(1)}, u32[]{:S(2)}, u32[]{:S(2)}) async-start(bf16[8,56,1664]{2,1,0:T(8,128)(2,1)} %broadcast_in_dim.14), calls=%async_computation | async-start | bytes 2981888 | tf_op jit(solution)/shard_map/all_to_all | solution.py:26
  25.8 5.7 %collective-permute-start = (bf16[224,1664]{1,0:T(8,128)(2,1)S(1)}, bf16[224,1664]{1,0:T(8,128)(2,1)S(1)}, u32[]{:S(2)}, u32[]{:S(2)}) collective-permute-start(bf16[224,1664]{1,0:T(8,128)(2,1)S(1)} %all_gather.9), channel_id=1, source_target_pairs={{0,8},{8,0},{1,9},{9,1},{2,10},{10,2},{3,11},{11,3},{4,12},{12,4},... | collective-permute-start | bytes 2236424 | tf_op jit(solution)/shard_map/ppermute | solution.py:30
  32.9 5.1 %collective-permute-start.1 = (f32[8,128]{1,0:T(8,128)S(1)}, f32[8,128]{1,0:T(8,128)S(1)}, u32[]{:S(2)}, u32[]{:S(2)}) collective-permute-start(f32[8,128]{1,0:T(8,128)S(1)} %broadcast_in_dim.15), channel_id=1, source_target_pairs={{0,128},{128,0},{256,384},{384,256},{1,129},{129,1},{257,385},{385... | collective-permute-start | bytes 12296 | tf_op jit(solution)/shard_map/ppermute | solution.py:35
  38.6 6.2 %collective-permute-start.2 = (f32[8,128]{1,0:T(8,128)S(1)}, f32[8,128]{1,0:T(8,128)S(1)}, u32[]{:S(2)}, u32[]{:S(2)}) collective-permute-start(f32[8,128]{1,0:T(8,128)S(1)} %broadcast_add_fusion), channel_id=1, source_target_pairs={{0,256},{128,384},{256,0},{384,128},{1,257},{129,385},{257,1},{385... | collective-permute-start | bytes 12296 | tf_op jit(solution)/shard_map/ppermute | solution.py:35
  50.0 5.6 %copy-start.1 = (bf16[8,56,1664]{2,1,0:T(8,128)(2,1)}, bf16[8,56,1664]{2,1,0:T(8,128)(2,1)S(1)}, u32[]{:S(2)}) copy-start(bf16[8,56,1664]{2,1,0:T(8,128)(2,1)S(1)} %all-to-all-done) | copy-start | bytes 4472836
  50.6 5.4 %collective-permute-start.3 = (bf16[448,224]{1,0:T(8,128)(2,1)S(1)}, bf16[448,224]{1,0:T(8,128)(2,1)S(1)}, u32[]{:S(2)}, u32[]{:S(2)}) collective-permute-start(bf16[448,224]{1,0:T(8,128)(2,1)S(1)} %convolution_convert_fusion), channel_id=1, source_target_pairs={{0,8},{8,0},{1,9},{9,1},{2,10},{10,2},{3,11},{11,3},{4,12},{12,4},... | collective-permute-start | bytes 602120 | tf_op jit(solution)/shard_map/ppermute | solution.py:30
  96.0 24.5 %all-to-all-start.3 = ((bf16[4,8,2,56,256]{4,3,2,1,0:T(8,128)(2,1)}), bf16[4,8,2,56,256]{4,3,2,1,0:T(8,128)(2,1)S(1)}, u32[]{:S(2)}, u32[]{:S(2)}) async-start(bf16[4,8,2,56,256]{4,3,2,1,0:T(8,128)(2,1)} %broadcast_in_dim.34), calls=%async_computation.3 | async-start | bytes 3670016 | tf_op jit(solution)/shard_map/all_to_all | solution.py:26
  120.7 1.4 copy-start.2
  122.1 26.6 %collective-permute-start.4 = (bf16[448,1664]{1,0:T(8,128)(2,1)S(1)}, bf16[448,1664]{1,0:T(8,128)(2,1)}, u32[]{:S(2)}, u32[]{:S(2)}) collective-permute-start(bf16[448,1664]{1,0:T(8,128)(2,1)S(1)} %bitcast.32), channel_id=1, source_target_pairs={{0,8},{8,0},{1,9},{9,1},{2,10},{10,2},{3,11},{11,3},{4,12},{12,4},... | collective-permute-start | bytes 4472840 | tf_op jit(solution)/shard_map/ppermute | solution.py:30
  128.0 20.1 %all-to-all-start.4 = ((bf16[8,112,224]{2,1,0:T(8,128)(2,1)}), bf16[8,112,224]{2,1,0:T(8,128)(2,1)S(1)}, u32[]{:S(2)}, u32[]{:S(2)}) async-start(bf16[8,112,224]{2,1,0:T(8,128)(2,1)} %get-tuple-element.30), calls=%async_computation.4 | async-start | bytes 917504 | tf_op jit(solution)/shard_map/all_to_all | solution.py:158

commit v3 on v2

v3 whole, which is shorter than its diff:
```python
import math

import jax
import jax.numpy as jnp
from jax import lax
from jax.experimental import pallas as pl
from jax.experimental.pallas import tpu as pltpu
from jax.sharding import Mesh, PartitionSpec as P

M = 3584
N = 13312

coef_a = 3.4445
coef_b = -4.775
coef_c = 2.0315

bf16 = jnp.bfloat16
f32 = jnp.float32


def swap(size, bit):
    return [(i, i ^ bit) for i in range(size)]


def from_next_z(block):
    up = [(2 * z, 2 * ((z + 1) % 8)) for z in range(8)]
    down = [(2 * z + 1, 2 * ((z - 1) % 8) + 1) for z in range(8)]
    return lax.ppermute(block, ("zh", "zl", "c"), up + down)


def other_core(block):
    return lax.ppermute(block, "c", swap(2, 1))


def rows_dot(left, right):
    return lax.dot_general(left, right, (((1,), (1,)), ((), ())), preferred_element_type=f32)


def in_lanes(first, total, rest):
    high = total.astype(bf16).astype(f32)
    middle = (total - high).astype(bf16).astype(f32)
    lane = lax.broadcasted_iota(jnp.int32, rest.shape, 1) - first
    low = jnp.where(lane == 2, total - high - middle, rest)
    return jnp.where(lane == 0, high, jnp.where(lane == 1, middle, low))


def local(kernel, out_shape, in_spaces, flops):
    spaces = [pl.BlockSpec(memory_space=space) for space in in_spaces]
    return pl.pallas_call(
        kernel,
        out_shape=out_shape,
        in_specs=spaces,
        out_specs=jax.tree.map(lambda _: pl.BlockSpec(memory_space=pltpu.VMEM), out_shape),
        compiler_params=pltpu.CompilerParams(vmem_limit_bytes=32 * 1024 * 1024),
        cost_estimate=pl.CostEstimate(flops=flops, bytes_accessed=3_000_000, transcendentals=0),
    )


def start_kernel(momentum_ref, raw_ref, copies_ref):
    momentum = momentum_ref[...]
    raw = momentum.astype(bf16)
    for zh in range(4):
        copies_ref[zh] = raw
    total = jnp.sum(momentum * momentum, keepdims=True)
    more = in_lanes(0, jnp.broadcast_to(total, (8, 1664)), jnp.zeros((8, 1664), f32))
    raw_ref[...] = jnp.concatenate([momentum, more], axis=0).astype(bf16)


def copies_kernel(block_ref, copies_ref):
    for x in range(4):
        copies_ref[x] = block_ref[...]


def parts_kernel(place_ref, totals_ref, part_a_ref, part_b_ref, part_c_ref, rows_ref, rows_x_ref, parts_ref):
    zl, core = place_ref[0], place_ref[1]
    part_d = lax.dot_general(
        rows_ref[...], rows_x_ref[...], (((1,), (1,)), ((), ())), preferred_element_type=f32
    )
    total = jnp.zeros((8, 128), f32)
    for x in range(4):
        total += totals_ref[x, :, :128].astype(f32)[56:]
    total = jnp.sum(total[:1], axis=1, keepdims=True)
    lanes = in_lanes(0, jnp.broadcast_to(total, (56, 32)), jnp.zeros((56, 32), f32))
    for part, l, c in (
        (part_a_ref, zl, core),
        (part_b_ref, 1 - zl, core),
        (part_c_ref, zl, 1 - core),
        (part_d, 1 - zl, 1 - core),
    ):
        for zh in range(4):
            block = jnp.concatenate([part[56 * zh : 56 * zh + 56, :], lanes], axis=1)
            parts_ref[zh, l, c] = block.astype(bf16)


def product_kernel(place_ref, poly_ref, rows_a_ref, rows_b_ref, rows_c_ref, rows_d_ref, product_ref):
    zl, core = place_ref[0], place_ref[1]
    product = None
    for rows, l, c in (
        (rows_a_ref, zl, core),
        (rows_b_ref, 1 - zl, core),
        (rows_c_ref, zl, 1 - core),
        (rows_d_ref, 1 - zl, 1 - core),
    ):
        poly = jnp.concatenate([poly_ref[zh, l, c].astype(f32) for zh in range(4)], axis=0)
        term = lax.dot_general(
            poly.astype(bf16), rows[...], (((0,), (0,)), ((), ())), preferred_element_type=f32
        )
        product = term if product is None else product + term
    for x in range(4):
        product_ref[x] = product[56 * x : 56 * x + 56].astype(bf16)


def add_shares_kernel(shares_ref, piece_ref, copies_ref):
    summed = shares_ref[0].astype(f32)
    for share in range(1, 8):
        summed += shares_ref[share].astype(f32)
    total = jnp.sum(summed[:, 224:], axis=1, keepdims=True)
    lane = lax.broadcasted_iota(jnp.int32, (112, 256), 1)
    piece = in_lanes(224, total, jnp.where(lane < 224, summed, 0.0)).astype(bf16)
    piece_ref[...] = piece
    for share in range(8):
        copies_ref[share] = piece


def polynomial_kernel(left_ref, right_ref, gram_ref, poly_ref, factor_ref):
    square = jnp.zeros((112, 224), f32)
    lanes = jnp.zeros((112, 32), f32)
    for g in range(16):
        left = left_ref[g]
        right = jnp.concatenate(
            [right_ref[x, g // 2, g % 2].astype(f32) for x in range(4)], axis=0
        ).astype(bf16)
        square += jnp.dot(left[:, :224], right[:, :224], preferred_element_type=f32)
        lanes += left[:, 224:].astype(f32)
    total = jnp.sum(lanes, axis=1, keepdims=True)
    factor = math.sqrt(M) / 3.0 / (jnp.sqrt(total) + 1e-07)
    factor2 = factor * factor
    gram = (gram_ref[:, :224].astype(f32) * factor2).astype(bf16).astype(f32)
    square = ((square * factor2) * factor2).astype(bf16).astype(f32)
    poly = (coef_b * gram + coef_c * square).astype(bf16)
    for g in range(8):
        poly_ref[g] = poly
    factor_ref[...] = jnp.broadcast_to(factor, (112, 128))


def update_kernel(momentum_ref, product_ref, factor_ref, update_ref):
    factor = factor_ref[:56, :1]
    product = product_ref[0].astype(f32)
    for x in range(1, 4):
        product += product_ref[x].astype(f32)
    iterate = (momentum_ref[...] * factor).astype(bf16).astype(f32)
    update = (coef_a * iterate + factor * product) * (0.2 * math.sqrt(N))
    update_ref[...] = update.astype(bf16)


def per_device(momentum):
    place = jnp.stack([lax.axis_index("zl"), lax.axis_index("c")]).astype(jnp.int32)
    raw, copies = local(
        start_kernel,
        [jax.ShapeDtypeStruct((64, 1664), bf16), jax.ShapeDtypeStruct((4, 56, 1664), bf16)],
        [pltpu.VMEM],
        1_000_000,
    )(momentum)

    rows_a = lax.all_to_all(copies, "zh", 0, 0).reshape(224, 1664)
    gathered_x = lax.all_gather(raw, "x", axis=0)
    rows_x = gathered_x[:, :56].reshape(224, 1664)
    rows_a, rows_x = lax.optimization_barrier((rows_a, rows_x))
    rows_b = from_next_z(rows_a)
    rows_c = other_core(rows_a)
    rows_d = other_core(rows_b)

    parts = local(
        parts_kernel,
        jax.ShapeDtypeStruct((4, 2, 2, 56, 256), bf16),
        [pltpu.SMEM] + [pltpu.VMEM] * 6,
        2 * 224 * 224 * 1664,
    )(
        place,
        gathered_x[:, :, :128],
        *(rows_dot(rows, rows_x) for rows in (rows_a, rows_b, rows_c)),
        rows_d,
        rows_x,
    )
    piece, copies = local(
        add_shares_kernel,
        [jax.ShapeDtypeStruct((112, 256), bf16), jax.ShapeDtypeStruct((8, 112, 256), bf16)],
        [pltpu.VMEM],
        1_000_000,
    )(lax.all_to_all(parts.reshape(8, 112, 256), "y", 0, 0))

    right = lax.all_to_all(copies, "y", 0, 0)
    right, piece = lax.optimization_barrier((right, piece))
    copies = local(
        copies_kernel, jax.ShapeDtypeStruct((4, 8, 112, 256), bf16), [pltpu.VMEM], 1_000_000
    )(right)
    right = lax.all_to_all(copies, "x", 0, 0).reshape(4, 8, 2, 56, 256)
    left = lax.all_gather(piece, ("zh", "zl", "c"), axis=0)
    poly, factor = local(
        polynomial_kernel,
        [jax.ShapeDtypeStruct((8, 112, 224), bf16), jax.ShapeDtypeStruct((112, 128), f32)],
        [pltpu.VMEM] * 3,
        2 * 112 * 224 * M,
    )(left, right, piece)

    poly = lax.all_to_all(poly, "y", 0, 0).reshape(4, 2, 2, 56, 224)
    product = local(
        product_kernel,
        jax.ShapeDtypeStruct((4, 56, 1664), bf16),
        [pltpu.SMEM] + [pltpu.VMEM] * 5,
        2 * 896 * 224 * 1664,
    )(place, poly, rows_a, rows_b, rows_c, rows_d)
    return local(
        update_kernel,
        jax.ShapeDtypeStruct((56, 1664), bf16),
        [pltpu.VMEM] * 3,
        1_000_000,
    )(momentum, lax.all_to_all(product, "x", 0, 0), factor)


def solution(mesh):
    names = ("x", "zh", "zl", "c", "y")
    fine = Mesh(mesh.devices.reshape(4, 4, 2, 2, 8), names)
    spec = P(names[:4], "y")
    return jax.shard_map(
        per_device, mesh=fine, in_specs=(spec,), out_specs=spec, check_vma=False
    )
```

time: 166 us -> 157 us (0.946)
  blocking collectives: 84.8 us -> 107 us
  waiting for transfers between devices: 26.5 us -> 6.26 us
  starting transfers between devices: 40.7 us -> 31.8 us
  other arithmetic: 3.24 us -> 0.07 us
  Pallas kernels: 2.42 us -> 5.25 us
  matrix products: 3.81 us -> 1.18 us
    all_to_all x3 -> x4, blocking collectives: 51.8 us -> 72.6 us  [the longest x1 21.8 us: per_device(): lax.all_to_all(parts.reshape(8, 112, 256), 'y', 0, 0)]
    all_to_all x3 -> x2, waiting for transfers between devices: 21.1 us -> 0.96 us  [the longest x1 0.95 us: per_device(): rows_a = lax.all_to_all(copies, 'zh', 0, 0).reshape(224, 1664)]
    ppermute x3 -> x2, starting transfers between devices: 14.1 us -> 7.22 us  [other_core(): return lax.ppermute(block, 'c', swap(2, 1))]
    pallas_call x0 -> x4, Pallas kernels: none -> 3.62 us  [the longest x1 1.58 us: per_device(): local(product_kernel, jax.ShapeDtypeStruct((4, 56, 1664), bf16), [pltpu.S...]
    all_to_all x3 -> x2, starting transfers between devices: 18.5 us -> 15 us  [the longest x1 10.8 us: per_device(): rows_a = lax.all_to_all(copies, 'zh', 0, 0).reshape(224, 1664)]
    broadcast_in_dim x3 -> x0, local copies, waits for them, and re-layouts: 3.24 us -> none  [the longest x2 2.6 us: to_all(): jnp.broadcast_to(block[None], (size, *block.shape))]
    unnamed x6 -> x24, local copies, waits for them, and re-layouts: 0.11 us -> 3.18 us
    dot_general x2 -> x0, matrix products: 2.6 us -> none  [depth_dot(): lax.dot_general(left, right, (((0,), (0,)), ((), ())), preferred_element_...]
  transfers between devices with their start and end apart: 8 -> 5, of which waited for: 6 -> 3; matrix products, arithmetic and copies ran while one was open for 2% -> 1% of each run, Pallas kernels for 0% -> 0%
where the time goes in v3:
time: 157 us; the launch traced here: 156 us
  blocking collectives  107 us (68%)
  starting transfers between devices  31.8 us (20%)
  waiting for transfers between devices  6.26 us (4%)
  Pallas kernels  5.25 us (3%)
  local copies, waits for them, and re-layouts  4.08 us (3%)
    all_gather x1, blocking collectives, per_device(): left = lax.all_gather(piece, ('zh', 'zl', 'c'), axis=0)  21.9 us
    all_to_all x1, blocking collectives, per_device(): lax.all_to_all(parts.reshape(8, 112, 256), 'y', 0, 0)  21.8 us
    all_to_all x1, blocking collectives, per_device(): lax.all_to_all(product, 'x', 0, 0)  19.3 us
    all_to_all x1, blocking collectives, per_device(): right = lax.all_to_all(copies, 'y', 0, 0)  16.2 us
    all_to_all x1, blocking collectives, per_device(): poly = lax.all_to_all(poly, 'y', 0, 0).reshape(4, 2, 2, 56, 224)  15.3 us
    all_gather x1, blocking collectives, per_device(): gathered_x = lax.all_gather(raw, 'x', axis=0)  12.8 us
    all_to_all x1, starting transfers between devices, per_device(): rows_a = lax.all_to_all(copies, 'zh', 0, 0).reshape(224, 1664)  10.8 us
    ppermute x1, starting transfers between devices, from_next_z(): return lax.ppermute(block, ('zh', 'zl', 'c'), up + down)  9.52 us
  transfers between devices with their start and end apart: 5, of which 3 were waited for; matrix products, arithmetic and copies ran while one was open for 1% of the time, Pallas kernels for 0%

profile of v3, /device:TPU:1, one launch (start us, length us, event | category | flops | bytes accessed | tf_op | source)
XLA Modules:
  0.0 156.1 jit_solution(16716398826993339546)
XLA Ops:
  0.0 0.0 copy-start.7
  0.0 1.0 copy-done.7
  1.0 1.0 shard_map.17
  2.0 10.8 %all-to-all-start = ((bf16[4,56,1664]{2,1,0:T(8,128)(2,1)}), bf16[4,56,1664]{2,1,0:T(8,128)(2,1)S(1)}, u32[]{:S(2)}, u32[]{:S(2)}) async-start(bf16[4,56,1664]{2,1,0:T(8,128)(2,1)} %get-tuple-element.16), calls=%async_computation | async-start | bytes 1490944 | tf_op jit(solution)/shard_map/all_to_all | solution.py:165
  12.8 12.8 %all-gather = bf16[256,1664]{1,0:T(8,128)(2,1)S(1)} all-gather(bf16[64,1664]{1,0:T(8,128)(2,1)S(1)} %get-tuple-element.15), channel_id=2, replica_groups=mesh['x'=4,'zh'=4,'zl'=2,'c'=2,'y'=8] {'x'}, dimensions={0}, use_global_device_ids=true | all-gather | bytes 1064960 | tf_op jit(solution)/shard_map/all_gather | solution.py:166
  25.6 0.0 copy-start.11
  25.6 0.9 copy-done.11
  26.5 0.1 slice.9
  26.6 1.0 all-to-all-done
  27.5 9.5 %collective-permute-start = (bf16[224,1664]{1,0:T(8,128)(2,1)S(1)}, bf16[224,1664]{1,0:T(8,128)(2,1)S(1)}, u32[]{:S(2)}, u32[]{:S(2)}) collective-permute-start(bf16[224,1664]{1,0:T(8,128)(2,1)S(1)} %bitcast.20), channel_id=1, source_target_pairs={{0,16},{16,32},{32,48},{48,64},{64,80},{80,96},{96,112},{112,0},{8... | collective-permute-start | bytes 2236424 | tf_op jit(solution)/shard_map/ppermute | solution.py:28
  37.0 3.4 %collective-permute-start.1 = (bf16[224,1664]{1,0:T(8,128)(2,1)S(1)}, bf16[224,1664]{1,0:T(8,128)(2,1)S(1)}, u32[]{:S(2)}, u32[]{:S(2)}) collective-permute-start(bf16[224,1664]{1,0:T(8,128)(2,1)S(1)} %bitcast.21), channel_id=1, source_target_pairs={{0,8},{8,0},{1,9},{9,1},{2,10},{10,2},{3,11},{11,3},{4,12},{12,4},... | collective-permute-start | bytes 2236424 | tf_op jit(solution)/shard_map/ppermute | solution.py:32
  40.4 0.8 slice.8.totals_ref
  41.3 0.1 pad_add_fusion.place_ref
  41.3 0.0 copy-start.9
  41.3 4.7 %collective-permute-done.rows_b_ref = bf16[224,1664]{1,0:T(8,128)(2,1)S(1)} collective-permute-done((bf16[224,1664]{1,0:T(8,128)(2,1)S(1)}, bf16[224,1664]{1,0:T(8,128)(2,1)S(1)}, u32[]{:S(2)}, u32[]{:S(2)}) %collective-permute-start) | collective-permute-done | bytes 745504 | tf_op jit(solution)/shard_map/ppermute | solution.py:28
  46.0 0.0 copy-start.1
  46.0 3.9 %collective-permute-start.2 = (bf16[224,1664]{1,0:T(8,128)(2,1)S(1)}, bf16[224,1664]{1,0:T(8,128)(2,1)S(1)}, u32[]{:S(2)}, u32[]{:S(2)}) collective-permute-start(bf16[224,1664]{1,0:T(8,128)(2,1)S(1)} %collective-permute-done.rows_b_ref), channel_id=1, source_target_pairs={{0,8},{8,0},{1,9},{9,1},{2,10},{10,2},{3,11},{11,3},{4,12},{12,4},... | collective-permute-start | bytes 2236424 | tf_op jit(solution)/shard_map/ppermute | solution.py:32
  49.9 0.4 fusion.part_a_ref
  50.3 0.4 fusion.1.part_b_ref
  50.7 0.0 collective-permute-done.1.rows_c_ref
  50.7 0.0 copy-start.3
  50.7 0.4 fusion.2.part_c_ref
  51.1 0.0 copy-done.1
  51.1 0.6 collective-permute-done.2.rows_ref.rows_d_ref
  51.7 0.0 copy-done.9
  51.7 0.0 copy-start.5
  51.7 0.9 shard_map.18
  52.7 0.0 copy-done.3
  52.7 21.8 %all_to_all.30.shares_ref = bf16[8,112,256]{2,1,0:T(8,128)(2,1)S(1)} all-to-all(bf16[8,112,256]{2,1,0:T(8,128)(2,1)S(1)} %bitcast.26), channel_id=1, replica_groups=mesh['x'=4,'zh'=4,'zl'=2,'c'=2,'y'=8] {'y'}, dimensions={0} | all-to-all | bytes 917504 | tf_op jit(solution)/shard_map/all_to_all | solution.py:190
  74.5 0.2 shard_map.19
  74.8 0.0 copy-done.5
  74.8 16.2 %all_to_all.31.block_ref = bf16[8,112,256]{2,1,0:T(8,128)(2,1)S(1)} all-to-all(bf16[8,112,256]{2,1,0:T(8,128)(2,1)S(1)} %get-tuple-element.19), channel_id=1, replica_groups=mesh['x'=4,'zh'=4,'zl'=2,'c'=2,'y'=8] {'y'}, dimensions={0} | all-to-all | bytes 917504 | tf_op jit(solution)/shard_map/all_to_all | solution.py:192
  91.0 0.1 shard_map.20
  91.1 0.0 copy-start
  91.1 1.3 copy-done
  92.3 4.2 %all-to-all-start.3 = ((bf16[4,8,112,256]{3,2,1,0:T(8,128)(2,1)}), bf16[4,8,112,256]{3,2,1,0:T(8,128)(2,1)S(1)}, u32[]{:S(2)}, u32[]{:S(2)}) async-start(bf16[4,8,112,256]{3,2,1,0:T(8,128)(2,1)} %copy-done), calls=%async_computation.3 | async-start | bytes 3670016 | tf_op jit(solution)/shard_map/all_to_all | solution.py:197
  96.5 21.9 %all-gather.1 = bf16[1792,256]{1,0:T(8,128)(2,1)S(1)} all-gather(bf16[112,256]{1,0:T(8,128)(2,1)S(1)} %get-tuple-element.21.gram_ref), channel_id=3, replica_groups=mesh['x'=4,'zh'=4,'zl'=2,'c'=2,'y'=8] {'zh','zl','c'}, dimensions={0}, use_global_device_ids=true | all-gather | bytes 974848 | tf_op jit(solution)/shard_map/all_gather | solution.py:198
  118.5 0.0 all-to-all-done.3
  118.5 0.0 copy-start.2
  118.5 0.0 copy-start.4
  118.5 0.0 copy-start.6
  118.5 0.0 copy-start.10
  118.5 0.5 shard_map.21
  119.0 15.3 %all_to_all.32 = bf16[8,112,224]{2,1,0:T(8,128)(2,1)S(1)} all-to-all(bf16[8,112,224]{2,1,0:T(8,128)(2,1)S(1)} %get-tuple-element.23), channel_id=1, replica_groups=mesh['x'=4,'zh'=4,'zl'=2,'c'=2,'y'=8] {'y'}, dimensions={0} | all-to-all | bytes 802816 | tf_op jit(solution)/shard_map/all_to_all | solution.py:206
  134.2 0.0 copy-done.2
  134.2 0.0 copy-done.4
  134.2 0.0 copy-done.6
  134.2 0.0 copy-done.10
  134.2 0.0 copy-start.8
  134.2 1.6 %shard_map.22 = bf16[4,56,1664]{2,1,0:T(8,128)(2,1)S(1)} custom-call(s32[2]{0:T(128)S(1)} %copy-done.10, bf16[4,2,2,56,224]{4,3,2,1,0:T(8,128)(2,1)S(1)} %bitcast.25, bf16[224,1664]{1,0:T(8,128)(2,1)S(1)} %bitcast.23, bf16[224,1664]{1,0:T(8,128)(2,1)S(1)} %copy-done.2, bf16[224,1664]{1,0:T(8,128)(2,1)S(1)} %copy-done.4, bf16[224,1664]{1,0:T(8,128)(2,1)S(1)} %copy-done.6), custom_call_target="tpu_custom_call" | custom-call | flops 667942912 | bytes 3000000 | tf_op jit(solution)/shard_map/pallas_call | solution.py:207
  135.8 19.3 %all_to_all.33.product_ref = bf16[4,56,1664]{2,1,0:T(8,128)(2,1)S(1)} all-to-all(bf16[4,56,1664]{2,1,0:T(8,128)(2,1)S(1)} %shard_map.22), channel_id=1, replica_groups=mesh['x'=4,'zh'=4,'zl'=2,'c'=2,'y'=8] {'x'}, dimensions={0} | all-to-all | bytes 1490944 | tf_op jit(solution)/shard_map/all_to_all | solution.py:218
  155.2 0.0 copy-done.8
  155.2 0.9 shard_map.23
Async XLA Ops:
  0.0 1.0 copy-start.7
  2.0 25.5 %all-to-all-start = ((bf16[4,56,1664]{2,1,0:T(8,128)(2,1)}), bf16[4,56,1664]{2,1,0:T(8,128)(2,1)S(1)}, u32[]{:S(2)}, u32[]{:S(2)}) async-start(bf16[4,56,1664]{2,1,0:T(8,128)(2,1)} %get-tuple-element.16), calls=%async_computation | async-start | bytes 1490944 | tf_op jit(solution)/shard_map/all_to_all | solution.py:165
  25.6 0.9 copy-start.11
  27.5 18.5 %collective-permute-start = (bf16[224,1664]{1,0:T(8,128)(2,1)S(1)}, bf16[224,1664]{1,0:T(8,128)(2,1)S(1)}, u32[]{:S(2)}, u32[]{:S(2)}) collective-permute-start(bf16[224,1664]{1,0:T(8,128)(2,1)S(1)} %bitcast.20), channel_id=1, source_target_pairs={{0,16},{16,32},{32,48},{48,64},{64,80},{80,96},{96,112},{112,0},{8... | collective-permute-start | bytes 2236424 | tf_op jit(solution)/shard_map/ppermute | solution.py:28
  37.0 13.7 %collective-permute-start.1 = (bf16[224,1664]{1,0:T(8,128)(2,1)S(1)}, bf16[224,1664]{1,0:T(8,128)(2,1)S(1)}, u32[]{:S(2)}, u32[]{:S(2)}) collective-permute-start(bf16[224,1664]{1,0:T(8,128)(2,1)S(1)} %bitcast.21), channel_id=1, source_target_pairs={{0,8},{8,0},{1,9},{9,1},{2,10},{10,2},{3,11},{11,3},{4,12},{12,4},... | collective-permute-start | bytes 2236424 | tf_op jit(solution)/shard_map/ppermute | solution.py:32
  41.3 10.4 %copy-start.9 = (s32[2]{0:T(128)}, s32[2]{0:T(128)S(1)}, u32[]{:S(2)}) copy-start(s32[2]{0:T(128)S(1)} %pad_add_fusion.place_ref) | copy-start | bytes 28
  46.0 5.1 %copy-start.1 = (bf16[224,1664]{1,0:T(8,128)(2,1)}, bf16[224,1664]{1,0:T(8,128)(2,1)S(1)}, u32[]{:S(2)}) copy-start(bf16[224,1664]{1,0:T(8,128)(2,1)S(1)} %collective-permute-done.rows_b_ref) | copy-start | bytes 2236420
  46.0 5.7 %collective-permute-start.2 = (bf16[224,1664]{1,0:T(8,128)(2,1)S(1)}, bf16[224,1664]{1,0:T(8,128)(2,1)S(1)}, u32[]{:S(2)}, u32[]{:S(2)}) collective-permute-start(bf16[224,1664]{1,0:T(8,128)(2,1)S(1)} %collective-permute-done.rows_b_ref), channel_id=1, source_target_pairs={{0,8},{8,0},{1,9},{9,1},{2,10},{10,2},{3,11},{11,3},{4,12},{12,4},... | collective-permute-start | bytes 2236424 | tf_op jit(solution)/shard_map/ppermute | solution.py:32
  50.7 2.0 %copy-start.3 = (bf16[224,1664]{1,0:T(8,128)(2,1)}, bf16[224,1664]{1,0:T(8,128)(2,1)S(1)}, u32[]{:S(2)}) copy-start(bf16[224,1664]{1,0:T(8,128)(2,1)S(1)} %collective-permute-done.1.rows_c_ref) | copy-start | bytes 2236420
  51.7 23.0 %copy-start.5 = (bf16[224,1664]{1,0:T(8,128)(2,1)}, bf16[224,1664]{1,0:T(8,128)(2,1)S(1)}, u32[]{:S(2)}) copy-start(bf16[224,1664]{1,0:T(8,128)(2,1)S(1)} %collective-permute-done.2.rows_ref.rows_d_ref) | copy-start | bytes 2236420
  91.1 1.3 copy-start
  92.3 26.1 %all-to-all-start.3 = ((bf16[4,8,112,256]{3,2,1,0:T(8,128)(2,1)}), bf16[4,8,112,256]{3,2,1,0:T(8,128)(2,1)S(1)}, u32[]{:S(2)}, u32[]{:S(2)}) async-start(bf16[4,8,112,256]{3,2,1,0:T(8,128)(2,1)} %copy-done), calls=%async_computation.3 | async-start | bytes 3670016 | tf_op jit(solution)/shard_map/all_to_all | solution.py:197
  118.5 15.8 %copy-start.2 = (bf16[224,1664]{1,0:T(8,128)(2,1)S(1)}, bf16[224,1664]{1,0:T(8,128)(2,1)}, u32[]{:S(2)}) copy-start(bf16[224,1664]{1,0:T(8,128)(2,1)} %copy-done.1) | copy-start | bytes 2236420
  118.5 15.8 %copy-start.4 = (bf16[224,1664]{1,0:T(8,128)(2,1)S(1)}, bf16[224,1664]{1,0:T(8,128)(2,1)}, u32[]{:S(2)}) copy-start(bf16[224,1664]{1,0:T(8,128)(2,1)} %copy-done.3) | copy-start | bytes 2236420
  118.5 15.8 %copy-start.6 = (bf16[224,1664]{1,0:T(8,128)(2,1)S(1)}, bf16[224,1664]{1,0:T(8,128)(2,1)}, u32[]{:S(2)}) copy-start(bf16[224,1664]{1,0:T(8,128)(2,1)} %copy-done.5) | copy-start | bytes 2236420
  118.5 15.8 %copy-start.10 = (s32[2]{0:T(128)S(1)}, s32[2]{0:T(128)}, u32[]{:S(2)}) copy-start(s32[2]{0:T(128)} %copy-done.9) | copy-start | bytes 28
  134.2 20.9 %copy-start.8 = (f32[56,1664]{1,0:T(8,128)S(1)}, f32[56,1664]{1,0:T(8,128)}, u32[]{:S(2)}) copy-start(f32[56,1664]{1,0:T(8,128)} %momentum_ref.3) | copy-start | bytes 1118212

commit v4 on v3

--- a/solution.py
+++ b/solution.py
@@ -58,12 +58,12 @@
 
 def start_kernel(momentum_ref, raw_ref, copies_ref):
     momentum = momentum_ref[...]
-    raw = momentum.astype(bf16)
-    for zh in range(4):
-        copies_ref[zh] = raw
+    raw_ref[...] = momentum.astype(bf16)
     total = jnp.sum(momentum * momentum, keepdims=True)
     more = in_lanes(0, jnp.broadcast_to(total, (8, 1664)), jnp.zeros((8, 1664), f32))
-    raw_ref[...] = jnp.concatenate([momentum, more], axis=0).astype(bf16)
+    longer = jnp.concatenate([momentum, more], axis=0).astype(bf16)
+    for x in range(4):
+        copies_ref[x] = longer
 
 
 def copies_kernel(block_ref, copies_ref):
@@ -155,17 +155,17 @@
 
 def per_device(momentum):
     place = jnp.stack([lax.axis_index("zl"), lax.axis_index("c")]).astype(jnp.int32)
-    raw, copies = local(
+    short, copies = local(
         start_kernel,
-        [jax.ShapeDtypeStruct((64, 1664), bf16), jax.ShapeDtypeStruct((4, 56, 1664), bf16)],
+        [jax.ShapeDtypeStruct((56, 1664), bf16), jax.ShapeDtypeStruct((4, 64, 1664), bf16)],
         [pltpu.VMEM],
         1_000_000,
     )(momentum)
 
-    rows_a = lax.all_to_all(copies, "zh", 0, 0).reshape(224, 1664)
-    gathered_x = lax.all_gather(raw, "x", axis=0)
+    rows_a = lax.all_gather(short, "zh", axis=0, tiled=True)
+    rows_a, copies = lax.optimization_barrier((rows_a, copies))
+    gathered_x = lax.all_to_all(copies, "x", 0, 0)
     rows_x = gathered_x[:, :56].reshape(224, 1664)
-    rows_a, rows_x = lax.optimization_barrier((rows_a, rows_x))
     rows_b = from_next_z(rows_a)
     rows_c = other_core(rows_a)
     rows_d = other_core(rows_b)

time: 157 us -> 154 us (0.981)
  the two profiles are of different devices: /device:TPU:1 before, /device:TPU:64 now
where the time goes in v4:
time: 154 us
  blocking collectives  117 us (76%)
  starting transfers between devices  16.1 us (10%)
  waiting for transfers between devices  11.1 us (7%)
  Pallas kernels  5.48 us (4%)
  local copies, waits for them, and re-layouts  2.33 us (2%)
    all_gather x1, blocking collectives, per_device(): rows_a = lax.all_gather(short, 'zh', axis=0, tiled=True)  23.9 us
    all_to_all x1, blocking collectives, per_device(): lax.all_to_all(parts.reshape(8, 112, 256), 'y', 0, 0)  23.3 us
    all_gather x1, blocking collectives, per_device(): left = lax.all_gather(piece, ('zh', 'zl', 'c'), axis=0)  18.9 us
    all_to_all x1, blocking collectives, per_device(): poly = lax.all_to_all(poly, 'y', 0, 0).reshape(4, 2, 2, 56, 224)  17.8 us
    all_to_all x1, blocking collectives, per_device(): right = lax.all_to_all(copies, 'y', 0, 0)  17.6 us
    all_to_all x1, blocking collectives, per_device(): lax.all_to_all(product, 'x', 0, 0)  15.9 us
    all_to_all x1, waiting for transfers between devices, per_device(): gathered_x = lax.all_to_all(copies, 'x', 0, 0)  7.84 us
    ppermute x1, starting transfers between devices, from_next_z(): return lax.ppermute(block, ('zh', 'zl', 'c'), up + down)  4.35 us
  transfers between devices with their start and end apart: 5, of which 3 were waited for; matrix products, arithmetic and copies ran while one was open for 1% of the time, Pallas kernels for 0%

profile of v4, /device:TPU:64, one launch (start us, length us, event | category | flops | bytes accessed | tf_op | source)
XLA Modules:
  0.0 153.9 jit_solution(4998723250383580765)
XLA Ops:
  0.0 0.0 copy-start.7
  0.0 1.0 copy-done.7
  1.0 1.2 shard_map.17
  2.2 23.9 %all_gather.9.rows_a_ref = bf16[224,1664]{1,0:T(8,128)(2,1)S(1)} all-gather(bf16[56,1664]{1,0:T(8,128)(2,1)S(1)} %get-tuple-element.15), channel_id=1, replica_groups=mesh['x'=4,'zh'=4,'zl'=2,'c'=2,'y'=8] {'zh'}, dimensions={0}, use_global_device_ids=true | all-gather | bytes 931840 | tf_op jit(solution)/shard_map/all_gather | solution.py:165
  26.1 4.4 %collective-permute-start = (bf16[224,1664]{1,0:T(8,128)(2,1)S(1)}, bf16[224,1664]{1,0:T(8,128)(2,1)S(1)}, u32[]{:S(2)}, u32[]{:S(2)}) collective-permute-start(bf16[224,1664]{1,0:T(8,128)(2,1)S(1)} %all_gather.9.rows_a_ref), channel_id=1, source_target_pairs={{0,16},{16,32},{32,48},{48,64},{64,80},{80,96},{96,112},{112,0},{8... | collective-permute-start | bytes 2236424 | tf_op jit(solution)/shard_map/ppermute | solution.py:28
  30.5 4.3 %all-to-all-start = ((bf16[4,64,1664]{2,1,0:T(8,128)(2,1)}), bf16[4,64,1664]{2,1,0:T(8,128)(2,1)S(1)}, u32[]{:S(2)}, u32[]{:S(2)}) async-start(bf16[4,64,1664]{2,1,0:T(8,128)(2,1)} %get-tuple-element.17), calls=%async_computation | async-start | bytes 1703936 | tf_op jit(solution)/shard_map/all_to_all | solution.py:167
  34.8 1.9 %collective-permute-start.1 = (bf16[224,1664]{1,0:T(8,128)(2,1)S(1)}, bf16[224,1664]{1,0:T(8,128)(2,1)S(1)}, u32[]{:S(2)}, u32[]{:S(2)}) collective-permute-start(bf16[224,1664]{1,0:T(8,128)(2,1)S(1)} %all_gather.9.rows_a_ref), channel_id=1, source_target_pairs={{0,8},{8,0},{1,9},{9,1},{2,10},{10,2},{3,11},{11,3},{4,12},{12,4},... | collective-permute-start | bytes 2236424 | tf_op jit(solution)/shard_map/ppermute | solution.py:32
  36.7 0.1 pad_add_fusion.place_ref
  36.8 0.0 copy-start.9
  36.8 7.8 %all-to-all-done = bf16[4,64,1664]{2,1,0:T(8,128)(2,1)S(1)} async-done(((bf16[4,64,1664]{2,1,0:T(8,128)(2,1)}), bf16[4,64,1664]{2,1,0:T(8,128)(2,1)S(1)}, u32[]{:S(2)}, u32[]{:S(2)}) %all-to-all-start) | async-done | bytes 852000 | tf_op jit(solution)/shard_map/all_to_all | solution.py:167
  44.6 0.1 slice.9
  44.7 0.0 collective-permute-done.rows_b_ref
  44.7 0.0 copy-start.1
  44.7 1.9 %collective-permute-start.2 = (bf16[224,1664]{1,0:T(8,128)(2,1)S(1)}, bf16[224,1664]{1,0:T(8,128)(2,1)S(1)}, u32[]{:S(2)}, u32[]{:S(2)}) collective-permute-start(bf16[224,1664]{1,0:T(8,128)(2,1)S(1)} %collective-permute-done.rows_b_ref), channel_id=1, source_target_pairs={{0,8},{8,0},{1,9},{9,1},{2,10},{10,2},{3,11},{11,3},{4,12},{12,4},... | collective-permute-start | bytes 2236424 | tf_op jit(solution)/shard_map/ppermute | solution.py:32
  46.7 0.4 fusion.part_a_ref
  47.1 0.4 fusion.1.part_b_ref
  47.5 0.0 collective-permute-done.1.rows_c_ref
  47.5 0.0 copy-start.3
  47.5 0.4 fusion.2.part_c_ref
  47.9 0.0 copy-done.1
  47.9 1.0 collective-permute-done.2.rows_ref.rows_d_ref
  48.8 0.0 copy-done.9
  48.8 0.0 copy-start.5
  48.8 0.9 shard_map.18
  49.8 0.0 copy-done.3
  49.8 23.3 %all_to_all.30.shares_ref = bf16[8,112,256]{2,1,0:T(8,128)(2,1)S(1)} all-to-all(bf16[8,112,256]{2,1,0:T(8,128)(2,1)S(1)} %bitcast.20), channel_id=1, replica_groups=mesh['x'=4,'zh'=4,'zl'=2,'c'=2,'y'=8] {'y'}, dimensions={0} | all-to-all | bytes 917504 | tf_op jit(solution)/shard_map/all_to_all | solution.py:190
  73.1 0.2 shard_map.19
  73.3 0.0 copy-done.5
  73.3 17.6 %all_to_all.31.block_ref = bf16[8,112,256]{2,1,0:T(8,128)(2,1)S(1)} all-to-all(bf16[8,112,256]{2,1,0:T(8,128)(2,1)S(1)} %get-tuple-element.19), channel_id=1, replica_groups=mesh['x'=4,'zh'=4,'zl'=2,'c'=2,'y'=8] {'y'}, dimensions={0} | all-to-all | bytes 917504 | tf_op jit(solution)/shard_map/all_to_all | solution.py:192
  91.0 0.1 shard_map.20
  91.1 0.0 copy-start
  91.1 1.2 copy-done
  92.3 3.6 %all-to-all-start.3 = ((bf16[4,8,112,256]{3,2,1,0:T(8,128)(2,1)}), bf16[4,8,112,256]{3,2,1,0:T(8,128)(2,1)S(1)}, u32[]{:S(2)}, u32[]{:S(2)}) async-start(bf16[4,8,112,256]{3,2,1,0:T(8,128)(2,1)} %copy-done), calls=%async_computation.3 | async-start | bytes 3670016 | tf_op jit(solution)/shard_map/all_to_all | solution.py:197
  95.9 18.9 %all-gather = bf16[1792,256]{1,0:T(8,128)(2,1)S(1)} all-gather(bf16[112,256]{1,0:T(8,128)(2,1)S(1)} %get-tuple-element.21.gram_ref), channel_id=2, replica_groups=mesh['x'=4,'zh'=4,'zl'=2,'c'=2,'y'=8] {'zh','zl','c'}, dimensions={0}, use_global_device_ids=true | all-gather | bytes 974848 | tf_op jit(solution)/shard_map/all_gather | solution.py:198
  114.8 2.3 %all-to-all-done.3 = bf16[4,8,112,256]{3,2,1,0:T(8,128)(2,1)S(1)} async-done(((bf16[4,8,112,256]{3,2,1,0:T(8,128)(2,1)}), bf16[4,8,112,256]{3,2,1,0:T(8,128)(2,1)S(1)}, u32[]{:S(2)}, u32[]{:S(2)}) %all-to-all-start.3) | async-done | bytes 1835040 | tf_op jit(solution)/shard_map/all_to_all | solution.py:197
  117.1 0.0 copy-start.2
  117.1 0.0 copy-start.4
  117.1 0.0 copy-start.6
  117.1 0.0 copy-start.10
  117.2 0.5 shard_map.21
  117.7 17.8 %all_to_all.32 = bf16[8,112,224]{2,1,0:T(8,128)(2,1)S(1)} all-to-all(bf16[8,112,224]{2,1,0:T(8,128)(2,1)S(1)} %get-tuple-element.23), channel_id=1, replica_groups=mesh['x'=4,'zh'=4,'zl'=2,'c'=2,'y'=8] {'y'}, dimensions={0} | all-to-all | bytes 802816 | tf_op jit(solution)/shard_map/all_to_all | solution.py:206
  135.5 0.0 copy-done.2
  135.5 0.0 copy-done.4
  135.5 0.0 copy-done.6
  135.5 0.0 copy-done.10
  135.5 0.0 copy-start.8
  135.5 1.6 %shard_map.22 = bf16[4,56,1664]{2,1,0:T(8,128)(2,1)S(1)} custom-call(s32[2]{0:T(128)S(1)} %copy-done.10, bf16[4,2,2,56,224]{4,3,2,1,0:T(8,128)(2,1)S(1)} %bitcast.19, bf16[224,1664]{1,0:T(8,128)(2,1)S(1)} %all_gather.9.rows_a_ref, bf16[224,1664]{1,0:T(8,128)(2,1)S(1)} %copy-done.2, bf16[224,1664]{1,0:T(8,128)(2,1)S(1)} %copy-done.4, ...), custom_call_target="tpu_custom_call" | custom-call | flops 667942912 | bytes 3000000 | tf_op jit(solution)/shard_map/pallas_call | solution.py:207
  137.1 15.9 %all_to_all.33.product_ref = bf16[4,56,1664]{2,1,0:T(8,128)(2,1)S(1)} all-to-all(bf16[4,56,1664]{2,1,0:T(8,128)(2,1)S(1)} %shard_map.22), channel_id=1, replica_groups=mesh['x'=4,'zh'=4,'zl'=2,'c'=2,'y'=8] {'x'}, dimensions={0} | all-to-all | bytes 1490944 | tf_op jit(solution)/shard_map/all_to_all | solution.py:218
  153.0 0.0 copy-done.8
  153.0 0.9 shard_map.23
  (1 shorter events, 0.0 us)
Async XLA Ops:
  0.0 1.0 copy-start.7
  26.1 18.6 %collective-permute-start = (bf16[224,1664]{1,0:T(8,128)(2,1)S(1)}, bf16[224,1664]{1,0:T(8,128)(2,1)S(1)}, u32[]{:S(2)}, u32[]{:S(2)}) collective-permute-start(bf16[224,1664]{1,0:T(8,128)(2,1)S(1)} %all_gather.9.rows_a_ref), channel_id=1, source_target_pairs={{0,16},{16,32},{32,48},{48,64},{64,80},{80,96},{96,112},{112,0},{8... | collective-permute-start | bytes 2236424 | tf_op jit(solution)/shard_map/ppermute | solution.py:28
  30.5 14.1 %all-to-all-start = ((bf16[4,64,1664]{2,1,0:T(8,128)(2,1)}), bf16[4,64,1664]{2,1,0:T(8,128)(2,1)S(1)}, u32[]{:S(2)}, u32[]{:S(2)}) async-start(bf16[4,64,1664]{2,1,0:T(8,128)(2,1)} %get-tuple-element.17), calls=%async_computation | async-start | bytes 1703936 | tf_op jit(solution)/shard_map/all_to_all | solution.py:167
  34.8 12.7 %collective-permute-start.1 = (bf16[224,1664]{1,0:T(8,128)(2,1)S(1)}, bf16[224,1664]{1,0:T(8,128)(2,1)S(1)}, u32[]{:S(2)}, u32[]{:S(2)}) collective-permute-start(bf16[224,1664]{1,0:T(8,128)(2,1)S(1)} %all_gather.9.rows_a_ref), channel_id=1, source_target_pairs={{0,8},{8,0},{1,9},{9,1},{2,10},{10,2},{3,11},{11,3},{4,12},{12,4},... | collective-permute-start | bytes 2236424 | tf_op jit(solution)/shard_map/ppermute | solution.py:32
  36.8 12.1 %copy-start.9 = (s32[2]{0:T(128)}, s32[2]{0:T(128)S(1)}, u32[]{:S(2)}) copy-start(s32[2]{0:T(128)S(1)} %pad_add_fusion.place_ref) | copy-start | bytes 28
  44.7 3.2 %copy-start.1 = (bf16[224,1664]{1,0:T(8,128)(2,1)}, bf16[224,1664]{1,0:T(8,128)(2,1)S(1)}, u32[]{:S(2)}) copy-start(bf16[224,1664]{1,0:T(8,128)(2,1)S(1)} %collective-permute-done.rows_b_ref) | copy-start | bytes 2236420
  44.7 4.1 %collective-permute-start.2 = (bf16[224,1664]{1,0:T(8,128)(2,1)S(1)}, bf16[224,1664]{1,0:T(8,128)(2,1)S(1)}, u32[]{:S(2)}, u32[]{:S(2)}) collective-permute-start(bf16[224,1664]{1,0:T(8,128)(2,1)S(1)} %collective-permute-done.rows_b_ref), channel_id=1, source_target_pairs={{0,8},{8,0},{1,9},{9,1},{2,10},{10,2},{3,11},{11,3},{4,12},{12,4},... | collective-permute-start | bytes 2236424 | tf_op jit(solution)/shard_map/ppermute | solution.py:32
  47.5 2.3 %copy-start.3 = (bf16[224,1664]{1,0:T(8,128)(2,1)}, bf16[224,1664]{1,0:T(8,128)(2,1)S(1)}, u32[]{:S(2)}) copy-start(bf16[224,1664]{1,0:T(8,128)(2,1)S(1)} %collective-permute-done.1.rows_c_ref) | copy-start | bytes 2236420
  48.8 24.5 %copy-start.5 = (bf16[224,1664]{1,0:T(8,128)(2,1)}, bf16[224,1664]{1,0:T(8,128)(2,1)S(1)}, u32[]{:S(2)}) copy-start(bf16[224,1664]{1,0:T(8,128)(2,1)S(1)} %collective-permute-done.2.rows_ref.rows_d_ref) | copy-start | bytes 2236420
  91.1 1.2 copy-start
  92.3 24.8 %all-to-all-start.3 = ((bf16[4,8,112,256]{3,2,1,0:T(8,128)(2,1)}), bf16[4,8,112,256]{3,2,1,0:T(8,128)(2,1)S(1)}, u32[]{:S(2)}, u32[]{:S(2)}) async-start(bf16[4,8,112,256]{3,2,1,0:T(8,128)(2,1)} %copy-done), calls=%async_computation.3 | async-start | bytes 3670016 | tf_op jit(solution)/shard_map/all_to_all | solution.py:197
  117.1 18.4 %copy-start.2 = (bf16[224,1664]{1,0:T(8,128)(2,1)S(1)}, bf16[224,1664]{1,0:T(8,128)(2,1)}, u32[]{:S(2)}) copy-start(bf16[224,1664]{1,0:T(8,128)(2,1)} %copy-done.1) | copy-start | bytes 2236420
  117.1 18.4 %copy-start.4 = (bf16[224,1664]{1,0:T(8,128)(2,1)S(1)}, bf16[224,1664]{1,0:T(8,128)(2,1)}, u32[]{:S(2)}) copy-start(bf16[224,1664]{1,0:T(8,128)(2,1)} %copy-done.3) | copy-start | bytes 2236420
  117.1 18.4 %copy-start.6 = (bf16[224,1664]{1,0:T(8,128)(2,1)S(1)}, bf16[224,1664]{1,0:T(8,128)(2,1)}, u32[]{:S(2)}) copy-start(bf16[224,1664]{1,0:T(8,128)(2,1)} %copy-done.5) | copy-start | bytes 2236420
  117.1 18.4 %copy-start.10 = (s32[2]{0:T(128)S(1)}, s32[2]{0:T(128)}, u32[]{:S(2)}) copy-start(s32[2]{0:T(128)} %copy-done.9) | copy-start | bytes 28
  135.5 17.5 %copy-start.8 = (f32[56,1664]{1,0:T(8,128)S(1)}, f32[56,1664]{1,0:T(8,128)}, u32[]{:S(2)}) copy-start(f32[56,1664]{1,0:T(8,128)} %momentum_ref.3) | copy-start | bytes 1118212

commit v5 on v4

--- a/solution.py
+++ b/solution.py
@@ -71,8 +71,31 @@
         copies_ref[x] = block_ref[...]
 
 
+def pack(block, total):
+    high = block[:, 128:]
+    rest = high[88:]
+    if total is None:
+        spare = jnp.zeros((16, 32), f32)
+    else:
+        spare = in_lanes(0, jnp.broadcast_to(total, (16, 32)), jnp.zeros((16, 32), f32))
+    beside = jnp.concatenate([rest[:, :32], rest[:, 32:64], rest[:, 64:], spare], axis=0)
+    below = jnp.concatenate([high[:88], beside], axis=1)
+    return jnp.concatenate([block[:, :128], below], axis=0)
+
+
+def unpack(packed):
+    beside = packed[112:, 96:]
+    rest = jnp.concatenate([beside[:24], beside[24:48], beside[48:72]], axis=1)
+    high = jnp.concatenate([packed[112:, :96], rest], axis=0)
+    return jnp.concatenate([packed[:112], high], axis=1)
+
+
+def packed_total(packed):
+    return jnp.sum(packed[184:192, 96:][:1], axis=1, keepdims=True)
+
+
 def parts_kernel(place_ref, totals_ref, part_a_ref, part_b_ref, part_c_ref, rows_ref, rows_x_ref, parts_ref):
-    zl, core = place_ref[0], place_ref[1]
+    zl, first = place_ref[0], place_ref[1] == 0
     part_d = lax.dot_general(
         rows_ref[...], rows_x_ref[...], (((1,), (1,)), ((), ())), preferred_element_type=f32
     )
@@ -80,43 +103,22 @@
     for x in range(4):
         total += totals_ref[x, :, :128].astype(f32)[56:]
     total = jnp.sum(total[:1], axis=1, keepdims=True)
-    lanes = in_lanes(0, jnp.broadcast_to(total, (56, 32)), jnp.zeros((56, 32), f32))
-    for part, l, c in (
-        (part_a_ref, zl, core),
-        (part_b_ref, 1 - zl, core),
-        (part_c_ref, zl, 1 - core),
-        (part_d, 1 - zl, 1 - core),
-    ):
+    for own, other, l in ((part_a_ref, part_c_ref, zl), (part_b_ref, part_d, 1 - zl)):
         for zh in range(4):
-            block = jnp.concatenate([part[56 * zh : 56 * zh + 56, :], lanes], axis=1)
-            parts_ref[zh, l, c] = block.astype(bf16)
-
-
-def product_kernel(place_ref, poly_ref, rows_a_ref, rows_b_ref, rows_c_ref, rows_d_ref, product_ref):
-    zl, core = place_ref[0], place_ref[1]
-    product = None
-    for rows, l, c in (
-        (rows_a_ref, zl, core),
-        (rows_b_ref, 1 - zl, core),
-        (rows_c_ref, zl, 1 - core),
-        (rows_d_ref, 1 - zl, 1 - core),
-    ):
-        poly = jnp.concatenate([poly_ref[zh, l, c].astype(f32) for zh in range(4)], axis=0)
-        term = lax.dot_general(
-            poly.astype(bf16), rows[...], (((0,), (0,)), ((), ())), preferred_element_type=f32
-        )
-        product = term if product is None else product + term
-    for x in range(4):
-        product_ref[x] = product[56 * x : 56 * x + 56].astype(bf16)
+            mine, its = own[56 * zh : 56 * zh + 56, :], other[56 * zh : 56 * zh + 56, :]
+            block = jnp.concatenate(
+                [jnp.where(first, mine, its), jnp.where(first, its, mine)], axis=0
+            )
+            parts_ref[2 * zh + l] = pack(block, total).astype(bf16)
 
 
 def add_shares_kernel(shares_ref, piece_ref, copies_ref):
     summed = shares_ref[0].astype(f32)
     for share in range(1, 8):
         summed += shares_ref[share].astype(f32)
-    total = jnp.sum(summed[:, 224:], axis=1, keepdims=True)
-    lane = lax.broadcasted_iota(jnp.int32, (112, 256), 1)
-    piece = in_lanes(224, total, jnp.where(lane < 224, summed, 0.0)).astype(bf16)
+    row = lax.broadcasted_iota(jnp.int32, (200, 128), 0)
+    with_total = in_lanes(96, packed_total(summed), summed)
+    piece = jnp.where(row >= 184, with_total, summed).astype(bf16)
     piece_ref[...] = piece
     for share in range(8):
         copies_ref[share] = piece
@@ -124,27 +126,47 @@
 
 def polynomial_kernel(left_ref, right_ref, gram_ref, poly_ref, factor_ref):
     square = jnp.zeros((112, 224), f32)
-    lanes = jnp.zeros((112, 32), f32)
-    for g in range(16):
-        left = left_ref[g]
-        right = jnp.concatenate(
-            [right_ref[x, g // 2, g % 2].astype(f32) for x in range(4)], axis=0
-        ).astype(bf16)
-        square += jnp.dot(left[:, :224], right[:, :224], preferred_element_type=f32)
-        lanes += left[:, 224:].astype(f32)
-    total = jnp.sum(lanes, axis=1, keepdims=True)
+    total = jnp.zeros((1, 1), f32)
+    for z in range(8):
+        rights = [unpack(right_ref[x, z].astype(f32)) for x in range(4)]
+        for c in range(2):
+            left = left_ref[2 * z + c].astype(f32)
+            total += packed_total(left)
+            right = jnp.concatenate([block[56 * c : 56 * c + 56] for block in rights], axis=0)
+            square += jnp.dot(
+                unpack(left).astype(bf16), right.astype(bf16), preferred_element_type=f32
+            )
     factor = math.sqrt(M) / 3.0 / (jnp.sqrt(total) + 1e-07)
     factor2 = factor * factor
-    gram = (gram_ref[:, :224].astype(f32) * factor2).astype(bf16).astype(f32)
+    gram = (unpack(gram_ref[...].astype(f32)) * factor2).astype(bf16).astype(f32)
     square = ((square * factor2) * factor2).astype(bf16).astype(f32)
-    poly = (coef_b * gram + coef_c * square).astype(bf16)
-    for g in range(8):
-        poly_ref[g] = poly
-    factor_ref[...] = jnp.broadcast_to(factor, (112, 128))
+    poly = pack(coef_b * gram + coef_c * square, None).astype(bf16)
+    for share in range(8):
+        poly_ref[share] = poly
+    factor_ref[...] = jnp.broadcast_to(factor, (8, 128))
+
+
+def product_kernel(place_ref, poly_ref, rows_a_ref, rows_b_ref, rows_c_ref, rows_d_ref, product_ref):
+    zl, first = place_ref[0], place_ref[1] == 0
+    product = None
+    for own, other, l in ((rows_a_ref, rows_c_ref, zl), (rows_b_ref, rows_d_ref, 1 - zl)):
+        blocks = [unpack(poly_ref[2 * zh + l].astype(f32)) for zh in range(4)]
+        lower = jnp.concatenate([block[:56] for block in blocks], axis=0)
+        upper = jnp.concatenate([block[56:] for block in blocks], axis=0)
+        for rows, poly in (
+            (own, jnp.where(first, lower, upper)),
+            (other, jnp.where(first, upper, lower)),
+        ):
+            term = lax.dot_general(
+                poly.astype(bf16), rows[...], (((0,), (0,)), ((), ())), preferred_element_type=f32
+            )
+            product = term if product is None else product + term
+    for x in range(4):
+        product_ref[x] = product[56 * x : 56 * x + 56].astype(bf16)
 
 
 def update_kernel(momentum_ref, product_ref, factor_ref, update_ref):
-    factor = factor_ref[:56, :1]
+    factor = factor_ref[:1, :1]
     product = product_ref[0].astype(f32)
     for x in range(1, 4):
         product += product_ref[x].astype(f32)
@@ -172,7 +194,7 @@
 
     parts = local(
         parts_kernel,
-        jax.ShapeDtypeStruct((4, 2, 2, 56, 256), bf16),
+        jax.ShapeDtypeStruct((8, 200, 128), bf16),
         [pltpu.SMEM] + [pltpu.VMEM] * 6,
         2 * 224 * 224 * 1664,
     )(
@@ -184,26 +206,26 @@
     )
     piece, copies = local(
         add_shares_kernel,
-        [jax.ShapeDtypeStruct((112, 256), bf16), jax.ShapeDtypeStruct((8, 112, 256), bf16)],
+        [jax.ShapeDtypeStruct((200, 128), bf16), jax.ShapeDtypeStruct((8, 200, 128), bf16)],
         [pltpu.VMEM],
         1_000_000,
-    )(lax.all_to_all(parts.reshape(8, 112, 256), "y", 0, 0))
+    )(lax.all_to_all(parts, "y", 0, 0))
 
     right = lax.all_to_all(copies, "y", 0, 0)
     right, piece = lax.optimization_barrier((right, piece))
     copies = local(
-        copies_kernel, jax.ShapeDtypeStruct((4, 8, 112, 256), bf16), [pltpu.VMEM], 1_000_000
+        copies_kernel, jax.ShapeDtypeStruct((4, 8, 200, 128), bf16), [pltpu.VMEM], 1_000_000
     )(right)
-    right = lax.all_to_all(copies, "x", 0, 0).reshape(4, 8, 2, 56, 256)
+    right = lax.all_to_all(copies, "x", 0, 0)
     left = lax.all_gather(piece, ("zh", "zl", "c"), axis=0)
     poly, factor = local(
         polynomial_kernel,
-        [jax.ShapeDtypeStruct((8, 112, 224), bf16), jax.ShapeDtypeStruct((112, 128), f32)],
+        [jax.ShapeDtypeStruct((8, 200, 128), bf16), jax.ShapeDtypeStruct((8, 128), f32)],
         [pltpu.VMEM] * 3,
         2 * 112 * 224 * M,
     )(left, right, piece)
 
-    poly = lax.all_to_all(poly, "y", 0, 0).reshape(4, 2, 2, 56, 224)
+    poly = lax.all_to_all(poly, "y", 0, 0)
     product = local(
         product_kernel,
         jax.ShapeDtypeStruct((4, 56, 1664), bf16),

time: 154 us -> 152 us (0.987)
  the two profiles are of different devices: /device:TPU:64 before, /device:TPU:1 now
where the time goes in v5:
time: 152 us; the launch traced here: 149 us
  blocking collectives  110 us (72%)
  starting transfers between devices  20.9 us (14%)
  waiting for transfers between devices  8.76 us (6%)
  Pallas kernels  6.18 us (4%)
  local copies, waits for them, and re-layouts  2.26 us (1%)
    all_gather x1, blocking collectives, per_device(): rows_a = lax.all_gather(short, 'zh', axis=0, tiled=True)  22.9 us
    all_to_all x1, blocking collectives, per_device(): lax.all_to_all(parts, 'y', 0, 0)  20.9 us
    all_gather x1, blocking collectives, per_device(): left = lax.all_gather(piece, ('zh', 'zl', 'c'), axis=0)  19.8 us
    all_to_all x1, blocking collectives, per_device(): lax.all_to_all(product, 'x', 0, 0)  15.5 us
    all_to_all x1, blocking collectives, per_device(): poly = lax.all_to_all(poly, 'y', 0, 0)  15.3 us
    all_to_all x1, blocking collectives, per_device(): right = lax.all_to_all(copies, 'y', 0, 0)  15.1 us
    all_to_all x1, waiting for transfers between devices, per_device(): gathered_x = lax.all_to_all(copies, 'x', 0, 0)  8.15 us
    ppermute x2, starting transfers between devices, other_core(): return lax.ppermute(block, 'c', swap(2, 1))  7.61 us
  transfers between devices with their start and end apart: 5, of which 2 were waited for; matrix products, arithmetic and copies ran while one was open for 1% of the time, Pallas kernels for 0%

profile of v5, /device:TPU:1, one launch (start us, length us, event | category | flops | bytes accessed | tf_op | source)
XLA Modules:
  0.0 149.0 jit_solution(4758074261119221808)
XLA Ops:
  0.0 0.0 copy-start.7
  0.0 1.0 copy-done.7
  1.0 1.2 shard_map.17
  2.2 22.9 %all_gather.9.rows_a_ref = bf16[224,1664]{1,0:T(8,128)(2,1)S(1)} all-gather(bf16[56,1664]{1,0:T(8,128)(2,1)S(1)} %get-tuple-element.15), channel_id=1, replica_groups=mesh['x'=4,'zh'=4,'zl'=2,'c'=2,'y'=8] {'zh'}, dimensions={0}, use_global_device_ids=true | all-gather | bytes 931840 | tf_op jit(solution)/shard_map/all_gather | solution.py:187
  25.1 5.7 %collective-permute-start = (bf16[224,1664]{1,0:T(8,128)(2,1)S(1)}, bf16[224,1664]{1,0:T(8,128)(2,1)S(1)}, u32[]{:S(2)}, u32[]{:S(2)}) collective-permute-start(bf16[224,1664]{1,0:T(8,128)(2,1)S(1)} %all_gather.9.rows_a_ref), channel_id=1, source_target_pairs={{0,16},{16,32},{32,48},{48,64},{64,80},{80,96},{96,112},{112,0},{8... | collective-permute-start | bytes 2236424 | tf_op jit(solution)/shard_map/ppermute | solution.py:28
  30.7 4.0 %all-to-all-start = ((bf16[4,64,1664]{2,1,0:T(8,128)(2,1)}), bf16[4,64,1664]{2,1,0:T(8,128)(2,1)S(1)}, u32[]{:S(2)}, u32[]{:S(2)}) async-start(bf16[4,64,1664]{2,1,0:T(8,128)(2,1)} %get-tuple-element.17), calls=%async_computation | async-start | bytes 1703936 | tf_op jit(solution)/shard_map/all_to_all | solution.py:189
  34.8 3.3 %collective-permute-start.1 = (bf16[224,1664]{1,0:T(8,128)(2,1)S(1)}, bf16[224,1664]{1,0:T(8,128)(2,1)S(1)}, u32[]{:S(2)}, u32[]{:S(2)}) collective-permute-start(bf16[224,1664]{1,0:T(8,128)(2,1)S(1)} %all_gather.9.rows_a_ref), channel_id=1, source_target_pairs={{0,8},{8,0},{1,9},{9,1},{2,10},{10,2},{3,11},{11,3},{4,12},{12,4},... | collective-permute-start | bytes 2236424 | tf_op jit(solution)/shard_map/ppermute | solution.py:32
  38.1 0.1 pad_add_fusion.place_ref
  38.2 8.2 %all-to-all-done = bf16[4,64,1664]{2,1,0:T(8,128)(2,1)S(1)} async-done(((bf16[4,64,1664]{2,1,0:T(8,128)(2,1)}), bf16[4,64,1664]{2,1,0:T(8,128)(2,1)S(1)}, u32[]{:S(2)}, u32[]{:S(2)}) %all-to-all-start) | async-done | bytes 852000 | tf_op jit(solution)/shard_map/all_to_all | solution.py:189
  46.4 0.1 slice.9
  46.4 0.0 collective-permute-done.rows_b_ref
  46.4 0.0 copy-start.1
  46.5 4.3 %collective-permute-start.2 = (bf16[224,1664]{1,0:T(8,128)(2,1)S(1)}, bf16[224,1664]{1,0:T(8,128)(2,1)S(1)}, u32[]{:S(2)}, u32[]{:S(2)}) collective-permute-start(bf16[224,1664]{1,0:T(8,128)(2,1)S(1)} %collective-permute-done.rows_b_ref), channel_id=1, source_target_pairs={{0,8},{8,0},{1,9},{9,1},{2,10},{10,2},{3,11},{11,3},{4,12},{12,4},... | collective-permute-start | bytes 2236424 | tf_op jit(solution)/shard_map/ppermute | solution.py:32
  50.7 0.4 fusion.part_a_ref
  51.1 0.4 fusion.1.part_b_ref
  51.5 0.0 copy-done.1
  51.5 0.0 collective-permute-done.1.rows_c_ref
  51.6 0.0 copy-start.3
  51.6 0.4 fusion.2.part_c_ref
  52.0 0.6 collective-permute-done.2.rows_ref.rows_d_ref
  52.6 0.0 copy-start.5
  52.6 1.1 shard_map.18
  53.7 0.0 copy-done.3
  53.7 20.9 %all_to_all.30.shares_ref = bf16[8,200,128]{2,1,0:T(8,128)(2,1)S(1)} all-to-all(bf16[8,200,128]{2,1,0:T(8,128)(2,1)S(1)} %shard_map.18), channel_id=1, replica_groups=mesh['x'=4,'zh'=4,'zl'=2,'c'=2,'y'=8] {'y'}, dimensions={0} | all-to-all | bytes 819200 | tf_op jit(solution)/shard_map/all_to_all | solution.py:212
  74.6 0.0 copy-done.5
  74.6 0.2 shard_map.19
  74.8 15.1 %all_to_all.31.block_ref = bf16[8,200,128]{2,1,0:T(8,128)(2,1)S(1)} all-to-all(bf16[8,200,128]{2,1,0:T(8,128)(2,1)S(1)} %get-tuple-element.19), channel_id=1, replica_groups=mesh['x'=4,'zh'=4,'zl'=2,'c'=2,'y'=8] {'y'}, dimensions={0} | all-to-all | bytes 819200 | tf_op jit(solution)/shard_map/all_to_all | solution.py:214
  89.9 0.2 shard_map.20
  90.1 0.0 copy-start
  90.1 1.2 copy-done
  91.3 3.6 %all-to-all-start.3 = ((bf16[4,8,200,128]{3,2,1,0:T(8,128)(2,1)}), bf16[4,8,200,128]{3,2,1,0:T(8,128)(2,1)S(1)}, u32[]{:S(2)}, u32[]{:S(2)}) async-start(bf16[4,8,200,128]{3,2,1,0:T(8,128)(2,1)} %copy-done), calls=%async_computation.3 | async-start | bytes 3276800 | tf_op jit(solution)/shard_map/all_to_all | solution.py:219
  94.9 19.8 %all-gather = bf16[3200,128]{1,0:T(8,128)(2,1)S(1)} all-gather(bf16[200,128]{1,0:T(8,128)(2,1)S(1)} %get-tuple-element.21.gram_ref), channel_id=2, replica_groups=mesh['x'=4,'zh'=4,'zl'=2,'c'=2,'y'=8] {'zh','zl','c'}, dimensions={0}, use_global_device_ids=true | all-gather | bytes 870400 | tf_op jit(solution)/shard_map/all_gather | solution.py:220
  114.7 0.0 all-to-all-done.3.right_ref
  114.7 0.0 copy-start.2
  114.7 0.0 copy-start.4
  114.7 0.0 copy-start.6
  114.7 0.9 shard_map.21
  115.6 15.3 %all_to_all.32.poly_ref = bf16[8,200,128]{2,1,0:T(8,128)(2,1)S(1)} all-to-all(bf16[8,200,128]{2,1,0:T(8,128)(2,1)S(1)} %get-tuple-element.23), channel_id=1, replica_groups=mesh['x'=4,'zh'=4,'zl'=2,'c'=2,'y'=8] {'y'}, dimensions={0} | all-to-all | bytes 819200 | tf_op jit(solution)/shard_map/all_to_all | solution.py:228
  130.9 0.0 copy-done.2
  130.9 0.0 copy-done.4
  130.9 0.0 copy-done.6
  130.9 1.6 %shard_map.22 = bf16[4,56,1664]{2,1,0:T(8,128)(2,1)S(1)} custom-call(s32[2]{0:T(128)S(1)} %pad_add_fusion.place_ref, bf16[8,200,128]{2,1,0:T(8,128)(2,1)S(1)} %all_to_all.32.poly_ref, bf16[224,1664]{1,0:T(8,128)(2,1)S(1)} %all_gather.9.rows_a_ref, bf16[224,1664]{1,0:T(8,128)(2,1)S(1)} %copy-done.2, bf16[224,1664]{1,0:T(8,128)(2,1)S(1)} %copy-done.4, ...), custom_call_target="tpu_custom_call" | custom-call | flops 667942912 | bytes 3000000 | tf_op jit(solution)/shard_map/pallas_call | solution.py:229
  132.5 0.0 copy-start.8
  132.5 15.5 %all_to_all.33.product_ref = bf16[4,56,1664]{2,1,0:T(8,128)(2,1)S(1)} all-to-all(bf16[4,56,1664]{2,1,0:T(8,128)(2,1)S(1)} %shard_map.22), channel_id=1, replica_groups=mesh['x'=4,'zh'=4,'zl'=2,'c'=2,'y'=8] {'x'}, dimensions={0} | all-to-all | bytes 1490944 | tf_op jit(solution)/shard_map/all_to_all | solution.py:240
  148.1 0.0 copy-done.8
  148.1 0.9 shard_map.23
  (1 shorter events, 0.0 us)
Async XLA Ops:
  0.0 1.0 copy-start.7
  25.1 21.4 %collective-permute-start = (bf16[224,1664]{1,0:T(8,128)(2,1)S(1)}, bf16[224,1664]{1,0:T(8,128)(2,1)S(1)}, u32[]{:S(2)}, u32[]{:S(2)}) collective-permute-start(bf16[224,1664]{1,0:T(8,128)(2,1)S(1)} %all_gather.9.rows_a_ref), channel_id=1, source_target_pairs={{0,16},{16,32},{32,48},{48,64},{64,80},{80,96},{96,112},{112,0},{8... | collective-permute-start | bytes 2236424 | tf_op jit(solution)/shard_map/ppermute | solution.py:28
  30.7 15.6 %all-to-all-start = ((bf16[4,64,1664]{2,1,0:T(8,128)(2,1)}), bf16[4,64,1664]{2,1,0:T(8,128)(2,1)S(1)}, u32[]{:S(2)}, u32[]{:S(2)}) async-start(bf16[4,64,1664]{2,1,0:T(8,128)(2,1)} %get-tuple-element.17), calls=%async_computation | async-start | bytes 1703936 | tf_op jit(solution)/shard_map/all_to_all | solution.py:189
  34.8 16.8 %collective-permute-start.1 = (bf16[224,1664]{1,0:T(8,128)(2,1)S(1)}, bf16[224,1664]{1,0:T(8,128)(2,1)S(1)}, u32[]{:S(2)}, u32[]{:S(2)}) collective-permute-start(bf16[224,1664]{1,0:T(8,128)(2,1)S(1)} %all_gather.9.rows_a_ref), channel_id=1, source_target_pairs={{0,8},{8,0},{1,9},{9,1},{2,10},{10,2},{3,11},{11,3},{4,12},{12,4},... | collective-permute-start | bytes 2236424 | tf_op jit(solution)/shard_map/ppermute | solution.py:32
  46.4 5.1 %copy-start.1 = (bf16[224,1664]{1,0:T(8,128)(2,1)}, bf16[224,1664]{1,0:T(8,128)(2,1)S(1)}, u32[]{:S(2)}) copy-start(bf16[224,1664]{1,0:T(8,128)(2,1)S(1)} %collective-permute-done.rows_b_ref) | copy-start | bytes 2236420
  46.5 6.1 %collective-permute-start.2 = (bf16[224,1664]{1,0:T(8,128)(2,1)S(1)}, bf16[224,1664]{1,0:T(8,128)(2,1)S(1)}, u32[]{:S(2)}, u32[]{:S(2)}) collective-permute-start(bf16[224,1664]{1,0:T(8,128)(2,1)S(1)} %collective-permute-done.rows_b_ref), channel_id=1, source_target_pairs={{0,8},{8,0},{1,9},{9,1},{2,10},{10,2},{3,11},{11,3},{4,12},{12,4},... | collective-permute-start | bytes 2236424 | tf_op jit(solution)/shard_map/ppermute | solution.py:32
  51.6 2.1 %copy-start.3 = (bf16[224,1664]{1,0:T(8,128)(2,1)}, bf16[224,1664]{1,0:T(8,128)(2,1)S(1)}, u32[]{:S(2)}) copy-start(bf16[224,1664]{1,0:T(8,128)(2,1)S(1)} %collective-permute-done.1.rows_c_ref) | copy-start | bytes 2236420
  52.6 22.0 %copy-start.5 = (bf16[224,1664]{1,0:T(8,128)(2,1)}, bf16[224,1664]{1,0:T(8,128)(2,1)S(1)}, u32[]{:S(2)}) copy-start(bf16[224,1664]{1,0:T(8,128)(2,1)S(1)} %collective-permute-done.2.rows_ref.rows_d_ref) | copy-start | bytes 2236420
  90.1 1.2 copy-start
  91.3 23.4 %all-to-all-start.3 = ((bf16[4,8,200,128]{3,2,1,0:T(8,128)(2,1)}), bf16[4,8,200,128]{3,2,1,0:T(8,128)(2,1)S(1)}, u32[]{:S(2)}, u32[]{:S(2)}) async-start(bf16[4,8,200,128]{3,2,1,0:T(8,128)(2,1)} %copy-done), calls=%async_computation.3 | async-start | bytes 3276800 | tf_op jit(solution)/shard_map/all_to_all | solution.py:219
  114.7 16.2 %copy-start.2 = (bf16[224,1664]{1,0:T(8,128)(2,1)S(1)}, bf16[224,1664]{1,0:T(8,128)(2,1)}, u32[]{:S(2)}) copy-start(bf16[224,1664]{1,0:T(8,128)(2,1)} %copy-done.1) | copy-start | bytes 2236420
  114.7 16.2 %copy-start.4 = (bf16[224,1664]{1,0:T(8,128)(2,1)S(1)}, bf16[224,1664]{1,0:T(8,128)(2,1)}, u32[]{:S(2)}) copy-start(bf16[224,1664]{1,0:T(8,128)(2,1)} %copy-done.3) | copy-start | bytes 2236420
  114.7 16.2 %copy-start.6 = (bf16[224,1664]{1,0:T(8,128)(2,1)S(1)}, bf16[224,1664]{1,0:T(8,128)(2,1)}, u32[]{:S(2)}) copy-start(bf16[224,1664]{1,0:T(8,128)(2,1)} %copy-done.5) | copy-start | bytes 2236420
  132.5 15.6 %copy-start.8 = (f32[56,1664]{1,0:T(8,128)S(1)}, f32[56,1664]{1,0:T(8,128)}, u32[]{:S(2)}) copy-start(f32[56,1664]{1,0:T(8,128)} %momentum_ref.3) | copy-start | bytes 1118212

commit v6 on v5

--- a/solution.py
+++ b/solution.py
@@ -13,6 +13,8 @@
 coef_a = 3.4445
 coef_b = -4.775
 coef_c = 2.0315
+
+lift = 2.0**14
 
 bf16 = jnp.bfloat16
 f32 = jnp.float32
@@ -58,10 +60,11 @@
 
 def start_kernel(momentum_ref, raw_ref, copies_ref):
     momentum = momentum_ref[...]
-    raw_ref[...] = momentum.astype(bf16)
+    lifted = momentum * lift
+    raw_ref[...] = lifted.astype(bf16)
     total = jnp.sum(momentum * momentum, keepdims=True)
     more = in_lanes(0, jnp.broadcast_to(total, (8, 1664)), jnp.zeros((8, 1664), f32))
-    longer = jnp.concatenate([momentum, more], axis=0).astype(bf16)
+    longer = jnp.concatenate([lifted, more], axis=0).astype(bf16)
     for x in range(4):
         copies_ref[x] = longer
 
@@ -137,7 +140,7 @@
                 unpack(left).astype(bf16), right.astype(bf16), preferred_element_type=f32
             )
     factor = math.sqrt(M) / 3.0 / (jnp.sqrt(total) + 1e-07)
-    factor2 = factor * factor
+    factor2 = (factor / lift) * (factor / lift)
     gram = (unpack(gram_ref[...].astype(f32)) * factor2).astype(bf16).astype(f32)
     square = ((square * factor2) * factor2).astype(bf16).astype(f32)
     poly = pack(coef_b * gram + coef_c * square, None).astype(bf16)
@@ -146,7 +149,7 @@
     factor_ref[...] = jnp.broadcast_to(factor, (8, 128))
 
 
-def product_kernel(place_ref, poly_ref, rows_a_ref, rows_b_ref, rows_c_ref, rows_d_ref, product_ref):
+def product_kernel(place_ref, poly_ref, rows_a_ref, rows_b_ref, rows_c_ref, rows_d_ref, product_ref, diagonal_ref):
     zl, first = place_ref[0], place_ref[1] == 0
     product = None
     for own, other, l in ((rows_a_ref, rows_c_ref, zl), (rows_b_ref, rows_d_ref, 1 - zl)):
@@ -163,20 +166,29 @@
             product = term if product is None else product + term
     for x in range(4):
         product_ref[x] = product[56 * x : 56 * x + 56].astype(bf16)
-
-
-def update_kernel(momentum_ref, product_ref, factor_ref, update_ref):
+    block = unpack(poly_ref[2 * place_ref[2] + zl].astype(f32))
+    block = jnp.where(first, block[:56], block[56:])
+    row = lax.broadcasted_iota(jnp.int32, (56, 224), 0)
+    lane = lax.broadcasted_iota(jnp.int32, (56, 224), 1)
+    diagonal = jnp.where(lane == row + 56 * place_ref[3], block, 0.0)
+    diagonal_ref[...] = jnp.broadcast_to(jnp.sum(diagonal, axis=1, keepdims=True), (56, 128))
+
+
+def update_kernel(momentum_ref, product_ref, diagonal_ref, factor_ref, update_ref):
     factor = factor_ref[:1, :1]
     product = product_ref[0].astype(f32)
     for x in range(1, 4):
         product += product_ref[x].astype(f32)
-    iterate = (momentum_ref[...] * factor).astype(bf16).astype(f32)
-    update = (coef_a * iterate + factor * product) * (0.2 * math.sqrt(N))
-    update_ref[...] = update.astype(bf16)
+    momentum = momentum_ref[...]
+    iterate = (momentum * factor).astype(bf16).astype(f32)
+    small = factor / lift
+    change = iterate - small * (momentum * lift).astype(bf16).astype(f32)
+    product = small * product + diagonal_ref[:, :1] * change
+    update_ref[...] = ((coef_a * iterate + product) * (0.2 * math.sqrt(N))).astype(bf16)
 
 
 def per_device(momentum):
-    place = jnp.stack([lax.axis_index("zl"), lax.axis_index("c")]).astype(jnp.int32)
+    place = jnp.stack([lax.axis_index(name) for name in ("zl", "c", "zh", "x")]).astype(jnp.int32)
     short, copies = local(
         start_kernel,
         [jax.ShapeDtypeStruct((56, 1664), bf16), jax.ShapeDtypeStruct((4, 64, 1664), bf16)],
@@ -226,18 +238,18 @@
     )(left, right, piece)
 
     poly = lax.all_to_all(poly, "y", 0, 0)
-    product = local(
+    product, diagonal = local(
         product_kernel,
-        jax.ShapeDtypeStruct((4, 56, 1664), bf16),
+        [jax.ShapeDtypeStruct((4, 56, 1664), bf16), jax.ShapeDtypeStruct((56, 128), f32)],
         [pltpu.SMEM] + [pltpu.VMEM] * 5,
         2 * 896 * 224 * 1664,
     )(place, poly, rows_a, rows_b, rows_c, rows_d)
     return local(
         update_kernel,
         jax.ShapeDtypeStruct((56, 1664), bf16),
-        [pltpu.VMEM] * 3,
+        [pltpu.VMEM] * 4,
         1_000_000,
-    )(momentum, lax.all_to_all(product, "x", 0, 0), factor)
+    )(momentum, lax.all_to_all(product, "x", 0, 0), diagonal, factor)
 
 
 def solution(mesh):

time: 152 us -> 152 us (level)
  no operation moved by 1% of the time
where the time goes in v6:
time: 152 us; the launch traced here: 149 us
  blocking collectives  109 us (72%)
  starting transfers between devices  20.9 us (14%)
  waiting for transfers between devices  8.75 us (6%)
  Pallas kernels  6.3 us (4%)
  local copies, waits for them, and re-layouts  2.26 us (1%)
    all_gather x1, blocking collectives, per_device(): rows_a = lax.all_gather(short, 'zh', axis=0, tiled=True)  22.9 us
    all_to_all x1, blocking collectives, per_device(): lax.all_to_all(parts, 'y', 0, 0)  20.9 us
    all_gather x1, blocking collectives, per_device(): left = lax.all_gather(piece, ('zh', 'zl', 'c'), axis=0)  19.8 us
    all_to_all x1, blocking collectives, per_device(): lax.all_to_all(product, 'x', 0, 0)  15.4 us
    all_to_all x1, blocking collectives, per_device(): poly = lax.all_to_all(poly, 'y', 0, 0)  15.3 us
    all_to_all x1, blocking collectives, per_device(): right = lax.all_to_all(copies, 'y', 0, 0)  15.1 us
    all_to_all x1, waiting for transfers between devices, per_device(): gathered_x = lax.all_to_all(copies, 'x', 0, 0)  8.15 us
    ppermute x2, starting transfers between devices, other_core(): return lax.ppermute(block, 'c', swap(2, 1))  7.61 us
  transfers between devices with their start and end apart: 5, of which 2 were waited for; matrix products, arithmetic and copies ran while one was open for 1% of the time, Pallas kernels for 0%

profile of v6, /device:TPU:1, one launch (start us, length us, event | category | flops | bytes accessed | tf_op | source)
XLA Modules:
  0.0 149.0 jit_solution(15037933383646509846)
XLA Ops:
  0.0 0.0 copy-start.7
  0.0 1.0 copy-done.7
  1.0 1.2 shard_map.17
  2.2 22.9 %all_gather.9.rows_a_ref = bf16[224,1664]{1,0:T(8,128)(2,1)S(1)} all-gather(bf16[56,1664]{1,0:T(8,128)(2,1)S(1)} %get-tuple-element.17), channel_id=1, replica_groups=mesh['x'=4,'zh'=4,'zl'=2,'c'=2,'y'=8] {'zh'}, dimensions={0}, use_global_device_ids=true | all-gather | bytes 931840 | tf_op jit(solution)/shard_map/all_gather | solution.py:199
  25.1 5.7 %collective-permute-start = (bf16[224,1664]{1,0:T(8,128)(2,1)S(1)}, bf16[224,1664]{1,0:T(8,128)(2,1)S(1)}, u32[]{:S(2)}, u32[]{:S(2)}) collective-permute-start(bf16[224,1664]{1,0:T(8,128)(2,1)S(1)} %all_gather.9.rows_a_ref), channel_id=1, source_target_pairs={{0,16},{16,32},{32,48},{48,64},{64,80},{80,96},{96,112},{112,0},{8... | collective-permute-start | bytes 2236424 | tf_op jit(solution)/shard_map/ppermute | solution.py:30
  30.7 4.0 %all-to-all-start = ((bf16[4,64,1664]{2,1,0:T(8,128)(2,1)}), bf16[4,64,1664]{2,1,0:T(8,128)(2,1)S(1)}, u32[]{:S(2)}, u32[]{:S(2)}) async-start(bf16[4,64,1664]{2,1,0:T(8,128)(2,1)} %get-tuple-element.19), calls=%async_computation | async-start | bytes 1703936 | tf_op jit(solution)/shard_map/all_to_all | solution.py:201
  34.8 3.3 %collective-permute-start.1 = (bf16[224,1664]{1,0:T(8,128)(2,1)S(1)}, bf16[224,1664]{1,0:T(8,128)(2,1)S(1)}, u32[]{:S(2)}, u32[]{:S(2)}) collective-permute-start(bf16[224,1664]{1,0:T(8,128)(2,1)S(1)} %all_gather.9.rows_a_ref), channel_id=1, source_target_pairs={{0,8},{8,0},{1,9},{9,1},{2,10},{10,2},{3,11},{11,3},{4,12},{12,4},... | collective-permute-start | bytes 2236424 | tf_op jit(solution)/shard_map/ppermute | solution.py:34
  38.1 0.1 pad_add_fusion.place_ref
  38.2 8.1 %all-to-all-done = bf16[4,64,1664]{2,1,0:T(8,128)(2,1)S(1)} async-done(((bf16[4,64,1664]{2,1,0:T(8,128)(2,1)}), bf16[4,64,1664]{2,1,0:T(8,128)(2,1)S(1)}, u32[]{:S(2)}, u32[]{:S(2)}) %all-to-all-start) | async-done | bytes 852000 | tf_op jit(solution)/shard_map/all_to_all | solution.py:201
  46.4 0.1 slice.9
  46.4 0.0 collective-permute-done.rows_b_ref
  46.4 0.0 copy-start.1
  46.5 4.3 %collective-permute-start.2 = (bf16[224,1664]{1,0:T(8,128)(2,1)S(1)}, bf16[224,1664]{1,0:T(8,128)(2,1)S(1)}, u32[]{:S(2)}, u32[]{:S(2)}) collective-permute-start(bf16[224,1664]{1,0:T(8,128)(2,1)S(1)} %collective-permute-done.rows_b_ref), channel_id=1, source_target_pairs={{0,8},{8,0},{1,9},{9,1},{2,10},{10,2},{3,11},{11,3},{4,12},{12,4},... | collective-permute-start | bytes 2236424 | tf_op jit(solution)/shard_map/ppermute | solution.py:34
  50.7 0.4 fusion.part_a_ref
  51.1 0.4 fusion.1.part_b_ref
  51.5 0.0 copy-done.1
  51.6 0.0 collective-permute-done.1.rows_c_ref
  51.6 0.0 copy-start.3
  51.6 0.4 fusion.2.part_c_ref
  52.0 0.6 collective-permute-done.2.rows_ref.rows_d_ref
  52.6 0.0 copy-start.5
  52.6 1.1 shard_map.18
  53.7 0.0 copy-done.3
  53.7 20.9 %all_to_all.30.shares_ref = bf16[8,200,128]{2,1,0:T(8,128)(2,1)S(1)} all-to-all(bf16[8,200,128]{2,1,0:T(8,128)(2,1)S(1)} %shard_map.18), channel_id=1, replica_groups=mesh['x'=4,'zh'=4,'zl'=2,'c'=2,'y'=8] {'y'}, dimensions={0} | all-to-all | bytes 819200 | tf_op jit(solution)/shard_map/all_to_all | solution.py:224
  74.6 0.0 copy-done.5
  74.6 0.2 shard_map.19
  74.7 15.1 %all_to_all.31.block_ref = bf16[8,200,128]{2,1,0:T(8,128)(2,1)S(1)} all-to-all(bf16[8,200,128]{2,1,0:T(8,128)(2,1)S(1)} %get-tuple-element.21), channel_id=1, replica_groups=mesh['x'=4,'zh'=4,'zl'=2,'c'=2,'y'=8] {'y'}, dimensions={0} | all-to-all | bytes 819200 | tf_op jit(solution)/shard_map/all_to_all | solution.py:226
  89.9 0.2 shard_map.20
  90.1 0.0 copy-start
  90.1 1.2 copy-done
  91.3 3.6 %all-to-all-start.3 = ((bf16[4,8,200,128]{3,2,1,0:T(8,128)(2,1)}), bf16[4,8,200,128]{3,2,1,0:T(8,128)(2,1)S(1)}, u32[]{:S(2)}, u32[]{:S(2)}) async-start(bf16[4,8,200,128]{3,2,1,0:T(8,128)(2,1)} %copy-done), calls=%async_computation.3 | async-start | bytes 3276800 | tf_op jit(solution)/shard_map/all_to_all | solution.py:231
  94.8 19.8 %all-gather = bf16[3200,128]{1,0:T(8,128)(2,1)S(1)} all-gather(bf16[200,128]{1,0:T(8,128)(2,1)S(1)} %get-tuple-element.23.gram_ref), channel_id=2, replica_groups=mesh['x'=4,'zh'=4,'zl'=2,'c'=2,'y'=8] {'zh','zl','c'}, dimensions={0}, use_global_device_ids=true | all-gather | bytes 870400 | tf_op jit(solution)/shard_map/all_gather | solution.py:232
  114.7 0.0 all-to-all-done.3.right_ref
  114.7 0.0 copy-start.2
  114.7 0.0 copy-start.4
  114.7 0.0 copy-start.6
  114.7 0.9 shard_map.21
  115.6 15.3 %all_to_all.32.poly_ref = bf16[8,200,128]{2,1,0:T(8,128)(2,1)S(1)} all-to-all(bf16[8,200,128]{2,1,0:T(8,128)(2,1)S(1)} %get-tuple-element.25), channel_id=1, replica_groups=mesh['x'=4,'zh'=4,'zl'=2,'c'=2,'y'=8] {'y'}, dimensions={0} | all-to-all | bytes 819200 | tf_op jit(solution)/shard_map/all_to_all | solution.py:240
  130.9 0.0 copy-done.2
  130.9 0.0 copy-done.4
  130.9 0.0 copy-done.6
  130.9 0.0 copy-start.8
  130.9 1.6 %shard_map.22 = (bf16[4,56,1664]{2,1,0:T(8,128)(2,1)S(1)}, f32[56,128]{1,0:T(8,128)S(1)}) custom-call(s32[4]{0:T(128)S(1)} %pad_add_fusion.place_ref, bf16[8,200,128]{2,1,0:T(8,128)(2,1)S(1)} %all_to_all.32.poly_ref, bf16[224,1664]{1,0:T(8,128)(2,1)S(1)} %all_gather.9.rows_a_ref, bf16[224,1664]{1,0:T(8,128)(2,1)S(1)} %copy-done.2, ...), custom_call_target="tpu_custom_call" | custom-call | flops 667942912 | bytes 3000000 | tf_op jit(solution)/shard_map/pallas_call | solution.py:241
  132.5 15.4 %all_to_all.33.product_ref = bf16[4,56,1664]{2,1,0:T(8,128)(2,1)S(1)} all-to-all(bf16[4,56,1664]{2,1,0:T(8,128)(2,1)S(1)} %get-tuple-element.26), channel_id=1, replica_groups=mesh['x'=4,'zh'=4,'zl'=2,'c'=2,'y'=8] {'x'}, dimensions={0} | all-to-all | bytes 1490944 | tf_op jit(solution)/shard_map/all_to_all | solution.py:252
  147.9 0.0 copy-done.8
  147.9 1.1 shard_map.23
  (1 shorter events, 0.0 us)
Async XLA Ops:
  0.0 1.0 copy-start.7
  25.1 21.4 %collective-permute-start = (bf16[224,1664]{1,0:T(8,128)(2,1)S(1)}, bf16[224,1664]{1,0:T(8,128)(2,1)S(1)}, u32[]{:S(2)}, u32[]{:S(2)}) collective-permute-start(bf16[224,1664]{1,0:T(8,128)(2,1)S(1)} %all_gather.9.rows_a_ref), channel_id=1, source_target_pairs={{0,16},{16,32},{32,48},{48,64},{64,80},{80,96},{96,112},{112,0},{8... | collective-permute-start | bytes 2236424 | tf_op jit(solution)/shard_map/ppermute | solution.py:30
  30.7 15.6 %all-to-all-start = ((bf16[4,64,1664]{2,1,0:T(8,128)(2,1)}), bf16[4,64,1664]{2,1,0:T(8,128)(2,1)S(1)}, u32[]{:S(2)}, u32[]{:S(2)}) async-start(bf16[4,64,1664]{2,1,0:T(8,128)(2,1)} %get-tuple-element.19), calls=%async_computation | async-start | bytes 1703936 | tf_op jit(solution)/shard_map/all_to_all | solution.py:201
  34.8 16.8 %collective-permute-start.1 = (bf16[224,1664]{1,0:T(8,128)(2,1)S(1)}, bf16[224,1664]{1,0:T(8,128)(2,1)S(1)}, u32[]{:S(2)}, u32[]{:S(2)}) collective-permute-start(bf16[224,1664]{1,0:T(8,128)(2,1)S(1)} %all_gather.9.rows_a_ref), channel_id=1, source_target_pairs={{0,8},{8,0},{1,9},{9,1},{2,10},{10,2},{3,11},{11,3},{4,12},{12,4},... | collective-permute-start | bytes 2236424 | tf_op jit(solution)/shard_map/ppermute | solution.py:34
  46.4 5.1 %copy-start.1 = (bf16[224,1664]{1,0:T(8,128)(2,1)}, bf16[224,1664]{1,0:T(8,128)(2,1)S(1)}, u32[]{:S(2)}) copy-start(bf16[224,1664]{1,0:T(8,128)(2,1)S(1)} %collective-permute-done.rows_b_ref) | copy-start | bytes 2236420
  46.5 6.1 %collective-permute-start.2 = (bf16[224,1664]{1,0:T(8,128)(2,1)S(1)}, bf16[224,1664]{1,0:T(8,128)(2,1)S(1)}, u32[]{:S(2)}, u32[]{:S(2)}) collective-permute-start(bf16[224,1664]{1,0:T(8,128)(2,1)S(1)} %collective-permute-done.rows_b_ref), channel_id=1, source_target_pairs={{0,8},{8,0},{1,9},{9,1},{2,10},{10,2},{3,11},{11,3},{4,12},{12,4},... | collective-permute-start | bytes 2236424 | tf_op jit(solution)/shard_map/ppermute | solution.py:34
  51.6 2.1 %copy-start.3 = (bf16[224,1664]{1,0:T(8,128)(2,1)}, bf16[224,1664]{1,0:T(8,128)(2,1)S(1)}, u32[]{:S(2)}) copy-start(bf16[224,1664]{1,0:T(8,128)(2,1)S(1)} %collective-permute-done.1.rows_c_ref) | copy-start | bytes 2236420
  52.6 22.0 %copy-start.5 = (bf16[224,1664]{1,0:T(8,128)(2,1)}, bf16[224,1664]{1,0:T(8,128)(2,1)S(1)}, u32[]{:S(2)}) copy-start(bf16[224,1664]{1,0:T(8,128)(2,1)S(1)} %collective-permute-done.2.rows_ref.rows_d_ref) | copy-start | bytes 2236420
  90.1 1.2 copy-start
  91.3 23.4 %all-to-all-start.3 = ((bf16[4,8,200,128]{3,2,1,0:T(8,128)(2,1)}), bf16[4,8,200,128]{3,2,1,0:T(8,128)(2,1)S(1)}, u32[]{:S(2)}, u32[]{:S(2)}) async-start(bf16[4,8,200,128]{3,2,1,0:T(8,128)(2,1)} %copy-done), calls=%async_computation.3 | async-start | bytes 3276800 | tf_op jit(solution)/shard_map/all_to_all | solution.py:231
  114.7 16.2 %copy-start.2 = (bf16[224,1664]{1,0:T(8,128)(2,1)S(1)}, bf16[224,1664]{1,0:T(8,128)(2,1)}, u32[]{:S(2)}) copy-start(bf16[224,1664]{1,0:T(8,128)(2,1)} %copy-done.1) | copy-start | bytes 2236420
  114.7 16.2 %copy-start.4 = (bf16[224,1664]{1,0:T(8,128)(2,1)S(1)}, bf16[224,1664]{1,0:T(8,128)(2,1)}, u32[]{:S(2)}) copy-start(bf16[224,1664]{1,0:T(8,128)(2,1)} %copy-done.3) | copy-start | bytes 2236420
  114.7 16.2 %copy-start.6 = (bf16[224,1664]{1,0:T(8,128)(2,1)S(1)}, bf16[224,1664]{1,0:T(8,128)(2,1)}, u32[]{:S(2)}) copy-start(bf16[224,1664]{1,0:T(8,128)(2,1)} %copy-done.5) | copy-start | bytes 2236420
  130.9 17.1 %copy-start.8 = (f32[56,1664]{1,0:T(8,128)S(1)}, f32[56,1664]{1,0:T(8,128)}, u32[]{:S(2)}) copy-start(f32[56,1664]{1,0:T(8,128)} %momentum_ref.3) | copy-start | bytes 1118212

commit v7 on v6

--- a/solution.py
+++ b/solution.py
@@ -63,8 +63,8 @@
     lifted = momentum * lift
     raw_ref[...] = lifted.astype(bf16)
     total = jnp.sum(momentum * momentum, keepdims=True)
-    more = in_lanes(0, jnp.broadcast_to(total, (8, 1664)), jnp.zeros((8, 1664), f32))
-    longer = jnp.concatenate([lifted, more], axis=0).astype(bf16)
+    more = in_lanes(0, jnp.broadcast_to(total, (56, 128)), jnp.zeros((56, 128), f32))
+    longer = jnp.concatenate([lifted, more], axis=1).astype(bf16)
     for x in range(4):
         copies_ref[x] = longer
 
@@ -104,7 +104,7 @@
     )
     total = jnp.zeros((8, 128), f32)
     for x in range(4):
-        total += totals_ref[x, :, :128].astype(f32)[56:]
+        total += totals_ref[x].astype(f32)
     total = jnp.sum(total[:1], axis=1, keepdims=True)
     for own, other, l in ((part_a_ref, part_c_ref, zl), (part_b_ref, part_d, 1 - zl)):
         for zh in range(4):
@@ -191,7 +191,7 @@
     place = jnp.stack([lax.axis_index(name) for name in ("zl", "c", "zh", "x")]).astype(jnp.int32)
     short, copies = local(
         start_kernel,
-        [jax.ShapeDtypeStruct((56, 1664), bf16), jax.ShapeDtypeStruct((4, 64, 1664), bf16)],
+        [jax.ShapeDtypeStruct((56, 1664), bf16), jax.ShapeDtypeStruct((4, 56, 1792), bf16)],
         [pltpu.VMEM],
         1_000_000,
     )(momentum)
@@ -199,7 +199,7 @@
     rows_a = lax.all_gather(short, "zh", axis=0, tiled=True)
     rows_a, copies = lax.optimization_barrier((rows_a, copies))
     gathered_x = lax.all_to_all(copies, "x", 0, 0)
-    rows_x = gathered_x[:, :56].reshape(224, 1664)
+    rows_x = gathered_x[:, :, :1664].reshape(224, 1664)
     rows_b = from_next_z(rows_a)
     rows_c = other_core(rows_a)
     rows_d = other_core(rows_b)
@@ -211,7 +211,7 @@
         2 * 224 * 224 * 1664,
     )(
         place,
-        gathered_x[:, :, :128],
+        gathered_x[:, :8, 1664:],
         *(rows_dot(rows, rows_x) for rows in (rows_a, rows_b, rows_c)),
         rows_d,
         rows_x,

time: 152 us -> 151 us (level)
  no operation moved by 1% of the time
where the time goes in v7:
time: 151 us; the launch traced here: 148 us
  blocking collectives  109 us (72%)
  starting transfers between devices  20.9 us (14%)
  waiting for transfers between devices  8.22 us (5%)
  Pallas kernels  6.28 us (4%)
  local copies, waits for them, and re-layouts  2.25 us (1%)
    all_gather x1, blocking collectives, per_device(): rows_a = lax.all_gather(short, 'zh', axis=0, tiled=True)  22.9 us
    all_to_all x1, blocking collectives, per_device(): lax.all_to_all(parts, 'y', 0, 0)  20.9 us
    all_gather x1, blocking collectives, per_device(): left = lax.all_gather(piece, ('zh', 'zl', 'c'), axis=0)  19.8 us
    all_to_all x1, blocking collectives, per_device(): lax.all_to_all(product, 'x', 0, 0)  15.4 us
    all_to_all x1, blocking collectives, per_device(): poly = lax.all_to_all(poly, 'y', 0, 0)  15.3 us
    all_to_all x1, blocking collectives, per_device(): right = lax.all_to_all(copies, 'y', 0, 0)  15.1 us
    all_to_all x1, waiting for transfers between devices, per_device(): gathered_x = lax.all_to_all(copies, 'x', 0, 0)  7.62 us
    ppermute x2, starting transfers between devices, other_core(): return lax.ppermute(block, 'c', swap(2, 1))  7.61 us
  transfers between devices with their start and end apart: 5, of which 2 were waited for; matrix products, arithmetic and copies ran while one was open for 1% of the time, Pallas kernels for 0%

profile of v7, /device:TPU:1, one launch (start us, length us, event | category | flops | bytes accessed | tf_op | source)
XLA Modules:
  0.0 148.5 jit_solution(15567320411599669802)
XLA Ops:
  0.0 0.0 copy-start.7
  0.0 1.0 copy-done.7
  1.0 1.2 shard_map.17
  2.2 22.9 %all_gather.9.rows_a_ref = bf16[224,1664]{1,0:T(8,128)(2,1)S(1)} all-gather(bf16[56,1664]{1,0:T(8,128)(2,1)S(1)} %get-tuple-element.17), channel_id=1, replica_groups=mesh['x'=4,'zh'=4,'zl'=2,'c'=2,'y'=8] {'zh'}, dimensions={0}, use_global_device_ids=true | all-gather | bytes 931840 | tf_op jit(solution)/shard_map/all_gather | solution.py:199
  25.1 5.7 %collective-permute-start = (bf16[224,1664]{1,0:T(8,128)(2,1)S(1)}, bf16[224,1664]{1,0:T(8,128)(2,1)S(1)}, u32[]{:S(2)}, u32[]{:S(2)}) collective-permute-start(bf16[224,1664]{1,0:T(8,128)(2,1)S(1)} %all_gather.9.rows_a_ref), channel_id=1, source_target_pairs={{0,16},{16,32},{32,48},{48,64},{64,80},{80,96},{96,112},{112,0},{8... | collective-permute-start | bytes 2236424 | tf_op jit(solution)/shard_map/ppermute | solution.py:30
  30.7 4.0 %all-to-all-start = ((bf16[4,56,1792]{2,1,0:T(8,128)(2,1)}), bf16[4,56,1792]{2,1,0:T(8,128)(2,1)S(1)}, u32[]{:S(2)}, u32[]{:S(2)}) async-start(bf16[4,56,1792]{2,1,0:T(8,128)(2,1)} %get-tuple-element.19), calls=%async_computation | async-start | bytes 1605632 | tf_op jit(solution)/shard_map/all_to_all | solution.py:201
  34.8 3.3 %collective-permute-start.1 = (bf16[224,1664]{1,0:T(8,128)(2,1)S(1)}, bf16[224,1664]{1,0:T(8,128)(2,1)S(1)}, u32[]{:S(2)}, u32[]{:S(2)}) collective-permute-start(bf16[224,1664]{1,0:T(8,128)(2,1)S(1)} %all_gather.9.rows_a_ref), channel_id=1, source_target_pairs={{0,8},{8,0},{1,9},{9,1},{2,10},{10,2},{3,11},{11,3},{4,12},{12,4},... | collective-permute-start | bytes 2236424 | tf_op jit(solution)/shard_map/ppermute | solution.py:34
  38.1 0.1 pad_add_fusion.place_ref
  38.2 7.6 %all-to-all-done = bf16[4,56,1792]{2,1,0:T(8,128)(2,1)S(1)} async-done(((bf16[4,56,1792]{2,1,0:T(8,128)(2,1)}), bf16[4,56,1792]{2,1,0:T(8,128)(2,1)S(1)}, u32[]{:S(2)}, u32[]{:S(2)}) %all-to-all-start) | async-done | bytes 802848 | tf_op jit(solution)/shard_map/all_to_all | solution.py:201
  45.8 0.1 slice.9
  45.9 0.0 collective-permute-done.rows_b_ref
  45.9 0.0 copy-start.1
  45.9 4.3 %collective-permute-start.2 = (bf16[224,1664]{1,0:T(8,128)(2,1)S(1)}, bf16[224,1664]{1,0:T(8,128)(2,1)S(1)}, u32[]{:S(2)}, u32[]{:S(2)}) collective-permute-start(bf16[224,1664]{1,0:T(8,128)(2,1)S(1)} %collective-permute-done.rows_b_ref), channel_id=1, source_target_pairs={{0,8},{8,0},{1,9},{9,1},{2,10},{10,2},{3,11},{11,3},{4,12},{12,4},... | collective-permute-start | bytes 2236424 | tf_op jit(solution)/shard_map/ppermute | solution.py:34
  50.2 0.4 fusion.part_a_ref
  50.6 0.4 fusion.1.part_b_ref
  51.0 0.0 copy-done.1
  51.0 0.0 collective-permute-done.1.rows_c_ref
  51.0 0.0 copy-start.3
  51.0 0.4 fusion.2.part_c_ref
  51.4 0.6 collective-permute-done.2.rows_ref.rows_d_ref
  52.0 0.0 copy-start.5
  52.0 1.1 shard_map.18
  53.1 0.0 copy-done.3
  53.1 20.9 %all_to_all.30.shares_ref = bf16[8,200,128]{2,1,0:T(8,128)(2,1)S(1)} all-to-all(bf16[8,200,128]{2,1,0:T(8,128)(2,1)S(1)} %shard_map.18), channel_id=1, replica_groups=mesh['x'=4,'zh'=4,'zl'=2,'c'=2,'y'=8] {'y'}, dimensions={0} | all-to-all | bytes 819200 | tf_op jit(solution)/shard_map/all_to_all | solution.py:224
  74.0 0.0 copy-done.5
  74.0 0.2 shard_map.19
  74.2 15.1 %all_to_all.31.block_ref = bf16[8,200,128]{2,1,0:T(8,128)(2,1)S(1)} all-to-all(bf16[8,200,128]{2,1,0:T(8,128)(2,1)S(1)} %get-tuple-element.21), channel_id=1, replica_groups=mesh['x'=4,'zh'=4,'zl'=2,'c'=2,'y'=8] {'y'}, dimensions={0} | all-to-all | bytes 819200 | tf_op jit(solution)/shard_map/all_to_all | solution.py:226
  89.3 0.2 shard_map.20
  89.5 0.0 copy-start
  89.5 1.2 copy-done
  90.7 3.6 %all-to-all-start.3 = ((bf16[4,8,200,128]{3,2,1,0:T(8,128)(2,1)}), bf16[4,8,200,128]{3,2,1,0:T(8,128)(2,1)S(1)}, u32[]{:S(2)}, u32[]{:S(2)}) async-start(bf16[4,8,200,128]{3,2,1,0:T(8,128)(2,1)} %copy-done), calls=%async_computation.3 | async-start | bytes 3276800 | tf_op jit(solution)/shard_map/all_to_all | solution.py:231
  94.3 19.8 %all-gather = bf16[3200,128]{1,0:T(8,128)(2,1)S(1)} all-gather(bf16[200,128]{1,0:T(8,128)(2,1)S(1)} %get-tuple-element.23.gram_ref), channel_id=2, replica_groups=mesh['x'=4,'zh'=4,'zl'=2,'c'=2,'y'=8] {'zh','zl','c'}, dimensions={0}, use_global_device_ids=true | all-gather | bytes 870400 | tf_op jit(solution)/shard_map/all_gather | solution.py:232
  114.1 0.0 all-to-all-done.3.right_ref
  114.1 0.0 copy-start.2
  114.1 0.0 copy-start.4
  114.1 0.0 copy-start.6
  114.1 0.9 shard_map.21
  115.0 15.3 %all_to_all.32.poly_ref = bf16[8,200,128]{2,1,0:T(8,128)(2,1)S(1)} all-to-all(bf16[8,200,128]{2,1,0:T(8,128)(2,1)S(1)} %get-tuple-element.25), channel_id=1, replica_groups=mesh['x'=4,'zh'=4,'zl'=2,'c'=2,'y'=8] {'y'}, dimensions={0} | all-to-all | bytes 819200 | tf_op jit(solution)/shard_map/all_to_all | solution.py:240
  130.3 0.0 copy-done.2
  130.3 0.0 copy-done.4
  130.3 0.0 copy-done.6
  130.3 0.0 copy-start.8
  130.3 1.6 %shard_map.22 = (bf16[4,56,1664]{2,1,0:T(8,128)(2,1)S(1)}, f32[56,128]{1,0:T(8,128)S(1)}) custom-call(s32[4]{0:T(128)S(1)} %pad_add_fusion.place_ref, bf16[8,200,128]{2,1,0:T(8,128)(2,1)S(1)} %all_to_all.32.poly_ref, bf16[224,1664]{1,0:T(8,128)(2,1)S(1)} %all_gather.9.rows_a_ref, bf16[224,1664]{1,0:T(8,128)(2,1)S(1)} %copy-done.2, ...), custom_call_target="tpu_custom_call" | custom-call | flops 667942912 | bytes 3000000 | tf_op jit(solution)/shard_map/pallas_call | solution.py:241
  132.0 15.4 %all_to_all.33.product_ref = bf16[4,56,1664]{2,1,0:T(8,128)(2,1)S(1)} all-to-all(bf16[4,56,1664]{2,1,0:T(8,128)(2,1)S(1)} %get-tuple-element.26), channel_id=1, replica_groups=mesh['x'=4,'zh'=4,'zl'=2,'c'=2,'y'=8] {'x'}, dimensions={0} | all-to-all | bytes 1490944 | tf_op jit(solution)/shard_map/all_to_all | solution.py:252
  147.4 0.0 copy-done.8
  147.4 1.1 shard_map.23
  (1 shorter events, 0.0 us)
Async XLA Ops:
  0.0 1.0 copy-start.7
  25.1 20.8 %collective-permute-start = (bf16[224,1664]{1,0:T(8,128)(2,1)S(1)}, bf16[224,1664]{1,0:T(8,128)(2,1)S(1)}, u32[]{:S(2)}, u32[]{:S(2)}) collective-permute-start(bf16[224,1664]{1,0:T(8,128)(2,1)S(1)} %all_gather.9.rows_a_ref), channel_id=1, source_target_pairs={{0,16},{16,32},{32,48},{48,64},{64,80},{80,96},{96,112},{112,0},{8... | collective-permute-start | bytes 2236424 | tf_op jit(solution)/shard_map/ppermute | solution.py:30
  30.7 15.1 %all-to-all-start = ((bf16[4,56,1792]{2,1,0:T(8,128)(2,1)}), bf16[4,56,1792]{2,1,0:T(8,128)(2,1)S(1)}, u32[]{:S(2)}, u32[]{:S(2)}) async-start(bf16[4,56,1792]{2,1,0:T(8,128)(2,1)} %get-tuple-element.19), calls=%async_computation | async-start | bytes 1605632 | tf_op jit(solution)/shard_map/all_to_all | solution.py:201
  34.8 16.2 %collective-permute-start.1 = (bf16[224,1664]{1,0:T(8,128)(2,1)S(1)}, bf16[224,1664]{1,0:T(8,128)(2,1)S(1)}, u32[]{:S(2)}, u32[]{:S(2)}) collective-permute-start(bf16[224,1664]{1,0:T(8,128)(2,1)S(1)} %all_gather.9.rows_a_ref), channel_id=1, source_target_pairs={{0,8},{8,0},{1,9},{9,1},{2,10},{10,2},{3,11},{11,3},{4,12},{12,4},... | collective-permute-start | bytes 2236424 | tf_op jit(solution)/shard_map/ppermute | solution.py:34
  45.9 5.1 %copy-start.1 = (bf16[224,1664]{1,0:T(8,128)(2,1)}, bf16[224,1664]{1,0:T(8,128)(2,1)S(1)}, u32[]{:S(2)}) copy-start(bf16[224,1664]{1,0:T(8,128)(2,1)S(1)} %collective-permute-done.rows_b_ref) | copy-start | bytes 2236420
  45.9 6.1 %collective-permute-start.2 = (bf16[224,1664]{1,0:T(8,128)(2,1)S(1)}, bf16[224,1664]{1,0:T(8,128)(2,1)S(1)}, u32[]{:S(2)}, u32[]{:S(2)}) collective-permute-start(bf16[224,1664]{1,0:T(8,128)(2,1)S(1)} %collective-permute-done.rows_b_ref), channel_id=1, source_target_pairs={{0,8},{8,0},{1,9},{9,1},{2,10},{10,2},{3,11},{11,3},{4,12},{12,4},... | collective-permute-start | bytes 2236424 | tf_op jit(solution)/shard_map/ppermute | solution.py:34
  51.0 2.1 %copy-start.3 = (bf16[224,1664]{1,0:T(8,128)(2,1)}, bf16[224,1664]{1,0:T(8,128)(2,1)S(1)}, u32[]{:S(2)}) copy-start(bf16[224,1664]{1,0:T(8,128)(2,1)S(1)} %collective-permute-done.1.rows_c_ref) | copy-start | bytes 2236420
  52.0 22.0 %copy-start.5 = (bf16[224,1664]{1,0:T(8,128)(2,1)}, bf16[224,1664]{1,0:T(8,128)(2,1)S(1)}, u32[]{:S(2)}) copy-start(bf16[224,1664]{1,0:T(8,128)(2,1)S(1)} %collective-permute-done.2.rows_ref.rows_d_ref) | copy-start | bytes 2236420
  89.5 1.2 copy-start
  90.7 23.4 %all-to-all-start.3 = ((bf16[4,8,200,128]{3,2,1,0:T(8,128)(2,1)}), bf16[4,8,200,128]{3,2,1,0:T(8,128)(2,1)S(1)}, u32[]{:S(2)}, u32[]{:S(2)}) async-start(bf16[4,8,200,128]{3,2,1,0:T(8,128)(2,1)} %copy-done), calls=%async_computation.3 | async-start | bytes 3276800 | tf_op jit(solution)/shard_map/all_to_all | solution.py:231
  114.1 16.2 %copy-start.2 = (bf16[224,1664]{1,0:T(8,128)(2,1)S(1)}, bf16[224,1664]{1,0:T(8,128)(2,1)}, u32[]{:S(2)}) copy-start(bf16[224,1664]{1,0:T(8,128)(2,1)} %copy-done.1) | copy-start | bytes 2236420
  114.1 16.2 %copy-start.4 = (bf16[224,1664]{1,0:T(8,128)(2,1)S(1)}, bf16[224,1664]{1,0:T(8,128)(2,1)}, u32[]{:S(2)}) copy-start(bf16[224,1664]{1,0:T(8,128)(2,1)} %copy-done.3) | copy-start | bytes 2236420
  114.1 16.2 %copy-start.6 = (bf16[224,1664]{1,0:T(8,128)(2,1)S(1)}, bf16[224,1664]{1,0:T(8,128)(2,1)}, u32[]{:S(2)}) copy-start(bf16[224,1664]{1,0:T(8,128)(2,1)} %copy-done.5) | copy-start | bytes 2236420
  130.3 17.1 %copy-start.8 = (f32[56,1664]{1,0:T(8,128)S(1)}, f32[56,1664]{1,0:T(8,128)}, u32[]{:S(2)}) copy-start(f32[56,1664]{1,0:T(8,128)} %momentum_ref.3) | copy-start | bytes 1118212

commit v8 on v7

--- a/solution.py
+++ b/solution.py
@@ -67,11 +67,6 @@
     longer = jnp.concatenate([lifted, more], axis=1).astype(bf16)
     for x in range(4):
         copies_ref[x] = longer
-
-
-def copies_kernel(block_ref, copies_ref):
-    for x in range(4):
-        copies_ref[x] = block_ref[...]
 
 
 def pack(block, total):
@@ -225,9 +220,7 @@
 
     right = lax.all_to_all(copies, "y", 0, 0)
     right, piece = lax.optimization_barrier((right, piece))
-    copies = local(
-        copies_kernel, jax.ShapeDtypeStruct((4, 8, 200, 128), bf16), [pltpu.VMEM], 1_000_000
-    )(right)
+    copies = jnp.broadcast_to(right[None], (4, *right.shape))
     right = lax.all_to_all(copies, "x", 0, 0)
     left = lax.all_gather(piece, ("zh", "zl", "c"), axis=0)
     poly, factor = local(

time: 151 us -> 151 us (level)
  no operation moved by 1% of the time
where the time goes in v8:
time: 151 us; the launch traced here: 148 us
  blocking collectives  109 us (72%)
  starting transfers between devices  20.9 us (14%)
  waiting for transfers between devices  8.21 us (5%)
  Pallas kernels  6.09 us (4%)
  local copies, waits for them, and re-layouts  2.47 us (2%)
    all_gather x1, blocking collectives, per_device(): rows_a = lax.all_gather(short, 'zh', axis=0, tiled=True)  22.9 us
    all_to_all x1, blocking collectives, per_device(): lax.all_to_all(parts, 'y', 0, 0)  20.9 us
    all_gather x1, blocking collectives, per_device(): left = lax.all_gather(piece, ('zh', 'zl', 'c'), axis=0)  19.8 us
    all_to_all x1, blocking collectives, per_device(): lax.all_to_all(product, 'x', 0, 0)  15.4 us
    all_to_all x1, blocking collectives, per_device(): poly = lax.all_to_all(poly, 'y', 0, 0)  15.3 us
    all_to_all x1, blocking collectives, per_device(): right = lax.all_to_all(copies, 'y', 0, 0)  15.1 us
    all_to_all x1, waiting for transfers between devices, per_device(): gathered_x = lax.all_to_all(copies, 'x', 0, 0)  7.62 us
    ppermute x2, starting transfers between devices, other_core(): return lax.ppermute(block, 'c', swap(2, 1))  7.61 us
  transfers between devices with their start and end apart: 5, of which 2 were waited for; matrix products, arithmetic and copies ran while one was open for 1% of the time, Pallas kernels for 0%

profile of v8, /device:TPU:1, one launch (start us, length us, event | category | flops | bytes accessed | tf_op | source)
XLA Modules:
  0.0 148.5 jit_solution(14015275471803886687)
XLA Ops:
  0.0 0.0 copy-start.6
  0.0 1.0 copy-done.6
  1.0 1.2 shard_map.17
  2.2 22.9 %all_gather.9.rows_a_ref = bf16[224,1664]{1,0:T(8,128)(2,1)S(1)} all-gather(bf16[56,1664]{1,0:T(8,128)(2,1)S(1)} %get-tuple-element.17), channel_id=1, replica_groups=mesh['x'=4,'zh'=4,'zl'=2,'c'=2,'y'=8] {'zh'}, dimensions={0}, use_global_device_ids=true | all-gather | bytes 931840 | tf_op jit(solution)/shard_map/all_gather | solution.py:194
  25.1 5.7 %collective-permute-start = (bf16[224,1664]{1,0:T(8,128)(2,1)S(1)}, bf16[224,1664]{1,0:T(8,128)(2,1)S(1)}, u32[]{:S(2)}, u32[]{:S(2)}) collective-permute-start(bf16[224,1664]{1,0:T(8,128)(2,1)S(1)} %all_gather.9.rows_a_ref), channel_id=1, source_target_pairs={{0,16},{16,32},{32,48},{48,64},{64,80},{80,96},{96,112},{112,0},{8... | collective-permute-start | bytes 2236424 | tf_op jit(solution)/shard_map/ppermute | solution.py:30
  30.7 4.0 %all-to-all-start = ((bf16[4,56,1792]{2,1,0:T(8,128)(2,1)}), bf16[4,56,1792]{2,1,0:T(8,128)(2,1)S(1)}, u32[]{:S(2)}, u32[]{:S(2)}) async-start(bf16[4,56,1792]{2,1,0:T(8,128)(2,1)} %get-tuple-element.19), calls=%async_computation | async-start | bytes 1605632 | tf_op jit(solution)/shard_map/all_to_all | solution.py:196
  34.8 3.3 %collective-permute-start.1 = (bf16[224,1664]{1,0:T(8,128)(2,1)S(1)}, bf16[224,1664]{1,0:T(8,128)(2,1)S(1)}, u32[]{:S(2)}, u32[]{:S(2)}) collective-permute-start(bf16[224,1664]{1,0:T(8,128)(2,1)S(1)} %all_gather.9.rows_a_ref), channel_id=1, source_target_pairs={{0,8},{8,0},{1,9},{9,1},{2,10},{10,2},{3,11},{11,3},{4,12},{12,4},... | collective-permute-start | bytes 2236424 | tf_op jit(solution)/shard_map/ppermute | solution.py:34
  38.1 0.1 pad_add_fusion.place_ref
  38.2 7.6 %all-to-all-done = bf16[4,56,1792]{2,1,0:T(8,128)(2,1)S(1)} async-done(((bf16[4,56,1792]{2,1,0:T(8,128)(2,1)}), bf16[4,56,1792]{2,1,0:T(8,128)(2,1)S(1)}, u32[]{:S(2)}, u32[]{:S(2)}) %all-to-all-start) | async-done | bytes 802848 | tf_op jit(solution)/shard_map/all_to_all | solution.py:196
  45.8 0.1 slice.9
  45.9 0.0 collective-permute-done.rows_b_ref
  45.9 0.0 copy-start
  45.9 4.3 %collective-permute-start.2 = (bf16[224,1664]{1,0:T(8,128)(2,1)S(1)}, bf16[224,1664]{1,0:T(8,128)(2,1)S(1)}, u32[]{:S(2)}, u32[]{:S(2)}) collective-permute-start(bf16[224,1664]{1,0:T(8,128)(2,1)S(1)} %collective-permute-done.rows_b_ref), channel_id=1, source_target_pairs={{0,8},{8,0},{1,9},{9,1},{2,10},{10,2},{3,11},{11,3},{4,12},{12,4},... | collective-permute-start | bytes 2236424 | tf_op jit(solution)/shard_map/ppermute | solution.py:34
  50.2 0.4 fusion.part_a_ref
  50.6 0.4 fusion.1.part_b_ref
  51.0 0.0 copy-done
  51.0 0.0 collective-permute-done.1.rows_c_ref
  51.0 0.0 copy-start.2
  51.0 0.4 fusion.2.part_c_ref
  51.4 0.6 collective-permute-done.2.rows_ref.rows_d_ref
  52.0 0.0 copy-start.4
  52.0 1.1 shard_map.18
  53.1 0.0 copy-done.2
  53.1 20.9 %all_to_all.30.shares_ref = bf16[8,200,128]{2,1,0:T(8,128)(2,1)S(1)} all-to-all(bf16[8,200,128]{2,1,0:T(8,128)(2,1)S(1)} %shard_map.18), channel_id=1, replica_groups=mesh['x'=4,'zh'=4,'zl'=2,'c'=2,'y'=8] {'y'}, dimensions={0} | all-to-all | bytes 819200 | tf_op jit(solution)/shard_map/all_to_all | solution.py:219
  74.0 0.0 copy-done.4
  74.0 0.2 shard_map.19
  74.2 15.1 %all_to_all.31 = bf16[8,200,128]{2,1,0:T(8,128)(2,1)S(1)} all-to-all(bf16[8,200,128]{2,1,0:T(8,128)(2,1)S(1)} %get-tuple-element.21), channel_id=1, replica_groups=mesh['x'=4,'zh'=4,'zl'=2,'c'=2,'y'=8] {'y'}, dimensions={0} | all-to-all | bytes 819200 | tf_op jit(solution)/shard_map/all_to_all | solution.py:221
  89.3 1.4 broadcast_in_dim.2
  90.7 3.6 %all-to-all-start.3 = ((bf16[4,8,200,128]{3,2,1,0:T(8,128)(2,1)}), bf16[4,8,200,128]{3,2,1,0:T(8,128)(2,1)S(1)}, u32[]{:S(2)}, u32[]{:S(2)}) async-start(bf16[4,8,200,128]{3,2,1,0:T(8,128)(2,1)} %broadcast_in_dim.2), calls=%async_computation.3 | async-start | bytes 3276800 | tf_op jit(solution)/shard_map/all_to_all | solution.py:224
  94.3 19.8 %all-gather = bf16[3200,128]{1,0:T(8,128)(2,1)S(1)} all-gather(bf16[200,128]{1,0:T(8,128)(2,1)S(1)} %get-tuple-element.23.gram_ref), channel_id=2, replica_groups=mesh['x'=4,'zh'=4,'zl'=2,'c'=2,'y'=8] {'zh','zl','c'}, dimensions={0}, use_global_device_ids=true | all-gather | bytes 870400 | tf_op jit(solution)/shard_map/all_gather | solution.py:225
  114.1 0.0 all-to-all-done.3.right_ref
  114.1 0.0 copy-start.1
  114.1 0.0 copy-start.3
  114.1 0.0 copy-start.5
  114.1 0.9 shard_map.20
  115.1 15.3 %all_to_all.32.poly_ref = bf16[8,200,128]{2,1,0:T(8,128)(2,1)S(1)} all-to-all(bf16[8,200,128]{2,1,0:T(8,128)(2,1)S(1)} %get-tuple-element.25), channel_id=1, replica_groups=mesh['x'=4,'zh'=4,'zl'=2,'c'=2,'y'=8] {'y'}, dimensions={0} | all-to-all | bytes 819200 | tf_op jit(solution)/shard_map/all_to_all | solution.py:233
  130.3 0.0 copy-done.1
  130.3 0.0 copy-done.3
  130.3 0.0 copy-done.5
  130.3 0.0 copy-start.7
  130.3 1.6 %shard_map.21 = (bf16[4,56,1664]{2,1,0:T(8,128)(2,1)S(1)}, f32[56,128]{1,0:T(8,128)S(1)}) custom-call(s32[4]{0:T(128)S(1)} %pad_add_fusion.place_ref, bf16[8,200,128]{2,1,0:T(8,128)(2,1)S(1)} %all_to_all.32.poly_ref, bf16[224,1664]{1,0:T(8,128)(2,1)S(1)} %all_gather.9.rows_a_ref, bf16[224,1664]{1,0:T(8,128)(2,1)S(1)} %copy-done.1, ...), custom_call_target="tpu_custom_call" | custom-call | flops 667942912 | bytes 3000000 | tf_op jit(solution)/shard_map/pallas_call | solution.py:234
  132.0 15.4 %all_to_all.33.product_ref = bf16[4,56,1664]{2,1,0:T(8,128)(2,1)S(1)} all-to-all(bf16[4,56,1664]{2,1,0:T(8,128)(2,1)S(1)} %get-tuple-element.26), channel_id=1, replica_groups=mesh['x'=4,'zh'=4,'zl'=2,'c'=2,'y'=8] {'x'}, dimensions={0} | all-to-all | bytes 1490944 | tf_op jit(solution)/shard_map/all_to_all | solution.py:245
  147.4 0.0 copy-done.7
  147.4 1.1 shard_map.22
  (1 shorter events, 0.0 us)
Async XLA Ops:
  0.0 1.0 copy-start.6
  25.1 20.8 %collective-permute-start = (bf16[224,1664]{1,0:T(8,128)(2,1)S(1)}, bf16[224,1664]{1,0:T(8,128)(2,1)S(1)}, u32[]{:S(2)}, u32[]{:S(2)}) collective-permute-start(bf16[224,1664]{1,0:T(8,128)(2,1)S(1)} %all_gather.9.rows_a_ref), channel_id=1, source_target_pairs={{0,16},{16,32},{32,48},{48,64},{64,80},{80,96},{96,112},{112,0},{8... | collective-permute-start | bytes 2236424 | tf_op jit(solution)/shard_map/ppermute | solution.py:30
  30.7 15.1 %all-to-all-start = ((bf16[4,56,1792]{2,1,0:T(8,128)(2,1)}), bf16[4,56,1792]{2,1,0:T(8,128)(2,1)S(1)}, u32[]{:S(2)}, u32[]{:S(2)}) async-start(bf16[4,56,1792]{2,1,0:T(8,128)(2,1)} %get-tuple-element.19), calls=%async_computation | async-start | bytes 1605632 | tf_op jit(solution)/shard_map/all_to_all | solution.py:196
  34.8 16.2 %collective-permute-start.1 = (bf16[224,1664]{1,0:T(8,128)(2,1)S(1)}, bf16[224,1664]{1,0:T(8,128)(2,1)S(1)}, u32[]{:S(2)}, u32[]{:S(2)}) collective-permute-start(bf16[224,1664]{1,0:T(8,128)(2,1)S(1)} %all_gather.9.rows_a_ref), channel_id=1, source_target_pairs={{0,8},{8,0},{1,9},{9,1},{2,10},{10,2},{3,11},{11,3},{4,12},{12,4},... | collective-permute-start | bytes 2236424 | tf_op jit(solution)/shard_map/ppermute | solution.py:34
  45.9 5.1 %copy-start = (bf16[224,1664]{1,0:T(8,128)(2,1)}, bf16[224,1664]{1,0:T(8,128)(2,1)S(1)}, u32[]{:S(2)}) copy-start(bf16[224,1664]{1,0:T(8,128)(2,1)S(1)} %collective-permute-done.rows_b_ref) | copy-start | bytes 2236420
  45.9 6.1 %collective-permute-start.2 = (bf16[224,1664]{1,0:T(8,128)(2,1)S(1)}, bf16[224,1664]{1,0:T(8,128)(2,1)S(1)}, u32[]{:S(2)}, u32[]{:S(2)}) collective-permute-start(bf16[224,1664]{1,0:T(8,128)(2,1)S(1)} %collective-permute-done.rows_b_ref), channel_id=1, source_target_pairs={{0,8},{8,0},{1,9},{9,1},{2,10},{10,2},{3,11},{11,3},{4,12},{12,4},... | collective-permute-start | bytes 2236424 | tf_op jit(solution)/shard_map/ppermute | solution.py:34
  51.0 2.1 %copy-start.2 = (bf16[224,1664]{1,0:T(8,128)(2,1)}, bf16[224,1664]{1,0:T(8,128)(2,1)S(1)}, u32[]{:S(2)}) copy-start(bf16[224,1664]{1,0:T(8,128)(2,1)S(1)} %collective-permute-done.1.rows_c_ref) | copy-start | bytes 2236420
  52.0 22.0 %copy-start.4 = (bf16[224,1664]{1,0:T(8,128)(2,1)}, bf16[224,1664]{1,0:T(8,128)(2,1)S(1)}, u32[]{:S(2)}) copy-start(bf16[224,1664]{1,0:T(8,128)(2,1)S(1)} %collective-permute-done.2.rows_ref.rows_d_ref) | copy-start | bytes 2236420
  90.7 23.4 %all-to-all-start.3 = ((bf16[4,8,200,128]{3,2,1,0:T(8,128)(2,1)}), bf16[4,8,200,128]{3,2,1,0:T(8,128)(2,1)S(1)}, u32[]{:S(2)}, u32[]{:S(2)}) async-start(bf16[4,8,200,128]{3,2,1,0:T(8,128)(2,1)} %broadcast_in_dim.2), calls=%async_computation.3 | async-start | bytes 3276800 | tf_op jit(solution)/shard_map/all_to_all | solution.py:224
  114.1 16.2 %copy-start.1 = (bf16[224,1664]{1,0:T(8,128)(2,1)S(1)}, bf16[224,1664]{1,0:T(8,128)(2,1)}, u32[]{:S(2)}) copy-start(bf16[224,1664]{1,0:T(8,128)(2,1)} %copy-done) | copy-start | bytes 2236420
  114.1 16.2 %copy-start.3 = (bf16[224,1664]{1,0:T(8,128)(2,1)S(1)}, bf16[224,1664]{1,0:T(8,128)(2,1)}, u32[]{:S(2)}) copy-start(bf16[224,1664]{1,0:T(8,128)(2,1)} %copy-done.2) | copy-start | bytes 2236420
  114.1 16.2 %copy-start.5 = (bf16[224,1664]{1,0:T(8,128)(2,1)S(1)}, bf16[224,1664]{1,0:T(8,128)(2,1)}, u32[]{:S(2)}) copy-start(bf16[224,1664]{1,0:T(8,128)(2,1)} %copy-done.4) | copy-start | bytes 2236420
  130.3 17.1 %copy-start.7 = (f32[56,1664]{1,0:T(8,128)S(1)}, f32[56,1664]{1,0:T(8,128)}, u32[]{:S(2)}) copy-start(f32[56,1664]{1,0:T(8,128)} %momentum_ref.3) | copy-start | bytes 1118212

commit v9 on v8

--- a/solution.py
+++ b/solution.py
@@ -92,22 +92,31 @@
     return jnp.sum(packed[184:192, 96:][:1], axis=1, keepdims=True)
 
 
-def parts_kernel(place_ref, totals_ref, part_a_ref, part_b_ref, part_c_ref, rows_ref, rows_x_ref, parts_ref):
-    zl, first = place_ref[0], place_ref[1] == 0
-    part_d = lax.dot_general(
-        rows_ref[...], rows_x_ref[...], (((1,), (1,)), ((), ())), preferred_element_type=f32
-    )
+def with_other(first, own, other, zh, total):
+    mine, its = own[56 * zh : 56 * zh + 56, :], other[56 * zh : 56 * zh + 56, :]
+    block = jnp.concatenate([jnp.where(first, mine, its), jnp.where(first, its, mine)], axis=0)
+    return pack(block, total).astype(bf16)
+
+
+def same_kernel(place_ref, totals_ref, part_a_ref, part_c_ref, same_ref, total_ref):
     total = jnp.zeros((8, 128), f32)
     for x in range(4):
         total += totals_ref[x].astype(f32)
     total = jnp.sum(total[:1], axis=1, keepdims=True)
-    for own, other, l in ((part_a_ref, part_c_ref, zl), (part_b_ref, part_d, 1 - zl)):
-        for zh in range(4):
-            mine, its = own[56 * zh : 56 * zh + 56, :], other[56 * zh : 56 * zh + 56, :]
-            block = jnp.concatenate(
-                [jnp.where(first, mine, its), jnp.where(first, its, mine)], axis=0
-            )
-            parts_ref[2 * zh + l] = pack(block, total).astype(bf16)
+    total_ref[...] = jnp.broadcast_to(total, (8, 128))
+    for zh in range(4):
+        same_ref[zh] = with_other(place_ref[1] == 0, part_a_ref, part_c_ref, zh, total)
+
+
+def parts_kernel(place_ref, total_ref, same_ref, part_b_ref, rows_ref, rows_x_ref, parts_ref):
+    zl = place_ref[0]
+    part_d = lax.dot_general(
+        rows_ref[...], rows_x_ref[...], (((1,), (1,)), ((), ())), preferred_element_type=f32
+    )
+    total = total_ref[:1, :1]
+    for zh in range(4):
+        parts_ref[2 * zh + zl] = same_ref[zh]
+        parts_ref[2 * zh + 1 - zl] = with_other(place_ref[1] == 0, part_b_ref, part_d, zh, total)
 
 
 def add_shares_kernel(shares_ref, piece_ref, copies_ref):
@@ -199,18 +208,18 @@
     rows_c = other_core(rows_a)
     rows_d = other_core(rows_b)
 
+    same, total = local(
+        same_kernel,
+        [jax.ShapeDtypeStruct((4, 200, 128), bf16), jax.ShapeDtypeStruct((8, 128), f32)],
+        [pltpu.SMEM] + [pltpu.VMEM] * 3,
+        1_000_000,
+    )(place, gathered_x[:, :8, 1664:], rows_dot(rows_a, rows_x), rows_dot(rows_c, rows_x))
     parts = local(
         parts_kernel,
         jax.ShapeDtypeStruct((8, 200, 128), bf16),
-        [pltpu.SMEM] + [pltpu.VMEM] * 6,
+        [pltpu.SMEM] + [pltpu.VMEM] * 5,
         2 * 224 * 224 * 1664,
-    )(
-        place,
-        gathered_x[:, :8, 1664:],
-        *(rows_dot(rows, rows_x) for rows in (rows_a, rows_b, rows_c)),
-        rows_d,
-        rows_x,
-    )
+    )(place, total, same, rows_dot(rows_b, rows_x), rows_d, rows_x)
     piece, copies = local(
         add_shares_kernel,
         [jax.ShapeDtypeStruct((200, 128), bf16), jax.ShapeDtypeStruct((8, 200, 128), bf16)],

time: 151 us -> 152 us (level)
  transfers between devices with their start and end apart: 5 -> 5, of which waited for: 2 -> 1; matrix products, arithmetic and copies ran while one was open for 1% -> 1% of each run, Pallas kernels for 0% -> 0%
where the time goes in v9:
time: 152 us; the launch traced here: 149 us
  blocking collectives  110 us (72%)
  starting transfers between devices  20.9 us (14%)
  waiting for transfers between devices  7.63 us (5%)
  Pallas kernels  6.81 us (4%)
  local copies, waits for them, and re-layouts  2.47 us (2%)
    all_gather x1, blocking collectives, per_device(): rows_a = lax.all_gather(short, 'zh', axis=0, tiled=True)  22.9 us
    all_to_all x1, blocking collectives, per_device(): lax.all_to_all(parts, 'y', 0, 0)  21.2 us
    all_gather x1, blocking collectives, per_device(): left = lax.all_gather(piece, ('zh', 'zl', 'c'), axis=0)  19.1 us
    all_to_all x1, blocking collectives, per_device(): right = lax.all_to_all(copies, 'y', 0, 0)  15.9 us
    all_to_all x1, blocking collectives, per_device(): lax.all_to_all(product, 'x', 0, 0)  15.6 us
    all_to_all x1, blocking collectives, per_device(): poly = lax.all_to_all(poly, 'y', 0, 0)  15.2 us
    all_to_all x1, waiting for transfers between devices, per_device(): gathered_x = lax.all_to_all(copies, 'x', 0, 0)  7.62 us
    ppermute x2, starting transfers between devices, other_core(): return lax.ppermute(block, 'c', swap(2, 1))  7.61 us
  transfers between devices with their start and end apart: 5, of which 1 were waited for; matrix products, arithmetic and copies ran while one was open for 1% of the time, Pallas kernels for 0%

profile of v9, /device:TPU:1, one launch (start us, length us, event | category | flops | bytes accessed | tf_op | source)
XLA Modules:
  0.0 149.1 jit_solution(4308886514389171991)
XLA Ops:
  0.0 0.0 copy-start.6
  0.0 1.0 copy-done.6
  1.0 1.2 shard_map.17
  2.2 22.9 %all_gather.9.rows_a_ref = bf16[224,1664]{1,0:T(8,128)(2,1)S(1)} all-gather(bf16[56,1664]{1,0:T(8,128)(2,1)S(1)} %get-tuple-element.19), channel_id=1, replica_groups=mesh['x'=4,'zh'=4,'zl'=2,'c'=2,'y'=8] {'zh'}, dimensions={0}, use_global_device_ids=true | all-gather | bytes 931840 | tf_op jit(solution)/shard_map/all_gather | solution.py:203
  25.1 5.7 %collective-permute-start.1 = (bf16[224,1664]{1,0:T(8,128)(2,1)S(1)}, bf16[224,1664]{1,0:T(8,128)(2,1)S(1)}, u32[]{:S(2)}, u32[]{:S(2)}) collective-permute-start(bf16[224,1664]{1,0:T(8,128)(2,1)S(1)} %all_gather.9.rows_a_ref), channel_id=1, source_target_pairs={{0,16},{16,32},{32,48},{48,64},{64,80},{80,96},{96,112},{112,0},{8... | collective-permute-start | bytes 2236424 | tf_op jit(solution)/shard_map/ppermute | solution.py:30
  30.7 4.0 %all-to-all-start = ((bf16[4,56,1792]{2,1,0:T(8,128)(2,1)}), bf16[4,56,1792]{2,1,0:T(8,128)(2,1)S(1)}, u32[]{:S(2)}, u32[]{:S(2)}) async-start(bf16[4,56,1792]{2,1,0:T(8,128)(2,1)} %get-tuple-element.21), calls=%async_computation | async-start | bytes 1605632 | tf_op jit(solution)/shard_map/all_to_all | solution.py:205
  34.8 3.3 %collective-permute-start = (bf16[224,1664]{1,0:T(8,128)(2,1)S(1)}, bf16[224,1664]{1,0:T(8,128)(2,1)S(1)}, u32[]{:S(2)}, u32[]{:S(2)}) collective-permute-start(bf16[224,1664]{1,0:T(8,128)(2,1)S(1)} %all_gather.9.rows_a_ref), channel_id=1, source_target_pairs={{0,8},{8,0},{1,9},{9,1},{2,10},{10,2},{3,11},{11,3},{4,12},{12,4},... | collective-permute-start | bytes 2236424 | tf_op jit(solution)/shard_map/ppermute | solution.py:34
  38.1 0.1 pad_add_fusion.place_ref
  38.2 7.6 %all-to-all-done = bf16[4,56,1792]{2,1,0:T(8,128)(2,1)S(1)} async-done(((bf16[4,56,1792]{2,1,0:T(8,128)(2,1)}), bf16[4,56,1792]{2,1,0:T(8,128)(2,1)S(1)}, u32[]{:S(2)}, u32[]{:S(2)}) %all-to-all-start) | async-done | bytes 802848 | tf_op jit(solution)/shard_map/all_to_all | solution.py:205
  45.8 0.1 slice.9
  45.9 0.0 collective-permute-done.1.rows_b_ref
  45.9 0.0 copy-start
  45.9 4.3 %collective-permute-start.2 = (bf16[224,1664]{1,0:T(8,128)(2,1)S(1)}, bf16[224,1664]{1,0:T(8,128)(2,1)S(1)}, u32[]{:S(2)}, u32[]{:S(2)}) collective-permute-start(bf16[224,1664]{1,0:T(8,128)(2,1)S(1)} %collective-permute-done.1.rows_b_ref), channel_id=1, source_target_pairs={{0,8},{8,0},{1,9},{9,1},{2,10},{10,2},{3,11},{11,3},{4,12},{12,4},... | collective-permute-start | bytes 2236424 | tf_op jit(solution)/shard_map/ppermute | solution.py:34
  50.2 0.4 fusion.part_a_ref
  50.6 0.0 collective-permute-done.rows_c_ref
  50.6 0.0 copy-start.2
  50.6 0.4 fusion.1.part_c_ref
  51.0 0.7 shard_map.18
  51.7 0.0 copy-done
  51.7 0.4 fusion.2.part_b_ref
  52.1 0.0 copy-done.2
  52.1 0.0 collective-permute-done.2.rows_ref.rows_d_ref
  52.2 0.0 copy-start.4
  52.2 1.1 shard_map.19
  53.3 21.2 %all_to_all.30.shares_ref = bf16[8,200,128]{2,1,0:T(8,128)(2,1)S(1)} all-to-all(bf16[8,200,128]{2,1,0:T(8,128)(2,1)S(1)} %shard_map.19), channel_id=1, replica_groups=mesh['x'=4,'zh'=4,'zl'=2,'c'=2,'y'=8] {'y'}, dimensions={0} | all-to-all | bytes 819200 | tf_op jit(solution)/shard_map/all_to_all | solution.py:228
  74.5 0.2 shard_map.20
  74.7 0.0 copy-done.4
  74.7 15.9 %all_to_all.31 = bf16[8,200,128]{2,1,0:T(8,128)(2,1)S(1)} all-to-all(bf16[8,200,128]{2,1,0:T(8,128)(2,1)S(1)} %get-tuple-element.25), channel_id=1, replica_groups=mesh['x'=4,'zh'=4,'zl'=2,'c'=2,'y'=8] {'y'}, dimensions={0} | all-to-all | bytes 819200 | tf_op jit(solution)/shard_map/all_to_all | solution.py:230
  90.6 1.4 broadcast_in_dim.2
  91.9 3.6 %all-to-all-start.3 = ((bf16[4,8,200,128]{3,2,1,0:T(8,128)(2,1)}), bf16[4,8,200,128]{3,2,1,0:T(8,128)(2,1)S(1)}, u32[]{:S(2)}, u32[]{:S(2)}) async-start(bf16[4,8,200,128]{3,2,1,0:T(8,128)(2,1)} %broadcast_in_dim.2), calls=%async_computation.3 | async-start | bytes 3276800 | tf_op jit(solution)/shard_map/all_to_all | solution.py:233
  95.5 19.1 %all-gather = bf16[3200,128]{1,0:T(8,128)(2,1)S(1)} all-gather(bf16[200,128]{1,0:T(8,128)(2,1)S(1)} %get-tuple-element.27.gram_ref), channel_id=2, replica_groups=mesh['x'=4,'zh'=4,'zl'=2,'c'=2,'y'=8] {'zh','zl','c'}, dimensions={0}, use_global_device_ids=true | all-gather | bytes 870400 | tf_op jit(solution)/shard_map/all_gather | solution.py:234
  114.6 0.0 all-to-all-done.3.right_ref
  114.6 0.0 copy-start.1
  114.6 0.0 copy-start.3
  114.6 0.0 copy-start.5
  114.6 0.9 shard_map.21
  115.5 15.2 %all_to_all.32.poly_ref = bf16[8,200,128]{2,1,0:T(8,128)(2,1)S(1)} all-to-all(bf16[8,200,128]{2,1,0:T(8,128)(2,1)S(1)} %get-tuple-element.29), channel_id=1, replica_groups=mesh['x'=4,'zh'=4,'zl'=2,'c'=2,'y'=8] {'y'}, dimensions={0} | all-to-all | bytes 819200 | tf_op jit(solution)/shard_map/all_to_all | solution.py:242
  130.7 0.0 copy-done.1
  130.8 0.0 copy-done.3
  130.8 0.0 copy-done.5
  130.8 0.0 copy-start.7
  130.8 1.6 %shard_map.22 = (bf16[4,56,1664]{2,1,0:T(8,128)(2,1)S(1)}, f32[56,128]{1,0:T(8,128)S(1)}) custom-call(s32[4]{0:T(128)S(1)} %pad_add_fusion.place_ref, bf16[8,200,128]{2,1,0:T(8,128)(2,1)S(1)} %all_to_all.32.poly_ref, bf16[224,1664]{1,0:T(8,128)(2,1)S(1)} %all_gather.9.rows_a_ref, bf16[224,1664]{1,0:T(8,128)(2,1)S(1)} %copy-done.1, ...), custom_call_target="tpu_custom_call" | custom-call | flops 667942912 | bytes 3000000 | tf_op jit(solution)/shard_map/pallas_call | solution.py:243
  132.4 15.6 %all_to_all.33.product_ref = bf16[4,56,1664]{2,1,0:T(8,128)(2,1)S(1)} all-to-all(bf16[4,56,1664]{2,1,0:T(8,128)(2,1)S(1)} %get-tuple-element.30), channel_id=1, replica_groups=mesh['x'=4,'zh'=4,'zl'=2,'c'=2,'y'=8] {'x'}, dimensions={0} | all-to-all | bytes 1490944 | tf_op jit(solution)/shard_map/all_to_all | solution.py:254
  148.1 0.0 copy-done.7
  148.1 1.1 shard_map.23
  (1 shorter events, 0.0 us)
Async XLA Ops:
  0.0 1.0 copy-start.6
  25.1 20.8 %collective-permute-start.1 = (bf16[224,1664]{1,0:T(8,128)(2,1)S(1)}, bf16[224,1664]{1,0:T(8,128)(2,1)S(1)}, u32[]{:S(2)}, u32[]{:S(2)}) collective-permute-start(bf16[224,1664]{1,0:T(8,128)(2,1)S(1)} %all_gather.9.rows_a_ref), channel_id=1, source_target_pairs={{0,16},{16,32},{32,48},{48,64},{64,80},{80,96},{96,112},{112,0},{8... | collective-permute-start | bytes 2236424 | tf_op jit(solution)/shard_map/ppermute | solution.py:30
  30.7 15.1 %all-to-all-start = ((bf16[4,56,1792]{2,1,0:T(8,128)(2,1)}), bf16[4,56,1792]{2,1,0:T(8,128)(2,1)S(1)}, u32[]{:S(2)}, u32[]{:S(2)}) async-start(bf16[4,56,1792]{2,1,0:T(8,128)(2,1)} %get-tuple-element.21), calls=%async_computation | async-start | bytes 1605632 | tf_op jit(solution)/shard_map/all_to_all | solution.py:205
  34.8 15.8 %collective-permute-start = (bf16[224,1664]{1,0:T(8,128)(2,1)S(1)}, bf16[224,1664]{1,0:T(8,128)(2,1)S(1)}, u32[]{:S(2)}, u32[]{:S(2)}) collective-permute-start(bf16[224,1664]{1,0:T(8,128)(2,1)S(1)} %all_gather.9.rows_a_ref), channel_id=1, source_target_pairs={{0,8},{8,0},{1,9},{9,1},{2,10},{10,2},{3,11},{11,3},{4,12},{12,4},... | collective-permute-start | bytes 2236424 | tf_op jit(solution)/shard_map/ppermute | solution.py:34
  45.9 5.8 %copy-start = (bf16[224,1664]{1,0:T(8,128)(2,1)}, bf16[224,1664]{1,0:T(8,128)(2,1)S(1)}, u32[]{:S(2)}) copy-start(bf16[224,1664]{1,0:T(8,128)(2,1)S(1)} %collective-permute-done.1.rows_b_ref) | copy-start | bytes 2236420
  45.9 6.2 %collective-permute-start.2 = (bf16[224,1664]{1,0:T(8,128)(2,1)S(1)}, bf16[224,1664]{1,0:T(8,128)(2,1)S(1)}, u32[]{:S(2)}, u32[]{:S(2)}) collective-permute-start(bf16[224,1664]{1,0:T(8,128)(2,1)S(1)} %collective-permute-done.1.rows_b_ref), channel_id=1, source_target_pairs={{0,8},{8,0},{1,9},{9,1},{2,10},{10,2},{3,11},{11,3},{4,12},{12,4},... | collective-permute-start | bytes 2236424 | tf_op jit(solution)/shard_map/ppermute | solution.py:34
  50.6 1.5 %copy-start.2 = (bf16[224,1664]{1,0:T(8,128)(2,1)}, bf16[224,1664]{1,0:T(8,128)(2,1)S(1)}, u32[]{:S(2)}) copy-start(bf16[224,1664]{1,0:T(8,128)(2,1)S(1)} %collective-permute-done.rows_c_ref) | copy-start | bytes 2236420
  52.2 22.5 %copy-start.4 = (bf16[224,1664]{1,0:T(8,128)(2,1)}, bf16[224,1664]{1,0:T(8,128)(2,1)S(1)}, u32[]{:S(2)}) copy-start(bf16[224,1664]{1,0:T(8,128)(2,1)S(1)} %collective-permute-done.2.rows_ref.rows_d_ref) | copy-start | bytes 2236420
  91.9 22.7 %all-to-all-start.3 = ((bf16[4,8,200,128]{3,2,1,0:T(8,128)(2,1)}), bf16[4,8,200,128]{3,2,1,0:T(8,128)(2,1)S(1)}, u32[]{:S(2)}, u32[]{:S(2)}) async-start(bf16[4,8,200,128]{3,2,1,0:T(8,128)(2,1)} %broadcast_in_dim.2), calls=%async_computation.3 | async-start | bytes 3276800 | tf_op jit(solution)/shard_map/all_to_all | solution.py:233
  114.6 16.1 %copy-start.1 = (bf16[224,1664]{1,0:T(8,128)(2,1)S(1)}, bf16[224,1664]{1,0:T(8,128)(2,1)}, u32[]{:S(2)}) copy-start(bf16[224,1664]{1,0:T(8,128)(2,1)} %copy-done) | copy-start | bytes 2236420
  114.6 16.1 %copy-start.3 = (bf16[224,1664]{1,0:T(8,128)(2,1)S(1)}, bf16[224,1664]{1,0:T(8,128)(2,1)}, u32[]{:S(2)}) copy-start(bf16[224,1664]{1,0:T(8,128)(2,1)} %copy-done.2) | copy-start | bytes 2236420
  114.6 16.1 %copy-start.5 = (bf16[224,1664]{1,0:T(8,128)(2,1)S(1)}, bf16[224,1664]{1,0:T(8,128)(2,1)}, u32[]{:S(2)}) copy-start(bf16[224,1664]{1,0:T(8,128)(2,1)} %copy-done.4) | copy-start | bytes 2236420
  130.8 17.3 %copy-start.7 = (f32[56,1664]{1,0:T(8,128)S(1)}, f32[56,1664]{1,0:T(8,128)}, u32[]{:S(2)}) copy-start(f32[56,1664]{1,0:T(8,128)} %momentum_ref.3) | copy-start | bytes 1118212

commit v10 on v8

--- a/solution.py
+++ b/solution.py
@@ -222,7 +222,7 @@
     right, piece = lax.optimization_barrier((right, piece))
     copies = jnp.broadcast_to(right[None], (4, *right.shape))
     right = lax.all_to_all(copies, "x", 0, 0)
-    left = lax.all_gather(piece, ("zh", "zl", "c"), axis=0)
+    left = lax.all_gather(piece, ("zh", "zl", "c"), axis=0, tiled=True).reshape(16, 200, 128)
     poly, factor = local(
         polynomial_kernel,
         [jax.ShapeDtypeStruct((8, 200, 128), bf16), jax.ShapeDtypeStruct((8, 128), f32)],

time: 151 us -> 151 us (level)
  no operation moved by 1% of the time
where the time goes in v10:
time: 151 us; the launch traced here: 148 us
  blocking collectives  109 us (72%)
  starting transfers between devices  20.9 us (14%)
  waiting for transfers between devices  8.21 us (5%)
  Pallas kernels  6.09 us (4%)
  local copies, waits for them, and re-layouts  2.47 us (2%)
    all_gather x1, blocking collectives, per_device(): rows_a = lax.all_gather(short, 'zh', axis=0, tiled=True)  22.9 us
    all_to_all x1, blocking collectives, per_device(): lax.all_to_all(parts, 'y', 0, 0)  20.9 us
    all_gather x1, blocking collectives, per_device(): lax.all_gather(piece, ('zh', 'zl', 'c'), axis=0, tiled=True)  19.8 us
    all_to_all x1, blocking collectives, per_device(): lax.all_to_all(product, 'x', 0, 0)  15.4 us
    all_to_all x1, blocking collectives, per_device(): poly = lax.all_to_all(poly, 'y', 0, 0)  15.3 us
    all_to_all x1, blocking collectives, per_device(): right = lax.all_to_all(copies, 'y', 0, 0)  15.1 us
    all_to_all x1, waiting for transfers between devices, per_device(): gathered_x = lax.all_to_all(copies, 'x', 0, 0)  7.62 us
    ppermute x2, starting transfers between devices, other_core(): return lax.ppermute(block, 'c', swap(2, 1))  7.61 us
  transfers between devices with their start and end apart: 5, of which 2 were waited for; matrix products, arithmetic and copies ran while one was open for 1% of the time, Pallas kernels for 0%

profile of v10, /device:TPU:1, one launch (start us, length us, event | category | flops | bytes accessed | tf_op | source)
XLA Modules:
  0.0 148.5 jit_solution(14015275471803886687)
XLA Ops:
  0.0 0.0 copy-start.6
  0.0 1.0 copy-done.6
  1.0 1.2 shard_map.17
  2.2 22.9 %all_gather.6.rows_a_ref = bf16[224,1664]{1,0:T(8,128)(2,1)S(1)} all-gather(bf16[56,1664]{1,0:T(8,128)(2,1)S(1)} %get-tuple-element.17), channel_id=1, replica_groups=mesh['x'=4,'zh'=4,'zl'=2,'c'=2,'y'=8] {'zh'}, dimensions={0}, use_global_device_ids=true | all-gather | bytes 931840 | tf_op jit(solution)/shard_map/all_gather | solution.py:194
  25.1 5.7 %collective-permute-start = (bf16[224,1664]{1,0:T(8,128)(2,1)S(1)}, bf16[224,1664]{1,0:T(8,128)(2,1)S(1)}, u32[]{:S(2)}, u32[]{:S(2)}) collective-permute-start(bf16[224,1664]{1,0:T(8,128)(2,1)S(1)} %all_gather.6.rows_a_ref), channel_id=1, source_target_pairs={{0,16},{16,32},{32,48},{48,64},{64,80},{80,96},{96,112},{112,0},{8... | collective-permute-start | bytes 2236424 | tf_op jit(solution)/shard_map/ppermute | solution.py:30
  30.7 4.0 %all-to-all-start = ((bf16[4,56,1792]{2,1,0:T(8,128)(2,1)}), bf16[4,56,1792]{2,1,0:T(8,128)(2,1)S(1)}, u32[]{:S(2)}, u32[]{:S(2)}) async-start(bf16[4,56,1792]{2,1,0:T(8,128)(2,1)} %get-tuple-element.19), calls=%async_computation | async-start | bytes 1605632 | tf_op jit(solution)/shard_map/all_to_all | solution.py:196
  34.8 3.3 %collective-permute-start.1 = (bf16[224,1664]{1,0:T(8,128)(2,1)S(1)}, bf16[224,1664]{1,0:T(8,128)(2,1)S(1)}, u32[]{:S(2)}, u32[]{:S(2)}) collective-permute-start(bf16[224,1664]{1,0:T(8,128)(2,1)S(1)} %all_gather.6.rows_a_ref), channel_id=1, source_target_pairs={{0,8},{8,0},{1,9},{9,1},{2,10},{10,2},{3,11},{11,3},{4,12},{12,4},... | collective-permute-start | bytes 2236424 | tf_op jit(solution)/shard_map/ppermute | solution.py:34
  38.1 0.1 pad_add_fusion.place_ref
  38.2 7.6 %all-to-all-done = bf16[4,56,1792]{2,1,0:T(8,128)(2,1)S(1)} async-done(((bf16[4,56,1792]{2,1,0:T(8,128)(2,1)}), bf16[4,56,1792]{2,1,0:T(8,128)(2,1)S(1)}, u32[]{:S(2)}, u32[]{:S(2)}) %all-to-all-start) | async-done | bytes 802848 | tf_op jit(solution)/shard_map/all_to_all | solution.py:196
  45.8 0.1 slice.9
  45.9 0.0 collective-permute-done.rows_b_ref
  45.9 0.0 copy-start
  45.9 4.3 %collective-permute-start.2 = (bf16[224,1664]{1,0:T(8,128)(2,1)S(1)}, bf16[224,1664]{1,0:T(8,128)(2,1)S(1)}, u32[]{:S(2)}, u32[]{:S(2)}) collective-permute-start(bf16[224,1664]{1,0:T(8,128)(2,1)S(1)} %collective-permute-done.rows_b_ref), channel_id=1, source_target_pairs={{0,8},{8,0},{1,9},{9,1},{2,10},{10,2},{3,11},{11,3},{4,12},{12,4},... | collective-permute-start | bytes 2236424 | tf_op jit(solution)/shard_map/ppermute | solution.py:34
  50.2 0.4 fusion.part_a_ref
  50.6 0.4 fusion.1.part_b_ref
  51.0 0.0 copy-done
  51.0 0.0 collective-permute-done.1.rows_c_ref
  51.0 0.0 copy-start.2
  51.0 0.4 fusion.2.part_c_ref
  51.4 0.6 collective-permute-done.2.rows_ref.rows_d_ref
  52.0 0.0 copy-start.4
  52.0 1.1 shard_map.18
  53.1 0.0 copy-done.2
  53.1 20.9 %all_to_all.30.shares_ref = bf16[8,200,128]{2,1,0:T(8,128)(2,1)S(1)} all-to-all(bf16[8,200,128]{2,1,0:T(8,128)(2,1)S(1)} %shard_map.18), channel_id=1, replica_groups=mesh['x'=4,'zh'=4,'zl'=2,'c'=2,'y'=8] {'y'}, dimensions={0} | all-to-all | bytes 819200 | tf_op jit(solution)/shard_map/all_to_all | solution.py:219
  74.0 0.0 copy-done.4
  74.0 0.2 shard_map.19
  74.2 15.1 %all_to_all.31 = bf16[8,200,128]{2,1,0:T(8,128)(2,1)S(1)} all-to-all(bf16[8,200,128]{2,1,0:T(8,128)(2,1)S(1)} %get-tuple-element.21), channel_id=1, replica_groups=mesh['x'=4,'zh'=4,'zl'=2,'c'=2,'y'=8] {'y'}, dimensions={0} | all-to-all | bytes 819200 | tf_op jit(solution)/shard_map/all_to_all | solution.py:221
  89.3 1.4 broadcast_in_dim.2
  90.7 3.6 %all-to-all-start.3 = ((bf16[4,8,200,128]{3,2,1,0:T(8,128)(2,1)}), bf16[4,8,200,128]{3,2,1,0:T(8,128)(2,1)S(1)}, u32[]{:S(2)}, u32[]{:S(2)}) async-start(bf16[4,8,200,128]{3,2,1,0:T(8,128)(2,1)} %broadcast_in_dim.2), calls=%async_computation.3 | async-start | bytes 3276800 | tf_op jit(solution)/shard_map/all_to_all | solution.py:224
  94.3 19.8 %all_gather.7 = bf16[3200,128]{1,0:T(8,128)(2,1)S(1)} all-gather(bf16[200,128]{1,0:T(8,128)(2,1)S(1)} %get-tuple-element.23.gram_ref), channel_id=1, replica_groups=mesh['x'=4,'zh'=4,'zl'=2,'c'=2,'y'=8] {'zh','zl','c'}, dimensions={0}, use_global_device_ids=true | all-gather | bytes 870400 | tf_op jit(solution)/shard_map/all_gather | solution.py:225
  114.1 0.0 all-to-all-done.3.right_ref
  114.1 0.0 copy-start.1
  114.1 0.0 copy-start.3
  114.1 0.0 copy-start.5
  114.1 0.9 shard_map.20
  115.1 15.3 %all_to_all.32.poly_ref = bf16[8,200,128]{2,1,0:T(8,128)(2,1)S(1)} all-to-all(bf16[8,200,128]{2,1,0:T(8,128)(2,1)S(1)} %get-tuple-element.25), channel_id=1, replica_groups=mesh['x'=4,'zh'=4,'zl'=2,'c'=2,'y'=8] {'y'}, dimensions={0} | all-to-all | bytes 819200 | tf_op jit(solution)/shard_map/all_to_all | solution.py:233
  130.3 0.0 copy-done.1
  130.3 0.0 copy-done.3
  130.3 0.0 copy-done.5
  130.3 0.0 copy-start.7
  130.3 1.6 %shard_map.21 = (bf16[4,56,1664]{2,1,0:T(8,128)(2,1)S(1)}, f32[56,128]{1,0:T(8,128)S(1)}) custom-call(s32[4]{0:T(128)S(1)} %pad_add_fusion.place_ref, bf16[8,200,128]{2,1,0:T(8,128)(2,1)S(1)} %all_to_all.32.poly_ref, bf16[224,1664]{1,0:T(8,128)(2,1)S(1)} %all_gather.6.rows_a_ref, bf16[224,1664]{1,0:T(8,128)(2,1)S(1)} %copy-done.1, ...), custom_call_target="tpu_custom_call" | custom-call | flops 667942912 | bytes 3000000 | tf_op jit(solution)/shard_map/pallas_call | solution.py:234
  132.0 15.4 %all_to_all.33.product_ref = bf16[4,56,1664]{2,1,0:T(8,128)(2,1)S(1)} all-to-all(bf16[4,56,1664]{2,1,0:T(8,128)(2,1)S(1)} %get-tuple-element.26), channel_id=1, replica_groups=mesh['x'=4,'zh'=4,'zl'=2,'c'=2,'y'=8] {'x'}, dimensions={0} | all-to-all | bytes 1490944 | tf_op jit(solution)/shard_map/all_to_all | solution.py:245
  147.4 0.0 copy-done.7
  147.4 1.1 shard_map.22
  (1 shorter events, 0.0 us)
Async XLA Ops:
  0.0 1.0 copy-start.6
  25.1 20.8 %collective-permute-start = (bf16[224,1664]{1,0:T(8,128)(2,1)S(1)}, bf16[224,1664]{1,0:T(8,128)(2,1)S(1)}, u32[]{:S(2)}, u32[]{:S(2)}) collective-permute-start(bf16[224,1664]{1,0:T(8,128)(2,1)S(1)} %all_gather.6.rows_a_ref), channel_id=1, source_target_pairs={{0,16},{16,32},{32,48},{48,64},{64,80},{80,96},{96,112},{112,0},{8... | collective-permute-start | bytes 2236424 | tf_op jit(solution)/shard_map/ppermute | solution.py:30
  30.7 15.1 %all-to-all-start = ((bf16[4,56,1792]{2,1,0:T(8,128)(2,1)}), bf16[4,56,1792]{2,1,0:T(8,128)(2,1)S(1)}, u32[]{:S(2)}, u32[]{:S(2)}) async-start(bf16[4,56,1792]{2,1,0:T(8,128)(2,1)} %get-tuple-element.19), calls=%async_computation | async-start | bytes 1605632 | tf_op jit(solution)/shard_map/all_to_all | solution.py:196
  34.8 16.2 %collective-permute-start.1 = (bf16[224,1664]{1,0:T(8,128)(2,1)S(1)}, bf16[224,1664]{1,0:T(8,128)(2,1)S(1)}, u32[]{:S(2)}, u32[]{:S(2)}) collective-permute-start(bf16[224,1664]{1,0:T(8,128)(2,1)S(1)} %all_gather.6.rows_a_ref), channel_id=1, source_target_pairs={{0,8},{8,0},{1,9},{9,1},{2,10},{10,2},{3,11},{11,3},{4,12},{12,4},... | collective-permute-start | bytes 2236424 | tf_op jit(solution)/shard_map/ppermute | solution.py:34
  45.9 5.1 %copy-start = (bf16[224,1664]{1,0:T(8,128)(2,1)}, bf16[224,1664]{1,0:T(8,128)(2,1)S(1)}, u32[]{:S(2)}) copy-start(bf16[224,1664]{1,0:T(8,128)(2,1)S(1)} %collective-permute-done.rows_b_ref) | copy-start | bytes 2236420
  45.9 6.1 %collective-permute-start.2 = (bf16[224,1664]{1,0:T(8,128)(2,1)S(1)}, bf16[224,1664]{1,0:T(8,128)(2,1)S(1)}, u32[]{:S(2)}, u32[]{:S(2)}) collective-permute-start(bf16[224,1664]{1,0:T(8,128)(2,1)S(1)} %collective-permute-done.rows_b_ref), channel_id=1, source_target_pairs={{0,8},{8,0},{1,9},{9,1},{2,10},{10,2},{3,11},{11,3},{4,12},{12,4},... | collective-permute-start | bytes 2236424 | tf_op jit(solution)/shard_map/ppermute | solution.py:34
  51.0 2.1 %copy-start.2 = (bf16[224,1664]{1,0:T(8,128)(2,1)}, bf16[224,1664]{1,0:T(8,128)(2,1)S(1)}, u32[]{:S(2)}) copy-start(bf16[224,1664]{1,0:T(8,128)(2,1)S(1)} %collective-permute-done.1.rows_c_ref) | copy-start | bytes 2236420
  52.0 22.0 %copy-start.4 = (bf16[224,1664]{1,0:T(8,128)(2,1)}, bf16[224,1664]{1,0:T(8,128)(2,1)S(1)}, u32[]{:S(2)}) copy-start(bf16[224,1664]{1,0:T(8,128)(2,1)S(1)} %collective-permute-done.2.rows_ref.rows_d_ref) | copy-start | bytes 2236420
  90.7 23.4 %all-to-all-start.3 = ((bf16[4,8,200,128]{3,2,1,0:T(8,128)(2,1)}), bf16[4,8,200,128]{3,2,1,0:T(8,128)(2,1)S(1)}, u32[]{:S(2)}, u32[]{:S(2)}) async-start(bf16[4,8,200,128]{3,2,1,0:T(8,128)(2,1)} %broadcast_in_dim.2), calls=%async_computation.3 | async-start | bytes 3276800 | tf_op jit(solution)/shard_map/all_to_all | solution.py:224
  114.1 16.2 %copy-start.1 = (bf16[224,1664]{1,0:T(8,128)(2,1)S(1)}, bf16[224,1664]{1,0:T(8,128)(2,1)}, u32[]{:S(2)}) copy-start(bf16[224,1664]{1,0:T(8,128)(2,1)} %copy-done) | copy-start | bytes 2236420
  114.1 16.2 %copy-start.3 = (bf16[224,1664]{1,0:T(8,128)(2,1)S(1)}, bf16[224,1664]{1,0:T(8,128)(2,1)}, u32[]{:S(2)}) copy-start(bf16[224,1664]{1,0:T(8,128)(2,1)} %copy-done.2) | copy-start | bytes 2236420
  114.1 16.2 %copy-start.5 = (bf16[224,1664]{1,0:T(8,128)(2,1)S(1)}, bf16[224,1664]{1,0:T(8,128)(2,1)}, u32[]{:S(2)}) copy-start(bf16[224,1664]{1,0:T(8,128)(2,1)} %copy-done.4) | copy-start | bytes 2236420
  130.3 17.1 %copy-start.7 = (f32[56,1664]{1,0:T(8,128)S(1)}, f32[56,1664]{1,0:T(8,128)}, u32[]{:S(2)}) copy-start(f32[56,1664]{1,0:T(8,128)} %momentum_ref.3) | copy-start | bytes 1118212

commit v11 on v8

--- a/solution.py
+++ b/solution.py
@@ -126,13 +126,13 @@
     square = jnp.zeros((112, 224), f32)
     total = jnp.zeros((1, 1), f32)
     for z in range(8):
-        rights = [unpack(right_ref[x, z].astype(f32)) for x in range(4)]
+        rights = [unpack(right_ref[x, z]) for x in range(4)]
         for c in range(2):
             left = left_ref[2 * z + c].astype(f32)
             total += packed_total(left)
             right = jnp.concatenate([block[56 * c : 56 * c + 56] for block in rights], axis=0)
             square += jnp.dot(
-                unpack(left).astype(bf16), right.astype(bf16), preferred_element_type=f32
+                unpack(left).astype(bf16), right, preferred_element_type=f32
             )
     factor = math.sqrt(M) / 3.0 / (jnp.sqrt(total) + 1e-07)
     factor2 = (factor / lift) * (factor / lift)

time: 151 us -> 151 us (level)
  no operation moved by 1% of the time
where the time goes in v11:
time: 151 us; the launch traced here: 149 us
  blocking collectives  109 us (72%)
  starting transfers between devices  20.9 us (14%)
  waiting for transfers between devices  8.21 us (5%)
  Pallas kernels  6.07 us (4%)
  local copies, waits for them, and re-layouts  2.47 us (2%)
    all_gather x1, blocking collectives, per_device(): rows_a = lax.all_gather(short, 'zh', axis=0, tiled=True)  22.9 us
    all_to_all x1, blocking collectives, per_device(): lax.all_to_all(parts, 'y', 0, 0)  20.9 us
    all_gather x1, blocking collectives, per_device(): left = lax.all_gather(piece, ('zh', 'zl', 'c'), axis=0)  19.8 us
    all_to_all x1, blocking collectives, per_device(): lax.all_to_all(product, 'x', 0, 0)  15.4 us
    all_to_all x1, blocking collectives, per_device(): poly = lax.all_to_all(poly, 'y', 0, 0)  15.3 us
    all_to_all x1, blocking collectives, per_device(): right = lax.all_to_all(copies, 'y', 0, 0)  15.1 us
    all_to_all x1, waiting for transfers between devices, per_device(): gathered_x = lax.all_to_all(copies, 'x', 0, 0)  7.62 us
    ppermute x2, starting transfers between devices, other_core(): return lax.ppermute(block, 'c', swap(2, 1))  7.61 us
  transfers between devices with their start and end apart: 5, of which 2 were waited for; matrix products, arithmetic and copies ran while one was open for 1% of the time, Pallas kernels for 0%

profile of v11, /device:TPU:1, one launch (start us, length us, event | category | flops | bytes accessed | tf_op | source)
XLA Modules:
  0.0 148.5 jit_solution(1424416748903014558)
XLA Ops:
  0.0 0.0 copy-start.6
  0.0 1.0 copy-done.6
  1.0 1.2 shard_map.17
  2.2 22.9 %all_gather.9.rows_a_ref = bf16[224,1664]{1,0:T(8,128)(2,1)S(1)} all-gather(bf16[56,1664]{1,0:T(8,128)(2,1)S(1)} %get-tuple-element.17), channel_id=1, replica_groups=mesh['x'=4,'zh'=4,'zl'=2,'c'=2,'y'=8] {'zh'}, dimensions={0}, use_global_device_ids=true | all-gather | bytes 931840 | tf_op jit(solution)/shard_map/all_gather | solution.py:194
  25.1 5.7 %collective-permute-start = (bf16[224,1664]{1,0:T(8,128)(2,1)S(1)}, bf16[224,1664]{1,0:T(8,128)(2,1)S(1)}, u32[]{:S(2)}, u32[]{:S(2)}) collective-permute-start(bf16[224,1664]{1,0:T(8,128)(2,1)S(1)} %all_gather.9.rows_a_ref), channel_id=1, source_target_pairs={{0,16},{16,32},{32,48},{48,64},{64,80},{80,96},{96,112},{112,0},{8... | collective-permute-start | bytes 2236424 | tf_op jit(solution)/shard_map/ppermute | solution.py:30
  30.7 4.0 %all-to-all-start = ((bf16[4,56,1792]{2,1,0:T(8,128)(2,1)}), bf16[4,56,1792]{2,1,0:T(8,128)(2,1)S(1)}, u32[]{:S(2)}, u32[]{:S(2)}) async-start(bf16[4,56,1792]{2,1,0:T(8,128)(2,1)} %get-tuple-element.19), calls=%async_computation | async-start | bytes 1605632 | tf_op jit(solution)/shard_map/all_to_all | solution.py:196
  34.8 3.3 %collective-permute-start.1 = (bf16[224,1664]{1,0:T(8,128)(2,1)S(1)}, bf16[224,1664]{1,0:T(8,128)(2,1)S(1)}, u32[]{:S(2)}, u32[]{:S(2)}) collective-permute-start(bf16[224,1664]{1,0:T(8,128)(2,1)S(1)} %all_gather.9.rows_a_ref), channel_id=1, source_target_pairs={{0,8},{8,0},{1,9},{9,1},{2,10},{10,2},{3,11},{11,3},{4,12},{12,4},... | collective-permute-start | bytes 2236424 | tf_op jit(solution)/shard_map/ppermute | solution.py:34
  38.1 0.1 pad_add_fusion.place_ref
  38.2 7.6 %all-to-all-done = bf16[4,56,1792]{2,1,0:T(8,128)(2,1)S(1)} async-done(((bf16[4,56,1792]{2,1,0:T(8,128)(2,1)}), bf16[4,56,1792]{2,1,0:T(8,128)(2,1)S(1)}, u32[]{:S(2)}, u32[]{:S(2)}) %all-to-all-start) | async-done | bytes 802848 | tf_op jit(solution)/shard_map/all_to_all | solution.py:196
  45.8 0.1 slice.9
  45.9 0.0 collective-permute-done.rows_b_ref
  45.9 0.0 copy-start
  45.9 4.3 %collective-permute-start.2 = (bf16[224,1664]{1,0:T(8,128)(2,1)S(1)}, bf16[224,1664]{1,0:T(8,128)(2,1)S(1)}, u32[]{:S(2)}, u32[]{:S(2)}) collective-permute-start(bf16[224,1664]{1,0:T(8,128)(2,1)S(1)} %collective-permute-done.rows_b_ref), channel_id=1, source_target_pairs={{0,8},{8,0},{1,9},{9,1},{2,10},{10,2},{3,11},{11,3},{4,12},{12,4},... | collective-permute-start | bytes 2236424 | tf_op jit(solution)/shard_map/ppermute | solution.py:34
  50.2 0.4 fusion.part_a_ref
  50.6 0.4 fusion.1.part_b_ref
  51.0 0.0 copy-done
  51.0 0.0 collective-permute-done.1.rows_c_ref
  51.0 0.0 copy-start.2
  51.0 0.4 fusion.2.part_c_ref
  51.4 0.6 collective-permute-done.2.rows_ref.rows_d_ref
  52.0 0.0 copy-start.4
  52.0 1.1 shard_map.18
  53.1 0.0 copy-done.2
  53.1 20.9 %all_to_all.30.shares_ref = bf16[8,200,128]{2,1,0:T(8,128)(2,1)S(1)} all-to-all(bf16[8,200,128]{2,1,0:T(8,128)(2,1)S(1)} %shard_map.18), channel_id=1, replica_groups=mesh['x'=4,'zh'=4,'zl'=2,'c'=2,'y'=8] {'y'}, dimensions={0} | all-to-all | bytes 819200 | tf_op jit(solution)/shard_map/all_to_all | solution.py:219
  74.0 0.0 copy-done.4
  74.0 0.2 shard_map.19
  74.2 15.1 %all_to_all.31 = bf16[8,200,128]{2,1,0:T(8,128)(2,1)S(1)} all-to-all(bf16[8,200,128]{2,1,0:T(8,128)(2,1)S(1)} %get-tuple-element.21), channel_id=1, replica_groups=mesh['x'=4,'zh'=4,'zl'=2,'c'=2,'y'=8] {'y'}, dimensions={0} | all-to-all | bytes 819200 | tf_op jit(solution)/shard_map/all_to_all | solution.py:221
  89.3 1.4 broadcast_in_dim.2
  90.7 3.6 %all-to-all-start.3 = ((bf16[4,8,200,128]{3,2,1,0:T(8,128)(2,1)}), bf16[4,8,200,128]{3,2,1,0:T(8,128)(2,1)S(1)}, u32[]{:S(2)}, u32[]{:S(2)}) async-start(bf16[4,8,200,128]{3,2,1,0:T(8,128)(2,1)} %broadcast_in_dim.2), calls=%async_computation.3 | async-start | bytes 3276800 | tf_op jit(solution)/shard_map/all_to_all | solution.py:224
  94.3 19.8 %all-gather = bf16[3200,128]{1,0:T(8,128)(2,1)S(1)} all-gather(bf16[200,128]{1,0:T(8,128)(2,1)S(1)} %get-tuple-element.23.gram_ref), channel_id=2, replica_groups=mesh['x'=4,'zh'=4,'zl'=2,'c'=2,'y'=8] {'zh','zl','c'}, dimensions={0}, use_global_device_ids=true | all-gather | bytes 870400 | tf_op jit(solution)/shard_map/all_gather | solution.py:225
  114.1 0.0 all-to-all-done.3.right_ref
  114.1 0.0 copy-start.1
  114.1 0.0 copy-start.3
  114.1 0.0 copy-start.5
  114.1 0.9 shard_map.20
  115.0 15.3 %all_to_all.32.poly_ref = bf16[8,200,128]{2,1,0:T(8,128)(2,1)S(1)} all-to-all(bf16[8,200,128]{2,1,0:T(8,128)(2,1)S(1)} %get-tuple-element.25), channel_id=1, replica_groups=mesh['x'=4,'zh'=4,'zl'=2,'c'=2,'y'=8] {'y'}, dimensions={0} | all-to-all | bytes 819200 | tf_op jit(solution)/shard_map/all_to_all | solution.py:233
  130.3 0.0 copy-done.1
  130.3 0.0 copy-done.3
  130.3 0.0 copy-done.5
  130.3 0.0 copy-start.7
  130.3 1.6 %shard_map.21 = (bf16[4,56,1664]{2,1,0:T(8,128)(2,1)S(1)}, f32[56,128]{1,0:T(8,128)S(1)}) custom-call(s32[4]{0:T(128)S(1)} %pad_add_fusion.place_ref, bf16[8,200,128]{2,1,0:T(8,128)(2,1)S(1)} %all_to_all.32.poly_ref, bf16[224,1664]{1,0:T(8,128)(2,1)S(1)} %all_gather.9.rows_a_ref, bf16[224,1664]{1,0:T(8,128)(2,1)S(1)} %copy-done.1, ...), custom_call_target="tpu_custom_call" | custom-call | flops 667942912 | bytes 3000000 | tf_op jit(solution)/shard_map/pallas_call | solution.py:234
  132.0 15.4 %all_to_all.33.product_ref = bf16[4,56,1664]{2,1,0:T(8,128)(2,1)S(1)} all-to-all(bf16[4,56,1664]{2,1,0:T(8,128)(2,1)S(1)} %get-tuple-element.26), channel_id=1, replica_groups=mesh['x'=4,'zh'=4,'zl'=2,'c'=2,'y'=8] {'x'}, dimensions={0} | all-to-all | bytes 1490944 | tf_op jit(solution)/shard_map/all_to_all | solution.py:245
  147.4 0.0 copy-done.7
  147.4 1.1 shard_map.22
  (1 shorter events, 0.0 us)
Async XLA Ops:
  0.0 1.0 copy-start.6
  25.1 20.8 %collective-permute-start = (bf16[224,1664]{1,0:T(8,128)(2,1)S(1)}, bf16[224,1664]{1,0:T(8,128)(2,1)S(1)}, u32[]{:S(2)}, u32[]{:S(2)}) collective-permute-start(bf16[224,1664]{1,0:T(8,128)(2,1)S(1)} %all_gather.9.rows_a_ref), channel_id=1, source_target_pairs={{0,16},{16,32},{32,48},{48,64},{64,80},{80,96},{96,112},{112,0},{8... | collective-permute-start | bytes 2236424 | tf_op jit(solution)/shard_map/ppermute | solution.py:30
  30.7 15.1 %all-to-all-start = ((bf16[4,56,1792]{2,1,0:T(8,128)(2,1)}), bf16[4,56,1792]{2,1,0:T(8,128)(2,1)S(1)}, u32[]{:S(2)}, u32[]{:S(2)}) async-start(bf16[4,56,1792]{2,1,0:T(8,128)(2,1)} %get-tuple-element.19), calls=%async_computation | async-start | bytes 1605632 | tf_op jit(solution)/shard_map/all_to_all | solution.py:196
  34.8 16.2 %collective-permute-start.1 = (bf16[224,1664]{1,0:T(8,128)(2,1)S(1)}, bf16[224,1664]{1,0:T(8,128)(2,1)S(1)}, u32[]{:S(2)}, u32[]{:S(2)}) collective-permute-start(bf16[224,1664]{1,0:T(8,128)(2,1)S(1)} %all_gather.9.rows_a_ref), channel_id=1, source_target_pairs={{0,8},{8,0},{1,9},{9,1},{2,10},{10,2},{3,11},{11,3},{4,12},{12,4},... | collective-permute-start | bytes 2236424 | tf_op jit(solution)/shard_map/ppermute | solution.py:34
  45.9 5.1 %copy-start = (bf16[224,1664]{1,0:T(8,128)(2,1)}, bf16[224,1664]{1,0:T(8,128)(2,1)S(1)}, u32[]{:S(2)}) copy-start(bf16[224,1664]{1,0:T(8,128)(2,1)S(1)} %collective-permute-done.rows_b_ref) | copy-start | bytes 2236420
  45.9 6.1 %collective-permute-start.2 = (bf16[224,1664]{1,0:T(8,128)(2,1)S(1)}, bf16[224,1664]{1,0:T(8,128)(2,1)S(1)}, u32[]{:S(2)}, u32[]{:S(2)}) collective-permute-start(bf16[224,1664]{1,0:T(8,128)(2,1)S(1)} %collective-permute-done.rows_b_ref), channel_id=1, source_target_pairs={{0,8},{8,0},{1,9},{9,1},{2,10},{10,2},{3,11},{11,3},{4,12},{12,4},... | collective-permute-start | bytes 2236424 | tf_op jit(solution)/shard_map/ppermute | solution.py:34
  51.0 2.1 %copy-start.2 = (bf16[224,1664]{1,0:T(8,128)(2,1)}, bf16[224,1664]{1,0:T(8,128)(2,1)S(1)}, u32[]{:S(2)}) copy-start(bf16[224,1664]{1,0:T(8,128)(2,1)S(1)} %collective-permute-done.1.rows_c_ref) | copy-start | bytes 2236420
  52.0 22.0 %copy-start.4 = (bf16[224,1664]{1,0:T(8,128)(2,1)}, bf16[224,1664]{1,0:T(8,128)(2,1)S(1)}, u32[]{:S(2)}) copy-start(bf16[224,1664]{1,0:T(8,128)(2,1)S(1)} %collective-permute-done.2.rows_ref.rows_d_ref) | copy-start | bytes 2236420
  90.7 23.4 %all-to-all-start.3 = ((bf16[4,8,200,128]{3,2,1,0:T(8,128)(2,1)}), bf16[4,8,200,128]{3,2,1,0:T(8,128)(2,1)S(1)}, u32[]{:S(2)}, u32[]{:S(2)}) async-start(bf16[4,8,200,128]{3,2,1,0:T(8,128)(2,1)} %broadcast_in_dim.2), calls=%async_computation.3 | async-start | bytes 3276800 | tf_op jit(solution)/shard_map/all_to_all | solution.py:224
  114.1 16.2 %copy-start.1 = (bf16[224,1664]{1,0:T(8,128)(2,1)S(1)}, bf16[224,1664]{1,0:T(8,128)(2,1)}, u32[]{:S(2)}) copy-start(bf16[224,1664]{1,0:T(8,128)(2,1)} %copy-done) | copy-start | bytes 2236420
  114.1 16.2 %copy-start.3 = (bf16[224,1664]{1,0:T(8,128)(2,1)S(1)}, bf16[224,1664]{1,0:T(8,128)(2,1)}, u32[]{:S(2)}) copy-start(bf16[224,1664]{1,0:T(8,128)(2,1)} %copy-done.2) | copy-start | bytes 2236420
  114.1 16.2 %copy-start.5 = (bf16[224,1664]{1,0:T(8,128)(2,1)S(1)}, bf16[224,1664]{1,0:T(8,128)(2,1)}, u32[]{:S(2)}) copy-start(bf16[224,1664]{1,0:T(8,128)(2,1)} %copy-done.4) | copy-start | bytes 2236420
  130.3 17.1 %copy-start.7 = (f32[56,1664]{1,0:T(8,128)S(1)}, f32[56,1664]{1,0:T(8,128)}, u32[]{:S(2)}) copy-start(f32[56,1664]{1,0:T(8,128)} %momentum_ref.3) | copy-start | bytes 1118212
